TPU v7x, 32 devices: a whole 2x2x4 slice. The times are simulated.
32 devices in a mesh: group: 2 (over x), dp: 8 (over z, y), tensor: 2 (over core).
Axes of the slice: x: 2, y: 2, z: 4, core: 2. Of those that a mesh axis runs over, the one named last changes fastest.
Arguments:
- patch_feats: bfloat16 [6144, 3200], P(('group', 'dp')), parts along dimension 0, may hold values from -80 to 80
- ln_gain: float32 [12800], replicated, may hold values from 0.1 to 1.9
- ln_shift: float32 [12800], replicated, may hold values from -3 to 3
- merge_weight: bfloat16 [12800, 4096], P('dp', 'tensor'), may hold values from -0.0546875 to 0.0546875
- merge_bias: float32 [4096], P('tensor'), may hold values from -3 to 3
- tile_count: int32 [16], P('group'), parts along dimension 0, may hold values from 1 to 3
- tile_dest: int32 [48], P('group'), parts along dimension 0, may hold values from 0 to 23, each once
Outputs:
- placed: bfloat16 [1536, 4096], P(('group', 'dp'), 'tensor'), parts along dimension 0
There are 2 independent parts, one for each index of `group`. A program takes and returns all parts, laid end to end along the dimension named above; an argument that names none is the same for every part. Nothing has to cross between parts.
Inputs may be any that keep to these rules, and one draw needn't show every extreme that they name: A device's tiles of 128 patch rows after its first tile_count tiles are padding. `tile_dest`: every output tile slot is named by exactly one tile.
All inputs are finite; a program needn't handle non-finite values.
Results may differ from a plain program's by a relative error of at most 0.013.
Values may be sent and summed in bfloat16 or wider, within the bound.
No kernel may reach another device: no remote copies, remote signals or barrier semaphores. Data moves between devices by JAX's collectives and lax.ppermute only.
A program may use at most 64 MiB of HBM per device.

v0:
```python
import jax
import jax.numpy as jnp
from jax import lax
from jax.sharding import PartitionSpec as P

TILE = 128


def layer_norm(row_block, ln_gain, ln_shift):
    row_mean = jnp.mean(row_block, axis=1, keepdims=True)
    centred = row_block - row_mean
    variance = jnp.mean(centred * centred, axis=1, keepdims=True)
    return centred * lax.rsqrt(variance + 1e-06) * ln_gain + ln_shift


def finish(summed, merge_bias, row_live):
    activated = jax.nn.gelu(summed + merge_bias, approximate=False)
    return jnp.where(row_live[:, None], activated, 0.0).astype(jnp.bfloat16)


def body(patch_feats, ln_gain, ln_shift, merge_weight, merge_bias, tile_count, tile_dest):
    peer_count = lax.axis_size("dp")
    my_index = lax.axis_index("dp")
    patch_count, feature_width = patch_feats.shape
    own_rows = patch_count // 4
    merged_width = 4 * feature_width
    block_width = merged_width // peer_count
    tile_rows = TILE // 4
    tiles_dev = patch_count // TILE
    slot_count = peer_count * tiles_dev
    all_rows = peer_count * own_rows
    local_ids = jnp.arange(own_rows, dtype=jnp.int32)
    own_live = local_ids // tile_rows < tile_count[my_index]
    merged = patch_feats.reshape(own_rows, merged_width).astype(jnp.float32)
    normed = jnp.where(own_live[:, None], layer_norm(merged, ln_gain, ln_shift), 0.0).astype(
        jnp.bfloat16
    )
    pieces = normed.reshape(own_rows, peer_count, block_width)
    received = lax.all_to_all(pieces, "dp", split_axis=1, concat_axis=0, tiled=True)
    received = received.reshape(all_rows, block_width)
    row_ids = jnp.arange(all_rows, dtype=jnp.int32)
    source_live = row_ids % own_rows // tile_rows < tile_count[row_ids // own_rows]
    slot_ids = jnp.arange(slot_count, dtype=jnp.int32)
    anchor = jnp.zeros((slot_count,), jnp.int32).at[tile_dest].set(slot_ids)
    dest_rows = (
        anchor[:, None] * tile_rows + jnp.arange(tile_rows, dtype=jnp.int32)[None, :]
    ).reshape(all_rows)
    my_rows = lax.dynamic_slice_in_dim(dest_rows, my_index * own_rows, own_rows, 0)
    row_block = jnp.take(received, dest_rows, axis=0)
    summed = lax.psum_scatter(
        jnp.dot(row_block, merge_weight, preferred_element_type=jnp.float32).astype(jnp.bfloat16),
        "dp",
        scatter_dimension=0,
        tiled=True,
    ).astype(jnp.float32)
    row_live = jnp.take(source_live, my_rows, axis=0)
    return finish(summed, merge_bias, row_live)


def solution(mesh):
    in_specs = (
        P(("group", "dp"), None),
        P(),
        P(),
        P("dp", "tensor"),
        P("tensor"),
        P("group"),
        P("group"),
    )
    out_specs = P(("group", "dp"), "tensor")
    return jax.shard_map(body, mesh=mesh, in_specs=in_specs, out_specs=out_specs, check_vma=False)
```

profile of v0, /device:TPU:0, one launch (start us, length us, event | category | flops | bytes accessed | tf_op | source)
XLA Modules:
  0.0 185.1 jit_solution(10469012078598421435)
XLA Ops:
  6.5 0.0 copy-start
  6.5 0.0 copy-start.1
  6.5 0.0 copy-start.2
  6.5 0.0 copy-start.3
  6.5 5.5 %reshape.158 = f32[96,8,1600]{2,1,0:T(8,128)} reshape(bf16[384,3200]{1,0:T(8,128)(2,1)} %param.7) | data formatting | bytes 7372800 | tf_op jit(solution)/shard_map/convert_element_type | solution.py:34
  12.1 0.0 copy-done
  12.1 0.4 convert_reduce_fusion
  12.5 0.0 copy-done.1
  12.5 0.1 add.148
  12.5 0.0 copy-done.2
  12.5 0.1 mul.51
  12.6 0.1 reduce_sum.24
  12.7 0.1 reduce_sum.25
  12.9 0.1 sub.39
  12.9 0.1 sub.40
  13.1 0.8 multiply_reduce_fusion
  13.8 0.1 reduce_sum.36
  14.0 0.1 reduce_sum.37
  14.1 0.0 copy-done.3
  14.1 0.7 fusion.35
  14.8 0.6 fusion.31
  15.4 0.0 copy-start.5
  15.4 5.4 %fusion.4 = bf16[96,8,1600]{2,0,1:T(8,128)(2,1)} fusion(f32[96,8,1600]{2,1,0:T(8,128)} %reshape.158, f32[8,1600]{1,0:T(8,128)S(1)} %add.148, f32[8,1600]{1,0:T(8,128)S(1)} %mul.51, f32[96]{0:T(128)S(1)} %add_rsqrt_fusion, f32[96]{0:T(128)S(1)} %broadcast_multiply_fusion, pred[96]{0:T(512)(128)(4,1)S(1)} %fusion.31), kind=kLoop, calls=%fused_computation.8 | loop fusion | flops 7372800 | bytes 7476064 | tf_op jit(solution)/shard_map/convert_element_type | solution.py:35
  20.8 7.3 %all-to-all-start = ((bf16[96,8,1600]{2,0,1:T(8,128)(2,1)}), bf16[96,8,1600]{2,0,1:T(8,128)(2,1)S(1)}, u32[]{:S(2)}, u32[]{:S(2)}) async-start(bf16[96,8,1600]{2,0,1:T(8,128)(2,1)} %fusion.4), calls=%async_computation | async-start | bytes 5111808 | tf_op jit(solution)/shard_map/all_to_all | solution.py:39
  28.1 0.0 reduce-scatter.2.cloned.1.call-start
  28.2 0.0 copy-done.5
  28.2 0.6 scatter_custom_fusion
  28.9 0.1 iota_add_fusion
  28.9 0.1 add.151
  29.0 0.1 add.136
  29.1 57.1 %all-to-all-done = bf16[96,8,1600]{2,0,1:T(8,128)(2,1)S(1)} async-done(((bf16[96,8,1600]{2,0,1:T(8,128)(2,1)}), bf16[96,8,1600]{2,0,1:T(8,128)(2,1)S(1)}, u32[]{:S(2)}, u32[]{:S(2)}) %all-to-all-start) | async-done | bytes 2457632 | tf_op jit(solution)/shard_map/all_to_all | solution.py:39
  86.2 4.0 %gather_fusion.1 = bf16[768,1600]{1,0:T(8,128)(2,1)} fusion(bf16[768,1600]{1,0:T(8,128)(2,1)S(1)} %bitcast.15, s32[1024]{0:T(1024)S(1)} %pad_clamp_fusion), kind=kCustom, calls=%fused_computation.1 | custom fusion | bytes 4918272 | tf_op jit(solution)/shard_map/jit(_take)/gather | solution.py:49
  90.2 0.0 copy-start.4
  90.2 10.7 %convolution_convert_fusion = bf16[768,2048]{1,0:T(8,128)(2,1)} fusion(bf16[1600,2048]{1,0:T(8,128)(2,1)} %param.10, bf16[768,1600]{1,0:T(8,128)(2,1)} %gather_fusion.1, pred[768]{0:T(1024)(128)(4,1)S(1)} %compare_and_fusion), kind=kOutput, calls=%fused_computation.10 | convolution fusion | flops 5035966464 | bytes 12157696 | tf_op jit(solution)/shard_map/dot_general | solution.py:51
  100.9 0.0 reduce-scatter.2.cloned.1.call-update
  101.0 4.4 %fusion.29 = s32[768]{0:T(1024)S(1)} fusion(s32[]{:T(128)} %bitcast.1, s32[]{:T(128)} %bitcast.2, s32[]{:T(128)} %bitcast.3, s32[]{:T(128)} %bitcast.4, s32[]{:T(128)} %bitcast.5, s32[]{:T(128)} %bitcast.7, s32[]{:T(128)} %bitcast.6), kind=kLoop, calls=%fused_computation.70 | loop fusion | flops 17664 | bytes 3100 | tf_op jit(solution)/shard_map/gather | solution.py:42
  105.5 0.1 compare_select_fusion.9
  105.5 0.7 fusion.23
  106.2 1.3 gather_fusion
  107.5 0.1 and_select_fusion.2
  107.6 67.1 %reduce-scatter.2.cloned.1.call-done = bf16[96,2048]{1,0:T(8,128)(2,1)} async-done(((bf16[768,2048]{1,0:T(8,128)(2,1)}), bf16[96,2048]{1,0:T(8,128)(2,1)}) %reduce-scatter.2.cloned.1.call-update) | async-done | bytes 393232 | tf_op jit(solution)/shard_map/reduce_scatter | solution.py:50
  174.7 0.0 copy-done.4
  174.7 3.5 %fusion.11 = bf16[96,2048]{1,0:T(8,128)(2,1)} fusion(bf16[96,2048]{1,0:T(8,128)(2,1)} %reduce-scatter.2.cloned.1.call-done, f32[2048]{0:T(1024)S(1)} %copy-done.4, pred[96]{0:T(512)(128)(4,1)S(1)} %and_select_fusion.2), kind=kLoop, calls=%fused_computation.19 | loop fusion | flops 13369344 | bytes 794720 | tf_op jit(solution)/shard_map/convert_element_type | solution.py:18
  (10 shorter events, 0.1 us)
Async XLA Ops:
  6.5 5.5 %copy-start = (bf16[384,3200]{1,0:T(8,128)(2,1)S(1)}, bf16[384,3200]{1,0:T(8,128)(2,1)}, u32[]{:S(2)}) copy-start(bf16[384,3200]{1,0:T(8,128)(2,1)} %param.7) | copy-start | bytes 7372804
  6.5 5.9 %copy-start.1 = (f32[12800]{0:T(1024)S(1)}, f32[12800]{0:T(1024)}, u32[]{:S(2)}) copy-start(f32[12800]{0:T(1024)} %param.9) | copy-start | bytes 153604
  6.5 6.0 %copy-start.2 = (f32[12800]{0:T(1024)S(1)}, f32[12800]{0:T(1024)}, u32[]{:S(2)}) copy-start(f32[12800]{0:T(1024)} %param.8) | copy-start | bytes 153604
  6.5 7.5 %copy-start.3 = (s32[8]{0:T(128)S(1)}, s32[8]{0:T(128)}, u32[]{:S(2)}) copy-start(s32[8]{0:T(128)} %param.12) | copy-start | bytes 100
  15.4 12.7 %copy-start.5 = (s32[24]{0:T(128)S(1)}, s32[24]{0:T(128)}, u32[]{:S(2)}) copy-start(s32[24]{0:T(128)} %param.13) | copy-start | bytes 292
  20.8 65.4 %all-to-all-start = ((bf16[96,8,1600]{2,0,1:T(8,128)(2,1)}), bf16[96,8,1600]{2,0,1:T(8,128)(2,1)S(1)}, u32[]{:S(2)}, u32[]{:S(2)}) async-start(bf16[96,8,1600]{2,0,1:T(8,128)(2,1)} %fusion.4), calls=%async_computation | async-start | bytes 5111808 | tf_op jit(solution)/shard_map/all_to_all | solution.py:39
  28.1 146.6 %reduce-scatter.2.cloned.1.call-start = ((), (), s32[]{:S(2)}) async-start(), calls=%async_computation.2 | async-start | bytes 3538944 | tf_op jit(solution)/shard_map/reduce_scatter | solution.py:50
  90.2 84.5 %copy-start.4 = (f32[2048]{0:T(1024)S(1)}, f32[2048]{0:T(1024)}, u32[]{:S(2)}) copy-start(f32[2048]{0:T(1024)} %param.11) | copy-start | bytes 24580
Sparse Core Ops, SparseCore 0:
  101.1 73.5 reduce-scatter.1
where the time goes:
time: 185 us
  waiting for transfers between devices  124 us (67%)
  other arithmetic  16.4 us (9%)
  between operations  13.6 us (7%)
  local copies, waits for them, and re-layouts  12.9 us (7%)
  matrix products  10.7 us (6%)
  starting transfers between devices  7.32 us (4%)
    reduce_scatter x1, waiting for transfers between devices, body(): lax.psum_scatter(jnp.dot(row_block, merge_weight, preferred_element_type=...  67.1 us
    all_to_all x1, waiting for transfers between devices, body(): lax.all_to_all(pieces, 'dp', split_axis=1, concat_axis=0, tiled=True)  57.1 us
    dot_general x1, matrix products, body(): jnp.dot(row_block, merge_weight, preferred_element_type=jnp.float32)  10.7 us
    all_to_all x1, starting transfers between devices, body(): lax.all_to_all(pieces, 'dp', split_axis=1, concat_axis=0, tiled=True)  7.28 us
    convert_element_type x1, local copies, waits for them, and re-layouts, body(): merged = patch_feats.reshape(own_rows, merged_width).astype(jnp.float32)  5.51 us
    convert_element_type x1, other arithmetic, body(): jnp.where(own_live[:, None], layer_norm(merged, ln_gain, ln_shift), 0.0)  5.39 us
    gather x2, other arithmetic, body(): tile_count[row_ids // own_rows]  4.48 us
    gather x1, local copies, waits for them, and re-layouts, body(): row_block = jnp.take(received, dest_rows, axis=0)  4.02 us
  transfers between devices with their start and end apart: 2, of which 2 were waited for; matrix products, arithmetic and copies ran while one was open for 4% of the time, Pallas kernels for 0%

commit v1 on v0

v1 whole, which is shorter than its diff:
```python
import functools

import jax
import jax.numpy as jnp
from jax import lax
from jax.experimental import pallas as pl
from jax.experimental.pallas import tpu as pltpu
from jax.sharding import PartitionSpec as P

TILE = 128
TILE_ROWS = TILE // 4
HALF = TILE_ROWS // 2
VMEM_LIMIT = 40 * 1024 * 1024


def vmem():
    return pl.BlockSpec(memory_space=pltpu.VMEM)


def arrangement(bits):
    if not bits:
        return [0]
    rest = arrangement(bits[1:])
    return [owner ^ (1 << bits[0]) for owner in rest] + rest


def prepare_kernel(peers, tiles, scalars, x_ref, gain_ref, shift_ref, *refs):
    outs, pieces = refs[:-1], refs[-1]
    me, count = scalars[0], scalars[2]
    rows = tiles * HALF
    width = x_ref.shape[-1]
    total = 4 * width
    block_width = total // peers
    x = x_ref[...].reshape(4 * rows, width)
    row_out = lax.broadcasted_iota(jnp.int32, (4 * rows, 4 * rows), 0)
    row_in = lax.broadcasted_iota(jnp.int32, (4 * rows, 4 * rows), 1)
    quarter = jnp.zeros_like(row_out)
    for q in range(1, 4):
        quarter += (row_out >= q * rows).astype(jnp.int32)
    source = 4 * (row_out - quarter * rows) + quarter
    mix = (row_in == source).astype(jnp.bfloat16)
    y = jnp.dot(mix, x, preferred_element_type=jnp.float32)
    parts = [y[q * rows:(q + 1) * rows] for q in range(4)]
    mean = sum(jnp.sum(part, axis=1, keepdims=True) for part in parts) / total
    parts = [part - mean for part in parts]
    variance = sum(jnp.sum(part * part, axis=1, keepdims=True) for part in parts) / total
    scale = lax.rsqrt(variance + 1e-06)
    tile_of = lax.broadcasted_iota(jnp.int32, (rows, 1), 0) // HALF
    live = tile_of < count
    per_patch = width // block_width
    for q in range(4):
        normed = parts[q] * scale * gain_ref[pl.ds(q, 1), :] + shift_ref[pl.ds(q, 1), :]
        normed = jnp.where(live, normed, 0.0).astype(jnp.bfloat16)
        for part in range(per_patch):
            pieces[q * per_patch + part] = normed[:, part * block_width:(part + 1) * block_width]
    for k in range(peers):
        outs[k][...] = pieces[jnp.bitwise_xor(me, k)]


def prepare(scalars, patch_feats, ln_gain, ln_shift, peers, tiles):
    width = patch_feats.shape[1]
    block_width = 4 * width // peers
    rows = tiles * HALF
    x = patch_feats.reshape(tiles, 2, TILE // 2, width)
    piece = jax.ShapeDtypeStruct((rows, block_width), jnp.bfloat16)
    return pl.pallas_call(
        functools.partial(prepare_kernel, peers, tiles),
        grid_spec=pltpu.PrefetchScalarGridSpec(
            num_scalar_prefetch=1,
            grid=(1,),
            in_specs=[
                pl.BlockSpec((tiles, 1, TILE // 2, width), lambda i, s: (0, s[1], 0, 0)),
                pl.BlockSpec((4, width), lambda i, s: (0, 0)),
                pl.BlockSpec((4, width), lambda i, s: (0, 0)),
            ],
            out_specs=[pl.BlockSpec((rows, block_width), lambda i, s: (0, 0))] * peers,
            scratch_shapes=[pltpu.VMEM((peers, rows, block_width), jnp.bfloat16)],
        ),
        out_shape=[piece] * peers,
        compiler_params=pltpu.CompilerParams(vmem_limit_bytes=VMEM_LIMIT),
        name="prepare",
    )(scalars, x, ln_gain.reshape(4, width), ln_shift.reshape(4, width))


def gather_kernel(peers, order_ref, *refs):
    ins, out, held = refs[:peers], refs[peers], refs[peers + 1]
    rows = ins[0].shape[0]
    for k in range(peers):
        held[pl.ds(k * rows, rows), :] = ins[k][...]
    for i in range(peers * rows // HALF):
        first = pl.multiple_of(order_ref[i] * HALF, HALF)
        out[pl.ds(i * HALF, HALF), :] = held[pl.ds(first, HALF), :]


def gather_tiles(order, received):
    peers = len(received)
    rows, block_width = received[0].shape
    return pl.pallas_call(
        functools.partial(gather_kernel, peers),
        grid_spec=pltpu.PrefetchScalarGridSpec(
            num_scalar_prefetch=1,
            grid=(1,),
            in_specs=[pl.BlockSpec((rows, block_width), lambda i, s: (0, 0))] * peers,
            out_specs=pl.BlockSpec((peers * rows, block_width), lambda i, s: (0, 0)),
            scratch_shapes=[pltpu.VMEM((peers * rows, block_width), jnp.bfloat16)],
        ),
        out_shape=jax.ShapeDtypeStruct((peers * rows, block_width), jnp.bfloat16),
        compiler_params=pltpu.CompilerParams(vmem_limit_bytes=VMEM_LIMIT),
        name="gather_tiles",
    )(order, *received)


def project_kernel(swapped, a_ref, w_ref, send_ref, keep_ref):
    acc = jnp.dot(a_ref[...], w_ref[...], preferred_element_type=jnp.float32).astype(jnp.bfloat16)
    quarter = acc.shape[0] // 4
    parts = [acc[i * quarter:(i + 1) * quarter] for i in range(4)]
    if swapped:
        parts = [parts[0], parts[2], parts[1], parts[3]]
    for i in range(2):
        send_ref[pl.ds(i * quarter, quarter), :] = parts[i]
        keep_ref[pl.ds(i * quarter, quarter), :] = parts[2 + i]


def project(a, weight, first, columns, swapped, block=256):
    rows, depth = a.shape
    half = jax.ShapeDtypeStruct((rows // 2, columns), jnp.bfloat16)
    return pl.pallas_call(
        functools.partial(project_kernel, swapped),
        grid=(columns // block,),
        in_specs=[
            pl.BlockSpec((rows, depth), lambda i: (0, 0)),
            pl.BlockSpec((depth, block), lambda i: (0, first // block + i)),
        ],
        out_specs=[pl.BlockSpec((rows // 2, block), lambda i: (0, i))] * 2,
        out_shape=[half, half],
        compiler_params=pltpu.CompilerParams(vmem_limit_bytes=VMEM_LIMIT),
        cost_estimate=pl.CostEstimate(
            flops=2 * rows * depth * columns,
            bytes_accessed=2 * (rows * depth + depth * columns + rows * columns),
            transcendentals=0,
        ),
        name="project",
    )(a, weight)


def finish_kernel(tiles, chunks, columns, scalars, live_ref, bias_ref, *refs):
    out = refs[-1]
    core = scalars[1]
    for index, (half, first) in enumerate(chunks):
        keep, recv = refs[2 * index], refs[2 * index + 1]
        summed = keep[...].astype(jnp.float32) + recv[...].astype(jnp.float32)
        summed += bias_ref[:, first:first + columns]
        act = 0.5 * summed * (1.0 + lax.erf(summed * 0.7071067811865476))
        side = core if half == 0 else 1 - core
        for tile in range(tiles):
            value = jnp.where(live_ref[tile] > 0, act[tile * HALF:(tile + 1) * HALF], 0.0)
            out[tile, side, :, first:first + columns] = value.astype(jnp.bfloat16)


def finish(scalars, live, bias, sums, chunks, columns, tiles):
    width = bias.shape[0]
    flat = [array for pair in sums for array in pair]
    out = pl.pallas_call(
        functools.partial(finish_kernel, tiles, chunks, columns),
        grid_spec=pltpu.PrefetchScalarGridSpec(
            num_scalar_prefetch=2,
            grid=(1,),
            in_specs=[pl.BlockSpec((1, width), lambda i, s, l: (0, 0))]
            + [pl.BlockSpec(array.shape, lambda i, s, l: (0, 0)) for array in flat],
            out_specs=pl.BlockSpec((tiles, 2, HALF, width), lambda i, s, l: (0, 0, 0, 0)),
        ),
        out_shape=jax.ShapeDtypeStruct((tiles, 2, HALF, width), jnp.bfloat16),
        compiler_params=pltpu.CompilerParams(vmem_limit_bytes=VMEM_LIMIT),
        name="finish",
    )(scalars, live, bias.reshape(1, width), *flat)
    return out.reshape(tiles * TILE_ROWS, width)


def exchange(array, mask, peers):
    return lax.ppermute(array, "dp", [(d, d ^ mask) for d in range(peers)])


def halve(send, keep, bits, peers):
    for bit in bits[:-1]:
        recv = exchange(send, 1 << bit, peers)
        half = keep.shape[0] // 2
        summed = keep.astype(jnp.float32) + recv.astype(jnp.float32)
        send, keep = summed[:half].astype(jnp.bfloat16), summed[half:]
    return keep, exchange(send, 1 << bits[-1], peers)


def body(patch_feats, ln_gain, ln_shift, merge_weight, merge_bias, tile_count, tile_dest):
    peers = lax.axis_size("dp")
    me = lax.axis_index("dp").astype(jnp.int32)
    core = lax.axis_index("tensor").astype(jnp.int32)
    tiles = patch_feats.shape[0] // TILE
    slots = peers * tiles
    bits = list(range(peers.bit_length() - 1))
    columns = merge_weight.shape[1]

    source_ids = jnp.arange(peers, dtype=jnp.int32)
    my_count = jnp.sum(jnp.where(source_ids == me, tile_count, 0))
    scalars = jnp.stack([me, core, my_count])
    pieces = prepare(scalars, patch_feats, ln_gain, ln_shift, peers, tiles)

    owners = jnp.array(arrangement(bits), jnp.int32) ^ me
    wanted = (owners[:, None] * tiles + jnp.arange(tiles, dtype=jnp.int32)[None, :]).reshape(slots)
    tile_ids = jnp.arange(slots, dtype=jnp.int32)
    anchor = jnp.sum(jnp.where(tile_dest[None, :] == wanted[:, None], tile_ids[None, :], 0), axis=1)
    source, place = anchor // tiles, anchor % tiles
    order = (source ^ me) * tiles + place
    own_source, own_place = source[-tiles:], place[-tiles:]
    own_count = jnp.sum(jnp.where(own_source[:, None] == source_ids[None, :], tile_count[None, :], 0), axis=1)
    live = (own_place < own_count).astype(jnp.int32)

    received = {0: pieces[0]}
    for k in reversed(range(1, peers)):
        received[k] = exchange(pieces[k], k, peers)
    mine = gather_tiles(order, [received[k] for k in range(peers)])
    other = lax.ppermute(mine, "tensor", [(0, 1), (1, 0)])

    y_first = bits
    z_first = [bits[1], bits[0]] + bits[2:]
    half = columns // 2
    plan = [(0, 0, False), (0, half, True), (1, 0, False), (1, half, False)]
    sums, chunks = [], []
    for side, first, swapped in plan:
        send, keep = project(mine if side == 0 else other, merge_weight, first, half, swapped)
        sums.append(halve(send, keep, z_first if swapped else y_first, peers))
        chunks.append((side, first))
    return finish(scalars, live, merge_bias, sums, chunks, half, tiles)


def solution(mesh):
    in_specs = (
        P(("group", "dp"), None),
        P(),
        P(),
        P("dp", "tensor"),
        P("tensor"),
        P("group"),
        P("group"),
    )
    out_specs = P(("group", "dp"), "tensor")
    return jax.shard_map(body, mesh=mesh, in_specs=in_specs, out_specs=out_specs, check_vma=False)
```

time: 185 us -> 109 us (0.59)
  waiting for transfers between devices: 124 us -> 33 us
  starting transfers between devices: 7.32 us -> 42.4 us
  Pallas kernels: 0 us -> 15.5 us
  between operations: 13.6 us -> 0.29 us
  other arithmetic: 16.4 us -> 4.98 us
  matrix products: 10.7 us -> 0 us
    reduce_scatter x1 -> x0, waiting for transfers between devices: 67.1 us -> none  [body(): lax.psum_scatter(jnp.dot(row_block, merge_weight, preferred_element_type=...]
    all_to_all x1 -> x0, waiting for transfers between devices: 57.1 us -> none  [body(): lax.all_to_all(pieces, 'dp', split_axis=1, concat_axis=0, tiled=True)]
    ppermute x0 -> x20, starting transfers between devices: none -> 42.4 us  [the longest x19 42.4 us: exchange(): return lax.ppermute(array, 'dp', [(d, d ^ mask) for d in range(peers)])]
    ppermute x0 -> x20, waiting for transfers between devices: none -> 33 us  [the longest x19 33 us: exchange(): return lax.ppermute(array, 'dp', [(d, d ^ mask) for d in range(peers)])]
    pallas_call x0 -> x7, Pallas kernels: none -> 15.5 us  [the longest x4 10.8 us: project(): pl.pallas_call(functools.partial(project_kernel, swapped), grid=(columns...]
    dot_general x1 -> x0, matrix products: 10.7 us -> none  [body(): jnp.dot(row_block, merge_weight, preferred_element_type=jnp.float32)]
    convert_element_type x2 -> x1, other arithmetic: 8.91 us -> 0.07 us  [body(): live = (own_place < own_count).astype(jnp.int32)]
    unnamed x12, local copies, waits for them, and re-layouts: 0.02 us -> 7.43 us
  transfers between devices with their start and end apart: 2 -> 20, of which waited for: 2 -> 9; matrix products, arithmetic and copies ran while one was open for 4% -> 5% of each run, Pallas kernels for 0% -> 10%
where the time goes in v1:
time: 109 us
  starting transfers between devices  42.4 us (39%)
  waiting for transfers between devices  33 us (30%)
  Pallas kernels  15.5 us (14%)
  local copies, waits for them, and re-layouts  12.8 us (12%)
  other arithmetic  4.98 us (5%)
    ppermute x19, starting transfers between devices, exchange(): return lax.ppermute(array, 'dp', [(d, d ^ mask) for d in range(peers)])  42.4 us
    ppermute x19, waiting for transfers between devices, exchange(): return lax.ppermute(array, 'dp', [(d, d ^ mask) for d in range(peers)])  33 us
    pallas_call x4, Pallas kernels, project(): pl.pallas_call(functools.partial(project_kernel, swapped), grid=(columns...  10.8 us
    unnamed x12, local copies, waits for them, and re-layouts  7.43 us
    add x8, other arithmetic, halve(): summed = keep.astype(jnp.float32) + recv.astype(jnp.float32)  2.44 us
    pallas_call x1, Pallas kernels, prepare(): pl.pallas_call(functools.partial(prepare_kernel, peers, tiles), grid_spec...  2.39 us
  transfers between devices with their start and end apart: 20, of which 9 were waited for; matrix products, arithmetic and copies ran while one was open for 5% of the time, Pallas kernels for 10%

profile of v1, /device:TPU:0, one launch (start us, length us, event | category | flops | bytes accessed | tf_op | source)
XLA Modules:
  0.0 108.9 jit_solution(4323180408202889036)
XLA Ops:
  0.0 0.8 reshape.36.gain_ref
  0.8 0.8 reshape.37.shift_ref
  1.7 1.3 %fusion = (s32[]{:T(128)}, s32[8]{0:T(128)S(1)}) fusion(s32[8]{0:T(128)} %param.13, s32[]{:T(128)} %axis_index.23, s32[8]{0:T(128)} %constant.33.clone), kind=kLoop, calls=%fused_computation.24 | loop fusion | flops 39 | bytes 104 | tf_op jit(solution)/shard_map/reduce_sum | solution.py:202
  3.0 0.7 pad_add_fusion.scalars
  3.7 1.7 %copy-done.2 = bf16[384,3200]{1,0:T(8,128)(2,1)S(1)} copy-done((bf16[384,3200]{1,0:T(8,128)(2,1)S(1)}, bf16[384,3200]{1,0:T(8,128)(2,1)}, u32[]{:S(2)}) %copy-start.2) | copy-done | bytes 2457624
  5.4 2.4 %prepare.1 = (bf16[48,1600]{1,0:T(8,128)(2,1)S(1)}, bf16[48,1600]{1,0:T(8,128)(2,1)S(1)}, bf16[48,1600]{1,0:T(8,128)(2,1)S(1)}, bf16[48,1600]{1,0:T(8,128)(2,1)S...) custom-call(s32[3]{0:T(128)S(1)} %pad_add_fusion.scalars, ...), custom_call_target="tpu_custom_call" | custom-call | tf_op jit(solution)/shard_map/prepare/pallas_call | solution.py:66
  7.8 3.0 %collective-permute-start = (bf16[48,1600]{1,0:T(8,128)(2,1)S(1)}, bf16[48,1600]{1,0:T(8,128)(2,1)S(1)}, u32[]{:S(2)}, u32[]{:S(2)}) collective-permute-start(bf16[48,1600]{1,0:T(8,128)(2,1)S(1)} %get-tuple-element.22), channel_id=1, source_target_pairs={{0,2},{2,0},{4,6},{6,4},{8,10},{10,8},{12,14},{14,12},{1,3},{3,1},... | collective-permute-start | bytes 460808 | tf_op jit(solution)/shard_map/ppermute | solution.py:180
  10.8 1.6 %collective-permute-start.1 = (bf16[48,1600]{1,0:T(8,128)(2,1)S(1)}, bf16[48,1600]{1,0:T(8,128)(2,1)S(1)}, u32[]{:S(2)}, u32[]{:S(2)}) collective-permute-start(bf16[48,1600]{1,0:T(8,128)(2,1)S(1)} %get-tuple-element.23), channel_id=1, source_target_pairs={{0,4},{2,6},{4,0},{6,2},{8,12},{10,14},{12,8},{14,10},{1,5},{3,7},... | collective-permute-start | bytes 460808 | tf_op jit(solution)/shard_map/ppermute | solution.py:180
  12.4 3.0 %collective-permute-start.3 = (bf16[48,1600]{1,0:T(8,128)(2,1)S(1)}, bf16[48,1600]{1,0:T(8,128)(2,1)S(1)}, u32[]{:S(2)}, u32[]{:S(2)}) collective-permute-start(bf16[48,1600]{1,0:T(8,128)(2,1)S(1)} %get-tuple-element.25), channel_id=1, source_target_pairs={{0,8},{2,10},{4,12},{6,14},{8,0},{10,2},{12,4},{14,6},{1,9},{3,11}... | collective-permute-start | bytes 460808 | tf_op jit(solution)/shard_map/ppermute | solution.py:180
  15.4 1.3 %collective-permute-start.4 = (bf16[48,1600]{1,0:T(8,128)(2,1)S(1)}, bf16[48,1600]{1,0:T(8,128)(2,1)S(1)}, u32[]{:S(2)}, u32[]{:S(2)}) collective-permute-start(bf16[48,1600]{1,0:T(8,128)(2,1)S(1)} %get-tuple-element.26), channel_id=1, source_target_pairs={{0,10},{2,8},{4,14},{6,12},{8,2},{10,0},{12,6},{14,4},{1,11},{3,9}... | collective-permute-start | bytes 460808 | tf_op jit(solution)/shard_map/ppermute | solution.py:180
  16.7 0.1 iota_add_fusion
  16.7 0.1 add.57
  16.8 0.2 select_reduce_fusion
  17.0 0.0 collective-permute-done.refs_1_
  17.0 3.7 %collective-permute-start.5 = (bf16[48,1600]{1,0:T(8,128)(2,1)S(1)}, bf16[48,1600]{1,0:T(8,128)(2,1)S(1)}, u32[]{:S(2)}, u32[]{:S(2)}) collective-permute-start(bf16[48,1600]{1,0:T(8,128)(2,1)S(1)} %get-tuple-element.27), channel_id=1, source_target_pairs={{0,12},{2,14},{4,8},{6,10},{8,4},{10,6},{12,0},{14,2},{1,13},{3,15... | collective-permute-start | bytes 460808 | tf_op jit(solution)/shard_map/ppermute | solution.py:180
  20.7 3.0 %collective-permute-done.1.refs_2_ = bf16[48,1600]{1,0:T(8,128)(2,1)S(1)} collective-permute-done((bf16[48,1600]{1,0:T(8,128)(2,1)S(1)}, bf16[48,1600]{1,0:T(8,128)(2,1)S(1)}, u32[]{:S(2)}, u32[]{:S(2)}) %collective-permute-start.1) | collective-permute-done | bytes 153632 | tf_op jit(solution)/shard_map/ppermute | solution.py:180
  23.6 1.1 %collective-permute-start.6 = (bf16[48,1600]{1,0:T(8,128)(2,1)S(1)}, bf16[48,1600]{1,0:T(8,128)(2,1)S(1)}, u32[]{:S(2)}, u32[]{:S(2)}) collective-permute-start(bf16[48,1600]{1,0:T(8,128)(2,1)S(1)} %get-tuple-element.28), channel_id=1, source_target_pairs={{0,14},{2,12},{4,10},{6,8},{8,6},{10,4},{12,2},{14,0},{1,15},{3,13... | collective-permute-start | bytes 460808 | tf_op jit(solution)/shard_map/ppermute | solution.py:180
  24.8 0.2 collective-permute-done.2.refs_3_
  25.0 0.0 collective-permute-done.3.refs_4_
  25.0 13.5 %collective-permute-done.4.refs_5_ = bf16[48,1600]{1,0:T(8,128)(2,1)S(1)} collective-permute-done((bf16[48,1600]{1,0:T(8,128)(2,1)S(1)}, bf16[48,1600]{1,0:T(8,128)(2,1)S(1)}, u32[]{:S(2)}, u32[]{:S(2)}) %collective-permute-start.4) | collective-permute-done | bytes 153632 | tf_op jit(solution)/shard_map/ppermute | solution.py:180
  38.5 0.0 collective-permute-done.5.refs_6_
  38.5 0.7 gather_tiles.1.a_ref
  39.2 1.6 %copy.12 = bf16[384,1600]{0,1:T(8,128)(2,1)} copy(bf16[384,1600]{1,0:T(8,128)(2,1)S(1)} %gather_tiles.1.a_ref) | data formatting | bytes 2457600 | tf_op jit(solution)/shard_map/gather_tiles/pallas_call | solution.py:98
  40.7 0.0 collective-permute-start.13
  40.8 2.9 %copy-done = bf16[1600,2048]{1,0:T(8,128)(2,1)S(1)} copy-done((bf16[1600,2048]{1,0:T(8,128)(2,1)S(1)}, bf16[1600,2048]{1,0:T(8,128)(2,1)}, u32[]{:S(2)}) %copy-start) | copy-done | bytes 6553624
  43.6 2.7 %project.4 = (bf16[192,1024]{1,0:T(8,128)(2,1)S(1)}, bf16[192,1024]{1,0:T(8,128)(2,1)S(1)}) custom-call(bf16[384,1600]{1,0:T(8,128)(2,1)S(1)} %gather_tiles.1.a_ref, bf16[1600,2048]{1,0:T(8,128)(2,1)S(1)} %copy-done), custom_call_target="tpu_custom_call" | custom-call | flops 1258291200 | bytes 5292032 | tf_op jit(solution)/shard_map/project/pallas_call | solution.py:127
  46.3 0.0 copy-start.4
  46.3 0.8 collective-permute-start.7
  47.2 2.7 %project.5 = (bf16[192,1024]{1,0:T(8,128)(2,1)S(1)}, bf16[192,1024]{1,0:T(8,128)(2,1)S(1)}) custom-call(bf16[384,1600]{1,0:T(8,128)(2,1)S(1)} %gather_tiles.1.a_ref, bf16[1600,2048]{1,0:T(8,128)(2,1)S(1)} %copy-done), custom_call_target="tpu_custom_call" | custom-call | flops 1258291200 | bytes 5292032 | tf_op jit(solution)/shard_map/project/pallas_call | solution.py:127
  49.9 5.8 %collective-permute-start.10 = (bf16[192,1024]{1,0:T(8,128)(2,1)S(1)}, bf16[192,1024]{1,0:T(8,128)(2,1)S(1)}, u32[]{:S(2)}, u32[]{:S(2)}) collective-permute-start(bf16[192,1024]{1,0:T(8,128)(2,1)S(1)} %get-tuple-element.32), channel_id=1, source_target_pairs={{0,4},{2,6},{4,0},{6,2},{8,12},{10,14},{12,8},{14,10},{1,5},{3,7},... | collective-permute-start | bytes 1179656 | tf_op jit(solution)/shard_map/ppermute | solution.py:180
  55.7 0.1 slice.63
  55.8 0.2 select_reduce_fusion.1
  56.0 2.0 %collective-permute-done.7 = bf16[192,1024]{1,0:T(8,128)(2,1)S(1)} collective-permute-done((bf16[192,1024]{1,0:T(8,128)(2,1)S(1)}, bf16[192,1024]{1,0:T(8,128)(2,1)S(1)}, u32[]{:S(2)}, u32[]{:S(2)}) %collective-permute-start.7) | collective-permute-done | bytes 393248 | tf_op jit(solution)/shard_map/ppermute | solution.py:180
  57.9 0.1 convert_add_fusion.3
  58.1 6.0 %collective-permute-start.8 = (bf16[96,1024]{1,0:T(8,128)(2,1)S(1)}, bf16[96,1024]{1,0:T(8,128)(2,1)}, u32[]{:S(2)}, u32[]{:S(2)}) collective-permute-start(bf16[96,1024]{1,0:T(8,128)(2,1)S(1)} %slice.112), channel_id=1, source_target_pairs={{0,4},{2,6},{4,0},{6,2},{8,12},{10,14},{12,8},{14,10},{1,5},{3,7},... | collective-permute-start | bytes 589832 | tf_op jit(solution)/shard_map/ppermute | solution.py:180
  64.1 1.5 %collective-permute-done.10 = bf16[192,1024]{1,0:T(8,128)(2,1)S(1)} collective-permute-done((bf16[192,1024]{1,0:T(8,128)(2,1)S(1)}, bf16[192,1024]{1,0:T(8,128)(2,1)S(1)}, u32[]{:S(2)}, u32[]{:S(2)}) %collective-permute-start.10) | collective-permute-done | bytes 393248 | tf_op jit(solution)/shard_map/ppermute | solution.py:180
  65.6 0.1 convert_add_fusion.2
  65.7 1.5 %collective-permute-start.11 = (bf16[96,1024]{1,0:T(8,128)(2,1)S(1)}, bf16[96,1024]{1,0:T(8,128)(2,1)}, u32[]{:S(2)}, u32[]{:S(2)}) collective-permute-start(bf16[96,1024]{1,0:T(8,128)(2,1)S(1)} %slice.111), channel_id=1, source_target_pairs={{0,2},{2,0},{4,6},{6,4},{8,10},{10,8},{12,14},{14,12},{1,3},{3,1},... | collective-permute-start | bytes 589832 | tf_op jit(solution)/shard_map/ppermute | solution.py:180
  67.3 0.0 collective-permute-done.13
  67.3 1.8 %copy.13.a_ref = bf16[384,1600]{1,0:T(8,128)(2,1)S(1)} copy(bf16[384,1600]{0,1:T(8,128)(2,1)} %collective-permute-done.13) | data formatting | bytes 2457600 | tf_op jit(solution)/shard_map/ppermute | solution.py:220
  69.1 0.0 copy-start.1
  69.1 2.9 %copy-done.1 = bf16[1600,2048]{1,0:T(8,128)(2,1)S(1)} copy-done((bf16[1600,2048]{1,0:T(8,128)(2,1)S(1)}, bf16[1600,2048]{1,0:T(8,128)(2,1)}, u32[]{:S(2)}) %copy-start.1) | copy-done | bytes 6553624
  72.0 2.7 %project.6 = (bf16[192,1024]{1,0:T(8,128)(2,1)S(1)}, bf16[192,1024]{1,0:T(8,128)(2,1)S(1)}) custom-call(bf16[384,1600]{1,0:T(8,128)(2,1)S(1)} %copy.13.a_ref, bf16[1600,2048]{1,0:T(8,128)(2,1)S(1)} %copy-done.1), custom_call_target="tpu_custom_call" | custom-call | flops 1258291200 | bytes 5292032 | tf_op jit(solution)/shard_map/project/pallas_call | solution.py:127
  74.7 0.6 collective-permute-start.14
  75.3 1.0 slice_add_fusion.3
  76.3 3.6 %collective-permute-start.9 = (bf16[48,1024]{1,0:T(8,128)(2,1)S(1)}, bf16[48,1024]{1,0:T(8,128)(2,1)S(1)}, u32[]{:S(2)}, u32[]{:S(2)}) collective-permute-start(bf16[48,1024]{1,0:T(8,128)(2,1)S(1)} %slice.116), channel_id=1, source_target_pairs={{0,8},{2,10},{4,12},{6,14},{8,0},{10,2},{12,4},{14,6},{1,9},{3,11}... | collective-permute-start | bytes 294920 | tf_op jit(solution)/shard_map/ppermute | solution.py:180
  79.9 2.7 %project.7 = (bf16[192,1024]{1,0:T(8,128)(2,1)S(1)}, bf16[192,1024]{1,0:T(8,128)(2,1)S(1)}) custom-call(bf16[384,1600]{1,0:T(8,128)(2,1)S(1)} %copy.13.a_ref, bf16[1600,2048]{1,0:T(8,128)(2,1)S(1)} %copy-done.1), custom_call_target="tpu_custom_call" | custom-call | flops 1258291200 | bytes 5292032 | tf_op jit(solution)/shard_map/project/pallas_call | solution.py:127
  82.7 1.9 %collective-permute-start.17 = (bf16[192,1024]{1,0:T(8,128)(2,1)S(1)}, bf16[192,1024]{1,0:T(8,128)(2,1)S(1)}, u32[]{:S(2)}, u32[]{:S(2)}) collective-permute-start(bf16[192,1024]{1,0:T(8,128)(2,1)S(1)} %get-tuple-element.36), channel_id=1, source_target_pairs={{0,2},{2,0},{4,6},{6,4},{8,10},{10,8},{12,14},{14,12},{1,3},{3,1},... | collective-permute-start | bytes 1179656 | tf_op jit(solution)/shard_map/ppermute | solution.py:180
  84.6 0.0 collective-permute-done.11
  84.6 1.0 slice_add_fusion.2
  85.6 0.1 collective-permute-start.12
  85.7 0.4 collective-permute-done.14
  86.1 0.1 convert_add_fusion.1
  86.2 2.3 %collective-permute-start.15 = (bf16[96,1024]{1,0:T(8,128)(2,1)S(1)}, bf16[96,1024]{1,0:T(8,128)(2,1)S(1)}, u32[]{:S(2)}, u32[]{:S(2)}) collective-permute-start(bf16[96,1024]{1,0:T(8,128)(2,1)S(1)} %slice.110), channel_id=1, source_target_pairs={{0,4},{2,6},{4,0},{6,2},{8,12},{10,14},{12,8},{14,10},{1,5},{3,7},... | collective-permute-start | bytes 589832 | tf_op jit(solution)/shard_map/ppermute | solution.py:180
  88.5 4.7 %collective-permute-done.17 = bf16[192,1024]{1,0:T(8,128)(2,1)S(1)} collective-permute-done((bf16[192,1024]{1,0:T(8,128)(2,1)S(1)}, bf16[192,1024]{1,0:T(8,128)(2,1)S(1)}, u32[]{:S(2)}, u32[]{:S(2)}) %collective-permute-start.17) | collective-permute-done | bytes 393248 | tf_op jit(solution)/shard_map/ppermute | solution.py:180
  93.2 0.1 convert_add_fusion
  93.4 1.5 %collective-permute-start.18 = (bf16[96,1024]{1,0:T(8,128)(2,1)S(1)}, bf16[96,1024]{1,0:T(8,128)(2,1)S(1)}, u32[]{:S(2)}, u32[]{:S(2)}) collective-permute-start(bf16[96,1024]{1,0:T(8,128)(2,1)S(1)} %slice.109), channel_id=1, source_target_pairs={{0,4},{2,6},{4,0},{6,2},{8,12},{10,14},{12,8},{14,10},{1,5},{3,7},... | collective-permute-start | bytes 589832 | tf_op jit(solution)/shard_map/ppermute | solution.py:180
  95.0 0.0 copy-start.3
  95.0 2.6 %collective-permute-start.16 = (bf16[48,1024]{1,0:T(8,128)(2,1)S(1)}, bf16[48,1024]{1,0:T(8,128)(2,1)S(1)}, u32[]{:S(2)}, u32[]{:S(2)}) collective-permute-start(bf16[48,1024]{1,0:T(8,128)(2,1)S(1)} %slice.114), channel_id=1, source_target_pairs={{0,8},{2,10},{4,12},{6,14},{8,0},{10,2},{12,4},{14,6},{1,9},{3,11}... | collective-permute-start | bytes 294920 | tf_op jit(solution)/shard_map/ppermute | solution.py:180
  97.6 3.4 %collective-permute-done.18 = bf16[96,1024]{1,0:T(8,128)(2,1)S(1)} collective-permute-done((bf16[96,1024]{1,0:T(8,128)(2,1)S(1)}, bf16[96,1024]{1,0:T(8,128)(2,1)S(1)}, u32[]{:S(2)}, u32[]{:S(2)}) %collective-permute-start.18) | collective-permute-done | bytes 196640 | tf_op jit(solution)/shard_map/ppermute | solution.py:180
  101.0 1.8 %collective-permute-start.19 = (bf16[48,1024]{1,0:T(8,128)(2,1)S(1)}, bf16[48,1024]{1,0:T(8,128)(2,1)S(1)}, u32[]{:S(2)}, u32[]{:S(2)}) collective-permute-start(bf16[48,1024]{1,0:T(8,128)(2,1)S(1)} %slice.113), channel_id=1, source_target_pairs={{0,8},{2,10},{4,12},{6,14},{8,0},{10,2},{12,4},{14,6},{1,9},{3,11}... | collective-permute-start | bytes 294920 | tf_op jit(solution)/shard_map/ppermute | solution.py:180
  102.8 0.1 compare_convert_fusion.live_ref
  103.0 4.3 %collective-permute-done.19.refs_7_ = bf16[48,1024]{1,0:T(8,128)(2,1)S(1)} collective-permute-done((bf16[48,1024]{1,0:T(8,128)(2,1)S(1)}, bf16[48,1024]{1,0:T(8,128)(2,1)S(1)}, u32[]{:S(2)}, u32[]{:S(2)}) %collective-permute-start.19) | collective-permute-done | bytes 98336 | tf_op jit(solution)/shard_map/ppermute | solution.py:180
  107.3 1.5 %finish.1 = bf16[3,2,16,2048]{3,2,1,0:T(8,128)(2,1)} custom-call(s32[3]{0:T(128)S(1)} %pad_add_fusion.scalars, s32[3]{0:T(128)S(1)} %compare_convert_fusion.live_ref, f32[1,2048]{1,0:T(1,128)S(1)} %bitcast.7, f32[48,1024]{1,0:T(8,128)S(1)} %slice.82.refs_0_, bf16[48,1024]{1,0:T(8,128)(2,1)S(1)} %collective-permute-done.9.refs_1_, ...), custom_call_target="tpu_custom_call" | custom-call | tf_op jit(solution)/shard_map/finish/pallas_call | solution.py:163
  (28 shorter events, 0.3 us)
Async XLA Ops:
  3.7 1.7 %copy-start.2 = (bf16[384,3200]{1,0:T(8,128)(2,1)S(1)}, bf16[384,3200]{1,0:T(8,128)(2,1)}, u32[]{:S(2)}) copy-start(bf16[384,3200]{1,0:T(8,128)(2,1)} %param.8) | copy-start | bytes 7372804
  5.4 11.4 %copy-start.5 = (s32[24]{0:T(128)S(1)}, s32[24]{0:T(128)}, u32[]{:S(2)}) copy-start(s32[24]{0:T(128)} %param.14) | copy-start | bytes 292
  7.8 9.2 %collective-permute-start = (bf16[48,1600]{1,0:T(8,128)(2,1)S(1)}, bf16[48,1600]{1,0:T(8,128)(2,1)S(1)}, u32[]{:S(2)}, u32[]{:S(2)}) collective-permute-start(bf16[48,1600]{1,0:T(8,128)(2,1)S(1)} %get-tuple-element.22), channel_id=1, source_target_pairs={{0,2},{2,0},{4,6},{6,4},{8,10},{10,8},{12,14},{14,12},{1,3},{3,1},... | collective-permute-start | bytes 460808 | tf_op jit(solution)/shard_map/ppermute | solution.py:180
  10.8 12.8 %collective-permute-start.1 = (bf16[48,1600]{1,0:T(8,128)(2,1)S(1)}, bf16[48,1600]{1,0:T(8,128)(2,1)S(1)}, u32[]{:S(2)}, u32[]{:S(2)}) collective-permute-start(bf16[48,1600]{1,0:T(8,128)(2,1)S(1)} %get-tuple-element.23), channel_id=1, source_target_pairs={{0,4},{2,6},{4,0},{6,2},{8,12},{10,14},{12,8},{14,10},{1,5},{3,7},... | collective-permute-start | bytes 460808 | tf_op jit(solution)/shard_map/ppermute | solution.py:180
  12.4 12.6 %collective-permute-start.2 = (bf16[48,1600]{1,0:T(8,128)(2,1)S(1)}, bf16[48,1600]{1,0:T(8,128)(2,1)S(1)}, u32[]{:S(2)}, u32[]{:S(2)}) collective-permute-start(bf16[48,1600]{1,0:T(8,128)(2,1)S(1)} %get-tuple-element.24), channel_id=1, source_target_pairs={{0,6},{2,4},{4,2},{6,0},{8,14},{10,12},{12,10},{14,8},{1,7},{3,5},... | collective-permute-start | bytes 460808 | tf_op jit(solution)/shard_map/ppermute | solution.py:180
  12.4 12.6 %collective-permute-start.3 = (bf16[48,1600]{1,0:T(8,128)(2,1)S(1)}, bf16[48,1600]{1,0:T(8,128)(2,1)S(1)}, u32[]{:S(2)}, u32[]{:S(2)}) collective-permute-start(bf16[48,1600]{1,0:T(8,128)(2,1)S(1)} %get-tuple-element.25), channel_id=1, source_target_pairs={{0,8},{2,10},{4,12},{6,14},{8,0},{10,2},{12,4},{14,6},{1,9},{3,11}... | collective-permute-start | bytes 460808 | tf_op jit(solution)/shard_map/ppermute | solution.py:180
  15.4 23.1 %collective-permute-start.4 = (bf16[48,1600]{1,0:T(8,128)(2,1)S(1)}, bf16[48,1600]{1,0:T(8,128)(2,1)S(1)}, u32[]{:S(2)}, u32[]{:S(2)}) collective-permute-start(bf16[48,1600]{1,0:T(8,128)(2,1)S(1)} %get-tuple-element.26), channel_id=1, source_target_pairs={{0,10},{2,8},{4,14},{6,12},{8,2},{10,0},{12,6},{14,4},{1,11},{3,9}... | collective-permute-start | bytes 460808 | tf_op jit(solution)/shard_map/ppermute | solution.py:180
  17.0 21.5 %collective-permute-start.5 = (bf16[48,1600]{1,0:T(8,128)(2,1)S(1)}, bf16[48,1600]{1,0:T(8,128)(2,1)S(1)}, u32[]{:S(2)}, u32[]{:S(2)}) collective-permute-start(bf16[48,1600]{1,0:T(8,128)(2,1)S(1)} %get-tuple-element.27), channel_id=1, source_target_pairs={{0,12},{2,14},{4,8},{6,10},{8,4},{10,6},{12,0},{14,2},{1,13},{3,15... | collective-permute-start | bytes 460808 | tf_op jit(solution)/shard_map/ppermute | solution.py:180
  23.6 14.8 %collective-permute-start.6 = (bf16[48,1600]{1,0:T(8,128)(2,1)S(1)}, bf16[48,1600]{1,0:T(8,128)(2,1)S(1)}, u32[]{:S(2)}, u32[]{:S(2)}) collective-permute-start(bf16[48,1600]{1,0:T(8,128)(2,1)S(1)} %get-tuple-element.28), channel_id=1, source_target_pairs={{0,14},{2,12},{4,10},{6,8},{8,6},{10,4},{12,2},{14,0},{1,15},{3,13... | collective-permute-start | bytes 460808 | tf_op jit(solution)/shard_map/ppermute | solution.py:180
  40.7 26.5 %collective-permute-start.13 = (bf16[384,1600]{0,1:T(8,128)(2,1)}, bf16[384,1600]{0,1:T(8,128)(2,1)}, u32[]{:S(2)}, u32[]{:S(2)}) collective-permute-start(bf16[384,1600]{0,1:T(8,128)(2,1)} %copy.12), channel_id=1, source_target_pairs={{0,1},{1,0},{2,3},{3,2},{4,5},{5,4},{6,7},{7,6},{8,9},{9,8},{10,11... | collective-permute-start | bytes 3686408 | tf_op jit(solution)/shard_map/ppermute | solution.py:220
  40.8 2.9 %copy-start = (bf16[1600,2048]{1,0:T(8,128)(2,1)S(1)}, bf16[1600,2048]{1,0:T(8,128)(2,1)}, u32[]{:S(2)}) copy-start(bf16[1600,2048]{1,0:T(8,128)(2,1)} %w_ref.7) | copy-start | bytes 19660804
  46.3 9.5 %copy-start.4 = (s32[8]{0:T(128)S(1)}, s32[8]{0:T(128)}, u32[]{:S(2)}) copy-start(s32[8]{0:T(128)} %param.13) | copy-start | bytes 100
  46.3 11.6 %collective-permute-start.7 = (bf16[192,1024]{1,0:T(8,128)(2,1)S(1)}, bf16[192,1024]{1,0:T(8,128)(2,1)S(1)}, u32[]{:S(2)}, u32[]{:S(2)}) collective-permute-start(bf16[192,1024]{1,0:T(8,128)(2,1)S(1)} %get-tuple-element.30), channel_id=1, source_target_pairs={{0,2},{2,0},{4,6},{6,4},{8,10},{10,8},{12,14},{14,12},{1,3},{3,1},... | collective-permute-start | bytes 1179656 | tf_op jit(solution)/shard_map/ppermute | solution.py:180
  49.9 15.7 %collective-permute-start.10 = (bf16[192,1024]{1,0:T(8,128)(2,1)S(1)}, bf16[192,1024]{1,0:T(8,128)(2,1)S(1)}, u32[]{:S(2)}, u32[]{:S(2)}) collective-permute-start(bf16[192,1024]{1,0:T(8,128)(2,1)S(1)} %get-tuple-element.32), channel_id=1, source_target_pairs={{0,4},{2,6},{4,0},{6,2},{8,12},{10,14},{12,8},{14,10},{1,5},{3,7},... | collective-permute-start | bytes 1179656 | tf_op jit(solution)/shard_map/ppermute | solution.py:180
  58.1 17.2 %collective-permute-start.8 = (bf16[96,1024]{1,0:T(8,128)(2,1)S(1)}, bf16[96,1024]{1,0:T(8,128)(2,1)}, u32[]{:S(2)}, u32[]{:S(2)}) collective-permute-start(bf16[96,1024]{1,0:T(8,128)(2,1)S(1)} %slice.112), channel_id=1, source_target_pairs={{0,4},{2,6},{4,0},{6,2},{8,12},{10,14},{12,8},{14,10},{1,5},{3,7},... | collective-permute-start | bytes 589832 | tf_op jit(solution)/shard_map/ppermute | solution.py:180
  65.7 18.8 %collective-permute-start.11 = (bf16[96,1024]{1,0:T(8,128)(2,1)S(1)}, bf16[96,1024]{1,0:T(8,128)(2,1)}, u32[]{:S(2)}, u32[]{:S(2)}) collective-permute-start(bf16[96,1024]{1,0:T(8,128)(2,1)S(1)} %slice.111), channel_id=1, source_target_pairs={{0,2},{2,0},{4,6},{6,4},{8,10},{10,8},{12,14},{14,12},{1,3},{3,1},... | collective-permute-start | bytes 589832 | tf_op jit(solution)/shard_map/ppermute | solution.py:180
  69.1 2.9 %copy-start.1 = (bf16[1600,2048]{1,0:T(8,128)(2,1)S(1)}, bf16[1600,2048]{1,0:T(8,128)(2,1)}, u32[]{:S(2)}) copy-start(bf16[1600,2048]{1,0:T(8,128)(2,1)} %w_ref.7) | copy-start | bytes 19660804
  74.7 11.4 %collective-permute-start.14 = (bf16[192,1024]{1,0:T(8,128)(2,1)S(1)}, bf16[192,1024]{1,0:T(8,128)(2,1)S(1)}, u32[]{:S(2)}, u32[]{:S(2)}) collective-permute-start(bf16[192,1024]{1,0:T(8,128)(2,1)S(1)} %get-tuple-element.34), channel_id=1, source_target_pairs={{0,2},{2,0},{4,6},{6,4},{8,10},{10,8},{12,14},{14,12},{1,3},{3,1},... | collective-permute-start | bytes 1179656 | tf_op jit(solution)/shard_map/ppermute | solution.py:180
  76.3 26.6 %collective-permute-start.9 = (bf16[48,1024]{1,0:T(8,128)(2,1)S(1)}, bf16[48,1024]{1,0:T(8,128)(2,1)S(1)}, u32[]{:S(2)}, u32[]{:S(2)}) collective-permute-start(bf16[48,1024]{1,0:T(8,128)(2,1)S(1)} %slice.116), channel_id=1, source_target_pairs={{0,8},{2,10},{4,12},{6,14},{8,0},{10,2},{12,4},{14,6},{1,9},{3,11}... | collective-permute-start | bytes 294920 | tf_op jit(solution)/shard_map/ppermute | solution.py:180
  82.7 10.6 %collective-permute-start.17 = (bf16[192,1024]{1,0:T(8,128)(2,1)S(1)}, bf16[192,1024]{1,0:T(8,128)(2,1)S(1)}, u32[]{:S(2)}, u32[]{:S(2)}) collective-permute-start(bf16[192,1024]{1,0:T(8,128)(2,1)S(1)} %get-tuple-element.36), channel_id=1, source_target_pairs={{0,2},{2,0},{4,6},{6,4},{8,10},{10,8},{12,14},{14,12},{1,3},{3,1},... | collective-permute-start | bytes 1179656 | tf_op jit(solution)/shard_map/ppermute | solution.py:180
  85.6 17.4 %collective-permute-start.12 = (bf16[48,1024]{1,0:T(8,128)(2,1)S(1)}, bf16[48,1024]{1,0:T(8,128)(2,1)S(1)}, u32[]{:S(2)}, u32[]{:S(2)}) collective-permute-start(bf16[48,1024]{1,0:T(8,128)(2,1)S(1)} %slice.115), channel_id=1, source_target_pairs={{0,8},{2,10},{4,12},{6,14},{8,0},{10,2},{12,4},{14,6},{1,9},{3,11}... | collective-permute-start | bytes 294920 | tf_op jit(solution)/shard_map/ppermute | solution.py:180
  86.2 8.7 %collective-permute-start.15 = (bf16[96,1024]{1,0:T(8,128)(2,1)S(1)}, bf16[96,1024]{1,0:T(8,128)(2,1)S(1)}, u32[]{:S(2)}, u32[]{:S(2)}) collective-permute-start(bf16[96,1024]{1,0:T(8,128)(2,1)S(1)} %slice.110), channel_id=1, source_target_pairs={{0,4},{2,6},{4,0},{6,2},{8,12},{10,14},{12,8},{14,10},{1,5},{3,7},... | collective-permute-start | bytes 589832 | tf_op jit(solution)/shard_map/ppermute | solution.py:180
  93.4 7.6 %collective-permute-start.18 = (bf16[96,1024]{1,0:T(8,128)(2,1)S(1)}, bf16[96,1024]{1,0:T(8,128)(2,1)S(1)}, u32[]{:S(2)}, u32[]{:S(2)}) collective-permute-start(bf16[96,1024]{1,0:T(8,128)(2,1)S(1)} %slice.109), channel_id=1, source_target_pairs={{0,4},{2,6},{4,0},{6,2},{8,12},{10,14},{12,8},{14,10},{1,5},{3,7},... | collective-permute-start | bytes 589832 | tf_op jit(solution)/shard_map/ppermute | solution.py:180
  95.0 12.4 %copy-start.3 = (f32[2048]{0:T(1024)S(1)}, f32[2048]{0:T(1024)}, u32[]{:S(2)}) copy-start(f32[2048]{0:T(1024)} %param.12) | copy-start | bytes 24580
  95.0 8.0 %collective-permute-start.16 = (bf16[48,1024]{1,0:T(8,128)(2,1)S(1)}, bf16[48,1024]{1,0:T(8,128)(2,1)S(1)}, u32[]{:S(2)}, u32[]{:S(2)}) collective-permute-start(bf16[48,1024]{1,0:T(8,128)(2,1)S(1)} %slice.114), channel_id=1, source_target_pairs={{0,8},{2,10},{4,12},{6,14},{8,0},{10,2},{12,4},{14,6},{1,9},{3,11}... | collective-permute-start | bytes 294920 | tf_op jit(solution)/shard_map/ppermute | solution.py:180
  101.0 6.3 %collective-permute-start.19 = (bf16[48,1024]{1,0:T(8,128)(2,1)S(1)}, bf16[48,1024]{1,0:T(8,128)(2,1)S(1)}, u32[]{:S(2)}, u32[]{:S(2)}) collective-permute-start(bf16[48,1024]{1,0:T(8,128)(2,1)S(1)} %slice.113), channel_id=1, source_target_pairs={{0,8},{2,10},{4,12},{6,14},{8,0},{10,2},{12,4},{14,6},{1,9},{3,11}... | collective-permute-start | bytes 294920 | tf_op jit(solution)/shard_map/ppermute | solution.py:180

commit v2 on v0

v2 whole, which is shorter than its diff:
```python
import functools
import math

import jax
import jax.numpy as jnp
from jax import lax
from jax.experimental import pallas as pl
from jax.experimental.pallas import tpu as pltpu
from jax.sharding import PartitionSpec as P

TILE = 128
TILE_ROWS = TILE // 4
PHASES = 2
PART = TILE_ROWS // PHASES
VMEM_LIMIT = 16 * 1024 * 1024
BIG_VMEM = 20 * 1024 * 1024
PROJECT_VMEM = 20 * 1024 * 1024
LANES = 128
STEPS = [(0, 0), (1, 0), (2, -1), (0, 1), (2, 0), (1, 1), (3, 0), (0, 2), (2, 1), (1, 2), (3, 1), (2, 2), (3, 2)]


def arrangement(bits):
    if not bits:
        return [0]
    rest = arrangement(bits[1:])
    return [owner ^ (1 << bits[0]) for owner in rest] + rest


def in_hbm(array):
    return pltpu.with_memory_space_constraint(array, pltpu.HBM)


def routes(peers):
    if peers == 8:
        return [[2, 4, 5, 1], [3, 6, 7, 0]]
    order = list(reversed(range(peers)))
    return [order[0::2], order[1::2]]


def prepare_kernel(peers, tiles, phase, x_hbm, gain_hbm, shift_hbm, count_hbm, *refs):
    outs, (pieces, x_ref, gain_ref, shift_ref, count_ref, sems) = refs[-6 - peers // 2:-6], refs[-6:]
    me, core = lax.axis_index("dp"), lax.axis_index("tensor")
    width = x_hbm.shape[-1]
    total = 4 * width
    block_width = total // peers
    per_patch = width // block_width
    rows = tiles * PART
    copies = [
        pltpu.make_async_copy(x_hbm.at[:, phase], x_ref, sems.at[0]),
        pltpu.make_async_copy(gain_hbm, gain_ref, sems.at[1]),
        pltpu.make_async_copy(shift_hbm, shift_ref, sems.at[2]),
        pltpu.make_async_copy(count_hbm, count_ref, sems.at[3]),
    ]
    for copy in copies:
        copy.start()
    row_out = lax.broadcasted_iota(jnp.int32, (4 * rows, 4 * rows), 0)
    row_in = lax.broadcasted_iota(jnp.int32, (4 * rows, 4 * rows), 1)
    quarter = sum((row_out >= q * rows).astype(jnp.int32) for q in range(1, 4))
    source = 4 * (row_out - quarter * rows) + quarter
    mix = (row_in == source).astype(jnp.bfloat16)
    tile_of = lax.broadcasted_iota(jnp.int32, (rows, 1), 0) // PART
    for copy in copies:
        copy.wait()
    live = tile_of < count_ref[me]
    x = x_ref[...].reshape(4 * rows, width)
    y = jnp.dot(mix, x, preferred_element_type=jnp.float32)
    parts = [y[q * rows:(q + 1) * rows] for q in range(4)]
    mean = sum(jnp.sum(part, axis=1, keepdims=True) for part in parts) / total
    parts = [part - mean for part in parts]
    variance = sum(jnp.sum(part * part, axis=1, keepdims=True) for part in parts) / total
    scale = lax.rsqrt(variance + 1e-06)
    for q in range(4):
        normed = []
        for lane in range(width // LANES):
            at = pl.ds(q * (width // LANES) + lane, 1)
            part = parts[q][:, lane * LANES:(lane + 1) * LANES]
            normed.append(part * scale * gain_ref[at, :] + shift_ref[at, :])
        normed = jnp.concatenate(normed, axis=1)
        normed = jnp.where(live, normed, 0.0).astype(jnp.bfloat16)
        for part in range(per_patch):
            pieces[q * per_patch + part] = normed[:, part * block_width:(part + 1) * block_width]
    for out, first, second in zip(outs, *routes(peers)):
        out[...] = pieces[jnp.bitwise_xor(me, jnp.where(core == 0, first, second))]


def prepare(tile_count, patch_feats, ln_gain, ln_shift, peers, tiles, phase, after):
    width = patch_feats.shape[1]
    block_width = 4 * width // peers
    rows = tiles * PART
    x = patch_feats.reshape(tiles, PHASES, 4 * PART, width)
    vectors = (4 * width // LANES, LANES)
    operands = [x, ln_gain.reshape(vectors), ln_shift.reshape(vectors), tile_count]
    return pl.pallas_call(
        functools.partial(prepare_kernel, peers, tiles, phase),
        in_specs=[pl.BlockSpec(memory_space=pl.ANY)] * (4 + len(after)),
        out_specs=[pl.BlockSpec(memory_space=pltpu.VMEM)] * (peers // 2),
        scratch_shapes=[
            pltpu.VMEM((peers, rows, block_width), jnp.bfloat16),
            pltpu.VMEM((tiles, 4 * PART, width), jnp.bfloat16),
            pltpu.VMEM(vectors, jnp.float32),
            pltpu.VMEM(vectors, jnp.float32),
            pltpu.SMEM(tile_count.shape, jnp.int32),
            pltpu.SemaphoreType.DMA((4,)),
        ],
        out_shape=[pltpu.VMEM((rows, block_width), jnp.bfloat16)] * (peers // 2),
        compiler_params=pltpu.CompilerParams(vmem_limit_bytes=BIG_VMEM),
        cost_estimate=pl.CostEstimate(flops=0, bytes_accessed=32 * rows * width, transcendentals=0),
        name="prepare",
    )(*[in_hbm(operand) for operand in operands], *after)


def scatter_pieces(pieces, peers):
    received = []
    for piece, first, second in zip(pieces, *routes(peers)):
        pairs = [(2 * d, 2 * (d ^ first)) for d in range(peers)]
        pairs += [(2 * d + 1, 2 * (d ^ second) + 1) for d in range(peers) if second != 0]
        received.append(lax.ppermute(piece, ("dp", "tensor"), pairs))
    return received


def pack_kernel(count, own_index, *refs):
    pieces, own, out = refs[:count], refs[count], refs[-1]
    rows, width = own.shape
    if out.shape[1] > width:
        out[:, width:] = jnp.zeros((out.shape[0], out.shape[1] - width), out.dtype)
    for i, piece in enumerate(pieces):
        value = piece[...]
        if i == own_index:
            value = jnp.where(lax.axis_index("tensor") == 0, value, own[...])
        out[i * rows:(i + 1) * rows, :width] = value


def pack(received, own, after):
    own_index = routes(2 * len(received))[1].index(0)
    rows, width = own.shape
    padded = -(-width // LANES) * LANES
    inside = pl.BlockSpec(memory_space=pltpu.VMEM)
    return pl.pallas_call(
        functools.partial(pack_kernel, len(received), own_index),
        in_specs=[inside] * (len(received) + 1) + [pl.BlockSpec(memory_space=pl.ANY)] * len(after),
        out_specs=inside,
        out_shape=pltpu.VMEM((len(received) * rows, padded), jnp.bfloat16),
        compiler_params=pltpu.CompilerParams(vmem_limit_bytes=VMEM_LIMIT),
        name="pack",
    )(*received, own, *after)


def load_kernel(w_hbm, *refs):
    w_ref, sem = refs[-2:]
    copy = pltpu.make_async_copy(w_hbm, w_ref, sem)
    copy.start()
    copy.wait()


def load(array, after):
    return pl.pallas_call(
        load_kernel,
        in_specs=[pl.BlockSpec(memory_space=pl.ANY)] * (1 + len(after)),
        out_specs=pl.BlockSpec(memory_space=pltpu.VMEM),
        out_shape=pltpu.VMEM(array.shape, array.dtype),
        scratch_shapes=[pltpu.SemaphoreType.DMA],
        compiler_params=pltpu.CompilerParams(vmem_limit_bytes=VMEM_LIMIT),
        cost_estimate=pl.CostEstimate(flops=0, bytes_accessed=4 * array.size, transcendentals=0),
        name="load",
    )(in_hbm(array), *after)


def multiply(first, block, a_ref, w_ref, send_ref, keep_ref):
    half = a_ref.shape[0] // 2
    for column in range(0, send_ref.shape[1], block):
        w = w_ref[:, first + column:first + column + block]
        acc = jnp.dot(a_ref[:, :w.shape[0]], w, preferred_element_type=jnp.float32)
        acc = acc.astype(jnp.bfloat16)
        send_ref[:, column:column + block] = acc[:half]
        keep_ref[:, column:column + block] = acc[half:]


def project_kernel(first, block, a_ref, w_ref, *refs):
    multiply(first, block, a_ref, w_ref, *refs[-2:])


def gather_kernel(first, block, order_ref, mine_ref, other_ref, w_ref, *refs):
    sorted_ref, send_ref, keep_ref, held = refs[-4:]
    core = lax.axis_index("tensor")
    held[core] = mine_ref[...]
    held[1 - core] = other_ref[...]
    half = mine_ref.shape[0] // PART
    for i in range(sorted_ref.shape[0] // PART):
        place = order_ref[i]
        side = (place >= half).astype(jnp.int32)
        start = pl.multiple_of((place - side * half) * PART, PART)
        sorted_ref[pl.ds(i * PART, PART), :] = held[side, pl.ds(start, PART), :]
    multiply(first, block, sorted_ref, w_ref, send_ref, keep_ref)


def cost(rows, depth, columns):
    return pl.CostEstimate(
        flops=2 * rows * depth * columns,
        bytes_accessed=2 * (rows * depth + depth * columns + rows * columns),
        transcendentals=0,
    )


def project(a, weight, first, columns, after, block=256):
    rows = a.shape[0]
    depth = weight.shape[0]
    half = pltpu.VMEM((rows // 2, columns), jnp.bfloat16)
    inside, outside = pl.BlockSpec(memory_space=pltpu.VMEM), pl.BlockSpec(memory_space=pl.ANY)
    return pl.pallas_call(
        functools.partial(project_kernel, first, block),
        in_specs=[inside] * 2 + [outside] * len(after),
        out_specs=[inside] * 2,
        out_shape=[half, half],
        compiler_params=pltpu.CompilerParams(vmem_limit_bytes=PROJECT_VMEM),
        cost_estimate=cost(rows, depth, columns),
        name="project",
    )(a, weight, *after)


def gather_and_project(order, mine, other, weight, first, columns, after, block=256):
    rows, padded = mine.shape
    depth = weight.shape[0]
    half = pltpu.VMEM((rows, columns), jnp.bfloat16)
    inside, outside = pl.BlockSpec(memory_space=pltpu.VMEM), pl.BlockSpec(memory_space=pl.ANY)
    return pl.pallas_call(
        functools.partial(gather_kernel, first, block),
        in_specs=[pl.BlockSpec(memory_space=pltpu.SMEM)] + [inside] * 3 + [outside] * len(after),
        out_specs=[inside] * 3,
        out_shape=[pltpu.VMEM((2 * rows, padded), jnp.bfloat16), half, half],
        scratch_shapes=[pltpu.VMEM((2, rows, padded), jnp.bfloat16)],
        compiler_params=pltpu.CompilerParams(vmem_limit_bytes=PROJECT_VMEM),
        cost_estimate=cost(2 * rows, depth, columns),
        name="gather_and_project",
    )(order, mine, other, weight, *after)


def activate(bias_ref, first, keep_ref, recv_ref):
    summed = keep_ref[...].astype(jnp.float32) + recv_ref[...].astype(jnp.float32)
    summed += bias_ref[:, first:first + summed.shape[1]]
    return (0.5 * summed * (1.0 + lax.erf(summed * 0.7071067811865476))).astype(jnp.bfloat16)


def early_kernel(first, bias_ref, keep_ref, recv_ref, *refs):
    refs[-1][...] = activate(bias_ref, first, keep_ref, recv_ref)


def early(bias, first, keep, recv, after):
    inside, outside = pl.BlockSpec(memory_space=pltpu.VMEM), pl.BlockSpec(memory_space=pl.ANY)
    return pl.pallas_call(
        functools.partial(early_kernel, first),
        in_specs=[inside] * 3 + [outside] * len(after),
        out_specs=inside,
        out_shape=pltpu.VMEM(keep.shape, jnp.bfloat16),
        compiler_params=pltpu.CompilerParams(vmem_limit_bytes=VMEM_LIMIT),
        name="early",
    )(bias.reshape(1, -1), keep, recv, *after)


def finish_kernel(tiles, chunks, live_ref, bias_ref, *refs):
    out, refs = refs[-1], list(refs[:-1])
    for phase, first, columns, count in chunks:
        parts, refs = refs[:count], refs[count:]
        value = parts[0][...] if count == 1 else activate(bias_ref, first, *parts)
        for tile in range(tiles):
            rows = value[tile * PART:(tile + 1) * PART]
            rows = jnp.where(live_ref[tile] > 0, rows, jnp.zeros_like(rows))
            out[tile, phase, :, first:first + columns] = rows


def finish(live, bias, chunks, flows, tiles):
    width = bias.shape[0]
    chunks = [chunk + (len(flow),) for chunk, flow in zip(chunks, flows)]
    flat = [array for flow in flows for array in flow]
    inside = pl.BlockSpec(memory_space=pltpu.VMEM)
    out = pl.pallas_call(
        functools.partial(finish_kernel, tiles, chunks),
        in_specs=[pl.BlockSpec(memory_space=pltpu.SMEM), inside] + [inside] * len(flat),
        out_specs=inside,
        out_shape=jax.ShapeDtypeStruct((tiles, PHASES, PART, width), jnp.bfloat16),
        compiler_params=pltpu.CompilerParams(vmem_limit_bytes=VMEM_LIMIT),
        name="finish",
    )(live, bias.reshape(1, width), *flat)
    return out.reshape(tiles * TILE_ROWS, width)


def exchange(array, masks, peers):
    pairs = [(2 * d + core, 2 * (d ^ mask) + core) for core, mask in enumerate(masks) for d in range(peers)]
    return lax.ppermute(array, ("dp", "tensor"), pairs)


def accumulate_kernel(count, *refs):
    send_out, keep_out = refs[-2:]
    half = send_out.shape[0]
    start = 0
    for index in range(count):
        keep_ref, recv_ref = refs[2 * index], refs[2 * index + 1]
        at = slice(start, start + keep_ref.shape[1])
        start = at.stop
        summed = keep_ref[...].astype(jnp.float32) + recv_ref[...].astype(jnp.float32)
        send_out[:, at] = summed[:half].astype(jnp.bfloat16)
        keep_out[:, at] = summed[half:]


def accumulate(flows, after):
    rows = flows[0][0].shape[0] // 2
    columns = sum(keep.shape[1] for keep, _ in flows)
    inside, outside = pl.BlockSpec(memory_space=pltpu.VMEM), pl.BlockSpec(memory_space=pl.ANY)
    return pl.pallas_call(
        functools.partial(accumulate_kernel, len(flows)),
        in_specs=[inside] * (2 * len(flows)) + [outside] * len(after),
        out_specs=[inside, inside],
        out_shape=[pltpu.VMEM((rows, columns), jnp.bfloat16), pltpu.VMEM((rows, columns), jnp.float32)],
        compiler_params=pltpu.CompilerParams(vmem_limit_bytes=VMEM_LIMIT),
        name="accumulate",
    )(*[array for flow in flows for array in flow], *after)


def body(patch_feats, ln_gain, ln_shift, merge_weight, merge_bias, tile_count, tile_dest):
    peers = lax.axis_size("dp")
    me = lax.axis_index("dp").astype(jnp.int32)
    tiles = patch_feats.shape[0] // TILE
    slots = peers * tiles
    bits = list(range(peers.bit_length() - 1))
    columns = merge_weight.shape[1]

    source_ids = jnp.arange(peers, dtype=jnp.int32)
    sequences = [bits, [bits[1], bits[0]] + bits[2:]]
    first_core = (lax.axis_index("tensor") == 0).astype(jnp.int32)
    owners = [jnp.array(arrangement(sequence), jnp.int32) for sequence in sequences]
    owners = jnp.where(first_core == 1, *owners) ^ me
    wanted = (owners[:, None] * tiles + jnp.arange(tiles, dtype=jnp.int32)[None, :]).reshape(slots)
    tile_ids = jnp.arange(slots, dtype=jnp.int32)
    anchor = jnp.sum(jnp.where(tile_dest[None, :] == wanted[:, None], tile_ids[None, :], 0), axis=1)
    source, place = anchor // tiles, anchor % tiles
    sequence = jnp.array(sum(routes(peers), []), jnp.int32)
    is_there = sequence[None, :] == (source ^ me)[:, None]
    order = jnp.sum(jnp.where(is_there, source_ids[None, :], 0), axis=1) * tiles + place
    own_source, own_place = source[-tiles:], place[-tiles:]
    own_count = jnp.sum(jnp.where(own_source[:, None] == source_ids[None, :], tile_count[None, :], 0), axis=1)
    live = (own_place < own_count).astype(jnp.int32)

    half = columns // 2
    chunks = [(0, 0, half), (0, half, half), (1, 0, half), (1, half, half)]
    pieces = [prepare(tile_count, patch_feats, ln_gain, ln_shift, peers, tiles, 0, [])]
    pieces.append(prepare(tile_count, patch_feats, ln_gain, ln_shift, peers, tiles, 1, pieces[0][:1]))
    scattered = [scatter_pieces(parts, peers) for parts in pieces]
    packed = {}

    flows, done, after = {}, {}, []
    steps = STEPS
    if len(bits) != 3:
        steps = [(index, step) for step in range(len(bits)) for index in range(len(chunks))]
    for index, step in steps:
        phase, first, count = chunks[index]
        if step < 0 or (step == 0 and first == 0 and phase not in packed):
            mine = pack(scattered[phase], pieces[phase][routes(peers)[1].index(0)], after)
            packed[phase] = mine, lax.ppermute(mine, "tensor", [(0, 1), (1, 0)])
            after = [mine]
            if phase == 0:
                weight = load(merge_weight, after)
            if step < 0:
                continue
        if step == len(bits):
            done[index] = early(merge_bias, first, *flows[index], after)
            after = [done[index]]
            continue
        if step > 0:
            send, keep = accumulate([flows[index]], after)
        elif first == 0:
            rows, send, keep = gather_and_project(order, *packed[phase], weight, first, count, after)
        else:
            send, keep = project(rows, weight, first, count, after)
        after = [keep]
        flows[index] = (keep, exchange(send, [1 << sequence[step] for sequence in sequences], peers))
    flows = [(done[i],) if i in done else flows[i] for i in range(len(chunks))]
    return finish(live, merge_bias, chunks, flows, tiles)


def solution(mesh):
    in_specs = (
        P(("group", "dp"), None),
        P(),
        P(),
        P("dp", "tensor"),
        P("tensor"),
        P("group"),
        P("group"),
    )
    out_specs = P(("group", "dp"), "tensor")
    return jax.shard_map(body, mesh=mesh, in_specs=in_specs, out_specs=out_specs, check_vma=False)
```

time: 185 us -> 85.7 us (0.46)
  waiting for transfers between devices: 124 us -> 36.3 us
  starting transfers between devices: 7.32 us -> 29.3 us
  Pallas kernels: 0 us -> 18.8 us
  other arithmetic: 16.4 us -> 0.63 us
  between operations: 13.6 us -> 0.27 us
  local copies, waits for them, and re-layouts: 12.9 us -> 0.19 us
  matrix products: 10.7 us -> 0 us
    reduce_scatter x1 -> x0, waiting for transfers between devices: 67.1 us -> none  [body(): lax.psum_scatter(jnp.dot(row_block, merge_weight, preferred_element_type=...]
    all_to_all x1 -> x0, waiting for transfers between devices: 57.1 us -> none  [body(): lax.all_to_all(pieces, 'dp', split_axis=1, concat_axis=0, tiled=True)]
    ppermute x0 -> x22, waiting for transfers between devices: none -> 36.3 us  [the longest x12 25 us: exchange(): return lax.ppermute(array, ('dp', 'tensor'), pairs)]
    ppermute x0 -> x22, starting transfers between devices: none -> 29.3 us  [the longest x12 17.6 us: exchange(): return lax.ppermute(array, ('dp', 'tensor'), pairs)]
    pallas_call x0 -> x18, Pallas kernels: none -> 18.8 us  [the longest x2 6.11 us: prepare(): pl.pallas_call(functools.partial(prepare_kernel, peers, tiles, phase), in...]
    dot_general x1 -> x0, matrix products: 10.7 us -> none  [body(): jnp.dot(row_block, merge_weight, preferred_element_type=jnp.float32)]
    convert_element_type x2 -> x1, other arithmetic: 8.91 us -> 0.07 us  [body(): live = (own_place < own_count).astype(jnp.int32)]
    all_to_all x1 -> x0, starting transfers between devices: 7.28 us -> none  [body(): lax.all_to_all(pieces, 'dp', split_axis=1, concat_axis=0, tiled=True)]
  transfers between devices with their start and end apart: 2 -> 22, of which waited for: 2 -> 13; matrix products, arithmetic and copies ran while one was open for 4% -> 1% of each run, Pallas kernels for 0% -> 17%
where the time goes in v2:
time: 85.7 us; the launch traced here: 85.4 us
  waiting for transfers between devices  36.3 us (42%)
  starting transfers between devices  29.3 us (34%)
  Pallas kernels  18.8 us (22%)
    ppermute x12, waiting for transfers between devices, exchange(): return lax.ppermute(array, ('dp', 'tensor'), pairs)  25 us
    ppermute x12, starting transfers between devices, exchange(): return lax.ppermute(array, ('dp', 'tensor'), pairs)  17.6 us
    ppermute x8, starting transfers between devices, scatter_pieces(): received.append(lax.ppermute(piece, ('dp', 'tensor'), pairs))  11.5 us
    ppermute x8, waiting for transfers between devices, scatter_pieces(): received.append(lax.ppermute(piece, ('dp', 'tensor'), pairs))  11.3 us
    pallas_call x2, Pallas kernels, prepare(): pl.pallas_call(functools.partial(prepare_kernel, peers, tiles, phase), in...  6.11 us
    pallas_call x2, Pallas kernels, gather_and_project(): pl.pallas_call(functools.partial(gather_kernel, first, block), in_specs=[...  4.45 us
    pallas_call x2, Pallas kernels, project(): pl.pallas_call(functools.partial(project_kernel, first, block), in_specs=...  3.23 us
    pallas_call x1, Pallas kernels, load(): pl.pallas_call(load_kernel, in_specs=[pl.BlockSpec(memory_space=pl.ANY)]...  2.87 us
  transfers between devices with their start and end apart: 22, of which 13 were waited for; matrix products, arithmetic and copies ran while one was open for 1% of the time, Pallas kernels for 17%

profile of v2, /device:TPU:0, one launch (start us, length us, event | category | flops | bytes accessed | tf_op | source)
XLA Modules:
  0.0 85.4 jit_solution(8731894486990035638)
XLA Ops:
  0.0 3.1 %prepare.2 = (bf16[48,1600]{1,0:T(8,128)(2,1)S(1)}, bf16[48,1600]{1,0:T(8,128)(2,1)S(1)}, bf16[48,1600]{1,0:T(8,128)(2,1)S(1)}, bf16[48,1600]{1,0:T(8,128)(2,1)S(1)}) custom-call(bf16[3,2,64,3200]{3,2,1,0:T(8,128)(2,1)} %bitcast.6, f32[100,128]{1,0:T(8,128)} %bitcast.8, f32[100,128]{1,0:T(8,128)} %bitcast.10, s32[8]{0:T(128)} %count_hbm.3), custom_call_target="tpu_custom_call" | custom-call | bytes 4915200 | tf_op jit(solution)/shard_map/prepare/pallas_call | solution.py:93
  3.1 0.0 copy-start.4
  3.1 0.0 copy-start.5
  3.1 4.1 %collective-permute-start.1 = (bf16[48,1600]{1,0:T(8,128)(2,1)S(1)}, bf16[48,1600]{1,0:T(8,128)(2,1)S(1)}, u32[]{:S(2)}, u32[]{:S(2)}) collective-permute-start(bf16[48,1600]{1,0:T(8,128)(2,1)S(1)} %get-tuple-element.40), channel_id=1, source_target_pairs={{0,8},{2,10},{4,12},{6,14},{8,0},{10,2},{12,4},{14,6},{1,13},{3,15... | collective-permute-start | bytes 460808 | tf_op jit(solution)/shard_map/ppermute | solution.py:117
  7.2 1.3 %collective-permute-start.2 = (bf16[48,1600]{1,0:T(8,128)(2,1)S(1)}, bf16[48,1600]{1,0:T(8,128)(2,1)S(1)}, u32[]{:S(2)}, u32[]{:S(2)}) collective-permute-start(bf16[48,1600]{1,0:T(8,128)(2,1)S(1)} %get-tuple-element.41), channel_id=1, source_target_pairs={{0,10},{2,8},{4,14},{6,12},{8,2},{10,0},{12,6},{14,4},{1,15},{3,13... | collective-permute-start | bytes 460808 | tf_op jit(solution)/shard_map/ppermute | solution.py:117
  8.5 1.6 %collective-permute-start = (bf16[48,1600]{1,0:T(8,128)(2,1)S(1)}, bf16[48,1600]{1,0:T(8,128)(2,1)S(1)}, u32[]{:S(2)}, u32[]{:S(2)}) collective-permute-start(bf16[48,1600]{1,0:T(8,128)(2,1)S(1)} %get-tuple-element.39.refs_0_), channel_id=1, source_target_pairs={{0,4},{2,6},{4,0},{6,2},{8,12},{10,14},{12,8},{14,10},{1,7},{3,5},... | collective-permute-start | bytes 460808 | tf_op jit(solution)/shard_map/ppermute | solution.py:117
  10.1 2.4 %collective-permute-start.3 = (bf16[48,1600]{1,0:T(8,128)(2,1)S(1)}, bf16[48,1600]{1,0:T(8,128)(2,1)S(1)}, u32[]{:S(2)}, u32[]{:S(2)}) collective-permute-start(bf16[48,1600]{1,0:T(8,128)(2,1)S(1)} %get-tuple-element.42.refs_4_), channel_id=1, source_target_pairs={{0,2},{2,0},{4,6},{6,4},{8,10},{10,8},{12,14},{14,12},{16,18},{18,... | collective-permute-start | bytes 460808 | tf_op jit(solution)/shard_map/ppermute | solution.py:117
  12.5 3.0 %prepare.3 = (bf16[48,1600]{1,0:T(8,128)(2,1)S(1)}, bf16[48,1600]{1,0:T(8,128)(2,1)S(1)}, bf16[48,1600]{1,0:T(8,128)(2,1)S(1)}, bf16[48,1600]{1,0:T(8,128)(2,1)S(1)}) custom-call(bf16[3,2,64,3200]{3,2,1,0:T(8,128)(2,1)} %bitcast.7, f32[100,128]{1,0:T(8,128)} %bitcast.9, f32[100,128]{1,0:T(8,128)} %bitcast.11, s32[8]{0:T(128)} %count_hbm.3, ...), custom_call_target="tpu_custom_call" | custom-call | bytes 4915200 | tf_op jit(solution)/shard_map/prepare/pallas_call | solution.py:93
  15.5 0.3 collective-permute-start.6
  15.8 0.1 iota_add_fusion
  15.9 0.1 add.37
  16.0 3.0 %collective-permute-done.1.refs_1_ = bf16[48,1600]{1,0:T(8,128)(2,1)S(1)} collective-permute-done((bf16[48,1600]{1,0:T(8,128)(2,1)S(1)}, bf16[48,1600]{1,0:T(8,128)(2,1)S(1)}, u32[]{:S(2)}, u32[]{:S(2)}) %collective-permute-start.1) | collective-permute-done | bytes 153632 | tf_op jit(solution)/shard_map/ppermute | solution.py:117
  19.0 6.0 %collective-permute-done.2.refs_2_ = bf16[48,1600]{1,0:T(8,128)(2,1)S(1)} collective-permute-done((bf16[48,1600]{1,0:T(8,128)(2,1)S(1)}, bf16[48,1600]{1,0:T(8,128)(2,1)S(1)}, u32[]{:S(2)}, u32[]{:S(2)}) %collective-permute-start.2) | collective-permute-done | bytes 153632 | tf_op jit(solution)/shard_map/ppermute | solution.py:117
  25.0 0.0 collective-permute-start.8
  25.0 0.0 collective-permute-done.refs_0_
  25.0 1.9 %collective-permute-start.9 = (bf16[48,1600]{1,0:T(8,128)(2,1)S(1)}, bf16[48,1600]{1,0:T(8,128)(2,1)S(1)}, u32[]{:S(2)}, u32[]{:S(2)}) collective-permute-start(bf16[48,1600]{1,0:T(8,128)(2,1)S(1)} %get-tuple-element.48.refs_4_), channel_id=1, source_target_pairs={{0,2},{2,0},{4,6},{6,4},{8,10},{10,8},{12,14},{14,12},{16,18},{18,... | collective-permute-start | bytes 460808 | tf_op jit(solution)/shard_map/ppermute | solution.py:117
  26.9 0.0 collective-permute-done.3.refs_3_
  26.9 0.1 pack.2.refs_0_.mine_ref
  27.0 0.1 collective-permute-start.4
  27.1 0.2 select_reduce_fusion
  27.3 0.1 select_reduce_fusion.1
  27.4 2.9 %load.1.w_ref = bf16[1600,2048]{1,0:T(8,128)(2,1)S(1)} custom-call(bf16[1600,2048]{1,0:T(8,128)(2,1)} %w_hbm.1, bf16[192,1664]{1,0:T(8,128)(2,1)S(1)} %pack.2.refs_0_.mine_ref), custom_call_target="tpu_custom_call" | custom-call | bytes 13107200 | tf_op jit(solution)/shard_map/load/pallas_call | solution.py:156
  30.3 2.2 %gather_and_project.2 = (bf16[384,1664]{1,0:T(8,128)(2,1)S(1)}, bf16[192,1024]{1,0:T(8,128)(2,1)S(1)}, bf16[192,1024]{1,0:T(8,128)(2,1)S(1)}) custom-call(s32[24]{0:T(128)S(1)} %get-tuple-element.73.order_ref, bf16[192,1664]{1,0:T(8,128)(2,1)S(1)} %pack.2.refs_0_.mine_ref, bf16[192,1664]{1,0:T(8,128)(2,1)S(1)} %collective-permute-done.4.other_ref, ...), custom_call_target="tpu_custom_call" | custom-call | flops 1258291200 | bytes 5292032 | tf_op jit(solution)/shard_map/gather_and_project/pallas_call | solution.py:225
  32.5 1.6 %project.2 = (bf16[192,1024]{1,0:T(8,128)(2,1)S(1)}, bf16[192,1024]{1,0:T(8,128)(2,1)S(1)}) custom-call(bf16[384,1664]{1,0:T(8,128)(2,1)S(1)} %get-tuple-element.49.a_ref, bf16[1600,2048]{1,0:T(8,128)(2,1)S(1)} %load.1.w_ref, bf16[192,1024]{1,0:T(8,128)(2,1)S(1)} %get-tuple-element.43.refs_0_), custom_call_target="tpu_custom_call" | custom-call | flops 1258291200 | bytes 5292032 | tf_op jit(solution)/shard_map/project/pallas_call | solution.py:209
  34.1 0.0 collective-permute-done.7.refs_1_
  34.2 2.2 %collective-permute-done.8.refs_2_ = bf16[48,1600]{1,0:T(8,128)(2,1)S(1)} collective-permute-done((bf16[48,1600]{1,0:T(8,128)(2,1)S(1)}, bf16[48,1600]{1,0:T(8,128)(2,1)S(1)}, u32[]{:S(2)}, u32[]{:S(2)}) %collective-permute-start.8) | collective-permute-done | bytes 153632 | tf_op jit(solution)/shard_map/ppermute | solution.py:117
  36.4 0.1 pack.3.refs_2_.mine_ref
  36.5 0.1 collective-permute-start.11
  36.5 0.6 collective-permute-start.5
  37.1 1.5 %collective-permute-start.12 = (bf16[192,1024]{1,0:T(8,128)(2,1)S(1)}, bf16[192,1024]{1,0:T(8,128)(2,1)S(1)}, u32[]{:S(2)}, u32[]{:S(2)}) collective-permute-start(bf16[192,1024]{1,0:T(8,128)(2,1)S(1)} %get-tuple-element.54), channel_id=1, source_target_pairs={{0,2},{2,0},{4,6},{6,4},{8,10},{10,8},{12,14},{14,12},{1,5},{3,7},... | collective-permute-start | bytes 1179656 | tf_op jit(solution)/shard_map/ppermute | solution.py:288
  38.6 5.8 %collective-permute-done.5.refs_1_ = bf16[192,1024]{1,0:T(8,128)(2,1)S(1)} collective-permute-done((bf16[192,1024]{1,0:T(8,128)(2,1)S(1)}, bf16[192,1024]{1,0:T(8,128)(2,1)S(1)}, u32[]{:S(2)}, u32[]{:S(2)}) %collective-permute-start.5) | collective-permute-done | bytes 393248 | tf_op jit(solution)/shard_map/ppermute | solution.py:288
  44.4 0.1 accumulate.8
  44.5 0.0 collective-permute-done.11.other_ref
  44.5 2.2 %gather_and_project.3 = (bf16[384,1664]{1,0:T(8,128)(2,1)S(1)}, bf16[192,1024]{1,0:T(8,128)(2,1)S(1)}, bf16[192,1024]{1,0:T(8,128)(2,1)S(1)}) custom-call(s32[24]{0:T(128)S(1)} %get-tuple-element.73.order_ref, bf16[192,1664]{1,0:T(8,128)(2,1)S(1)} %pack.3.refs_2_.mine_ref, bf16[192,1664]{1,0:T(8,128)(2,1)S(1)} %collective-permute-done.11.other_ref, ...), custom_call_target="tpu_custom_call" | custom-call | flops 1258291200 | bytes 5292032 | tf_op jit(solution)/shard_map/gather_and_project/pallas_call | solution.py:225
  46.7 0.6 collective-permute-start.15
  47.3 1.3 %collective-permute-done.12.refs_1_ = bf16[192,1024]{1,0:T(8,128)(2,1)S(1)} collective-permute-done((bf16[192,1024]{1,0:T(8,128)(2,1)S(1)}, bf16[192,1024]{1,0:T(8,128)(2,1)S(1)}, u32[]{:S(2)}, u32[]{:S(2)}) %collective-permute-start.12) | collective-permute-done | bytes 393248 | tf_op jit(solution)/shard_map/ppermute | solution.py:288
  48.6 0.1 accumulate.9
  48.7 1.6 %project.3 = (bf16[192,1024]{1,0:T(8,128)(2,1)S(1)}, bf16[192,1024]{1,0:T(8,128)(2,1)S(1)}) custom-call(bf16[384,1664]{1,0:T(8,128)(2,1)S(1)} %get-tuple-element.53.a_ref, bf16[1600,2048]{1,0:T(8,128)(2,1)S(1)} %load.1.w_ref, f32[96,1024]{1,0:T(8,128)S(1)} %get-tuple-element.56.refs_0_), custom_call_target="tpu_custom_call" | custom-call | flops 1258291200 | bytes 5292032 | tf_op jit(solution)/shard_map/project/pallas_call | solution.py:209
  50.3 0.0 copy-start.1
  50.3 0.6 collective-permute-start.18
  50.9 2.2 %collective-permute-start.10 = (bf16[96,1024]{1,0:T(8,128)(2,1)S(1)}, bf16[96,1024]{1,0:T(8,128)(2,1)S(1)}, u32[]{:S(2)}, u32[]{:S(2)}) collective-permute-start(bf16[96,1024]{1,0:T(8,128)(2,1)S(1)} %get-tuple-element.52), channel_id=1, source_target_pairs={{0,4},{2,6},{4,0},{6,2},{8,12},{10,14},{12,8},{14,10},{1,3},{3,1},... | collective-permute-start | bytes 589832 | tf_op jit(solution)/shard_map/ppermute | solution.py:288
  53.1 0.0 collective-permute-start.14
  53.1 5.8 %collective-permute-done.10.refs_1_ = bf16[96,1024]{1,0:T(8,128)(2,1)S(1)} collective-permute-done((bf16[96,1024]{1,0:T(8,128)(2,1)S(1)}, bf16[96,1024]{1,0:T(8,128)(2,1)S(1)}, u32[]{:S(2)}, u32[]{:S(2)}) %collective-permute-start.10) | collective-permute-done | bytes 196640 | tf_op jit(solution)/shard_map/ppermute | solution.py:288
  59.0 0.0 copy-start
  59.0 0.0 collective-permute-done.15.refs_1_
  59.0 0.1 accumulate.11
  59.1 2.1 %collective-permute-start.17 = (bf16[96,1024]{1,0:T(8,128)(2,1)S(1)}, bf16[96,1024]{1,0:T(8,128)(2,1)S(1)}, u32[]{:S(2)}, u32[]{:S(2)}) collective-permute-start(bf16[96,1024]{1,0:T(8,128)(2,1)S(1)} %get-tuple-element.65), channel_id=1, source_target_pairs={{0,4},{2,6},{4,0},{6,2},{8,12},{10,14},{12,8},{14,10},{1,3},{3,1},... | collective-permute-start | bytes 589832 | tf_op jit(solution)/shard_map/ppermute | solution.py:288
  61.2 0.5 collective-permute-done.14.refs_1_
  61.7 1.6 %collective-permute-done.18.refs_1_ = bf16[192,1024]{1,0:T(8,128)(2,1)S(1)} collective-permute-done((bf16[192,1024]{1,0:T(8,128)(2,1)S(1)}, bf16[192,1024]{1,0:T(8,128)(2,1)S(1)}, u32[]{:S(2)}, u32[]{:S(2)}) %collective-permute-start.18) | collective-permute-done | bytes 393248 | tf_op jit(solution)/shard_map/ppermute | solution.py:288
  63.3 0.1 accumulate.13
  63.4 4.1 %collective-permute-start.20 = (bf16[96,1024]{1,0:T(8,128)(2,1)S(1)}, bf16[96,1024]{1,0:T(8,128)(2,1)S(1)}, u32[]{:S(2)}, u32[]{:S(2)}) collective-permute-start(bf16[96,1024]{1,0:T(8,128)(2,1)S(1)} %get-tuple-element.70), channel_id=1, source_target_pairs={{0,4},{2,6},{4,0},{6,2},{8,12},{10,14},{12,8},{14,10},{1,3},{3,1},... | collective-permute-start | bytes 589832 | tf_op jit(solution)/shard_map/ppermute | solution.py:288
  67.5 0.1 slice.7
  67.6 0.2 select_reduce_fusion.2
  67.8 0.1 collective-permute-start.13
  67.9 2.9 %collective-permute-start.16 = (bf16[48,1024]{1,0:T(8,128)(2,1)S(1)}, bf16[48,1024]{1,0:T(8,128)(2,1)S(1)}, u32[]{:S(2)}, u32[]{:S(2)}) collective-permute-start(bf16[48,1024]{1,0:T(8,128)(2,1)S(1)} %get-tuple-element.64), channel_id=1, source_target_pairs={{0,8},{2,10},{4,12},{6,14},{8,0},{10,2},{12,4},{14,6},{1,9},{3,11}... | collective-permute-start | bytes 294920 | tf_op jit(solution)/shard_map/ppermute | solution.py:288
  70.8 3.3 %collective-permute-done.20.refs_1_ = bf16[96,1024]{1,0:T(8,128)(2,1)S(1)} collective-permute-done((bf16[96,1024]{1,0:T(8,128)(2,1)S(1)}, bf16[96,1024]{1,0:T(8,128)(2,1)S(1)}, u32[]{:S(2)}, u32[]{:S(2)}) %collective-permute-start.20) | collective-permute-done | bytes 196640 | tf_op jit(solution)/shard_map/ppermute | solution.py:288
  74.1 0.1 collective-permute-start.21
  74.2 2.9 %collective-permute-start.19 = (bf16[48,1024]{1,0:T(8,128)(2,1)S(1)}, bf16[48,1024]{1,0:T(8,128)(2,1)S(1)}, u32[]{:S(2)}, u32[]{:S(2)}) collective-permute-start(bf16[48,1024]{1,0:T(8,128)(2,1)S(1)} %get-tuple-element.69), channel_id=1, source_target_pairs={{0,8},{2,10},{4,12},{6,14},{8,0},{10,2},{12,4},{14,6},{1,9},{3,11}... | collective-permute-start | bytes 294920 | tf_op jit(solution)/shard_map/ppermute | solution.py:288
  77.1 0.1 compare_convert_fusion.live_ref
  77.2 2.3 %collective-permute-done.13.refs_1_ = bf16[48,1024]{1,0:T(8,128)(2,1)S(1)} collective-permute-done((bf16[48,1024]{1,0:T(8,128)(2,1)S(1)}, bf16[48,1024]{1,0:T(8,128)(2,1)S(1)}, u32[]{:S(2)}, u32[]{:S(2)}) %collective-permute-start.13) | collective-permute-done | bytes 98336 | tf_op jit(solution)/shard_map/ppermute | solution.py:288
  79.5 2.3 %collective-permute-done.16.refs_3_ = bf16[48,1024]{1,0:T(8,128)(2,1)S(1)} collective-permute-done((bf16[48,1024]{1,0:T(8,128)(2,1)S(1)}, bf16[48,1024]{1,0:T(8,128)(2,1)S(1)}, u32[]{:S(2)}, u32[]{:S(2)}) %collective-permute-start.16) | collective-permute-done | bytes 98336 | tf_op jit(solution)/shard_map/ppermute | solution.py:288
  81.8 1.1 %collective-permute-done.21.refs_7_ = bf16[48,1024]{1,0:T(8,128)(2,1)S(1)} collective-permute-done((bf16[48,1024]{1,0:T(8,128)(2,1)S(1)}, bf16[48,1024]{1,0:T(8,128)(2,1)S(1)}, u32[]{:S(2)}, u32[]{:S(2)}) %collective-permute-start.21) | collective-permute-done | bytes 98336 | tf_op jit(solution)/shard_map/ppermute | solution.py:288
  82.9 1.1 %collective-permute-done.19.refs_5_ = bf16[48,1024]{1,0:T(8,128)(2,1)S(1)} collective-permute-done((bf16[48,1024]{1,0:T(8,128)(2,1)S(1)}, bf16[48,1024]{1,0:T(8,128)(2,1)S(1)}, u32[]{:S(2)}, u32[]{:S(2)}) %collective-permute-start.19) | collective-permute-done | bytes 98336 | tf_op jit(solution)/shard_map/ppermute | solution.py:288
  83.9 1.5 %finish.1 = bf16[3,2,16,2048]{3,2,1,0:T(8,128)(2,1)} custom-call(s32[3]{0:T(128)S(1)} %compare_convert_fusion.live_ref, f32[1,2048]{1,0:T(1,128)S(1)} %bitcast.5, f32[48,1024]{1,0:T(8,128)S(1)} %get-tuple-element.58.refs_2_.refs_0_, bf16[48,1024]{1,0:T(8,128)(2,1)S(1)} %collective-permute-done.13.refs_1_, f32[48,1024]{1,0:T(8,128)S(1)} %get-tuple-element.63.refs_2_, ...), custom_call_target="tpu_custom_call" | custom-call | tf_op jit(solution)/shard_map/finish/pallas_call | solution.py:275
  (20 shorter events, 0.2 us)
Async XLA Ops:
  0.0 15.8 %copy-start.2 = (s32[8]{0:T(128)S(1)}, s32[8]{0:T(128)}, u32[]{:S(2)}) copy-start(s32[8]{0:T(128)} %constant.39.clone) | copy-start | bytes 100
  0.0 15.8 %copy-start.3 = (s32[8]{0:T(128)S(1)}, s32[8]{0:T(128)}, u32[]{:S(2)}) copy-start(s32[8]{0:T(128)} %constant.38.clone) | copy-start | bytes 100
  3.1 24.0 %copy-start.4 = (s32[24]{0:T(128)S(1)}, s32[24]{0:T(128)}, u32[]{:S(2)}) copy-start(s32[24]{0:T(128)} %param.16) | copy-start | bytes 292
  3.1 24.2 %copy-start.5 = (s32[8]{0:T(128)S(1)}, s32[8]{0:T(128)}, u32[]{:S(2)}) copy-start(s32[8]{0:T(128)} %constant.40.clone) | copy-start | bytes 100
  3.1 15.9 %collective-permute-start.1 = (bf16[48,1600]{1,0:T(8,128)(2,1)S(1)}, bf16[48,1600]{1,0:T(8,128)(2,1)S(1)}, u32[]{:S(2)}, u32[]{:S(2)}) collective-permute-start(bf16[48,1600]{1,0:T(8,128)(2,1)S(1)} %get-tuple-element.40), channel_id=1, source_target_pairs={{0,8},{2,10},{4,12},{6,14},{8,0},{10,2},{12,4},{14,6},{1,13},{3,15... | collective-permute-start | bytes 460808 | tf_op jit(solution)/shard_map/ppermute | solution.py:117
  7.2 17.8 %collective-permute-start.2 = (bf16[48,1600]{1,0:T(8,128)(2,1)S(1)}, bf16[48,1600]{1,0:T(8,128)(2,1)S(1)}, u32[]{:S(2)}, u32[]{:S(2)}) collective-permute-start(bf16[48,1600]{1,0:T(8,128)(2,1)S(1)} %get-tuple-element.41), channel_id=1, source_target_pairs={{0,10},{2,8},{4,14},{6,12},{8,2},{10,0},{12,6},{14,4},{1,15},{3,13... | collective-permute-start | bytes 460808 | tf_op jit(solution)/shard_map/ppermute | solution.py:117
  8.5 16.5 %collective-permute-start = (bf16[48,1600]{1,0:T(8,128)(2,1)S(1)}, bf16[48,1600]{1,0:T(8,128)(2,1)S(1)}, u32[]{:S(2)}, u32[]{:S(2)}) collective-permute-start(bf16[48,1600]{1,0:T(8,128)(2,1)S(1)} %get-tuple-element.39.refs_0_), channel_id=1, source_target_pairs={{0,4},{2,6},{4,0},{6,2},{8,12},{10,14},{12,8},{14,10},{1,7},{3,5},... | collective-permute-start | bytes 460808 | tf_op jit(solution)/shard_map/ppermute | solution.py:117
  10.1 16.9 %collective-permute-start.3 = (bf16[48,1600]{1,0:T(8,128)(2,1)S(1)}, bf16[48,1600]{1,0:T(8,128)(2,1)S(1)}, u32[]{:S(2)}, u32[]{:S(2)}) collective-permute-start(bf16[48,1600]{1,0:T(8,128)(2,1)S(1)} %get-tuple-element.42.refs_4_), channel_id=1, source_target_pairs={{0,2},{2,0},{4,6},{6,4},{8,10},{10,8},{12,14},{14,12},{16,18},{18,... | collective-permute-start | bytes 460808 | tf_op jit(solution)/shard_map/ppermute | solution.py:117
  15.5 18.6 %collective-permute-start.6 = (bf16[48,1600]{1,0:T(8,128)(2,1)S(1)}, bf16[48,1600]{1,0:T(8,128)(2,1)S(1)}, u32[]{:S(2)}, u32[]{:S(2)}) collective-permute-start(bf16[48,1600]{1,0:T(8,128)(2,1)S(1)} %get-tuple-element.45), channel_id=1, source_target_pairs={{0,4},{2,6},{4,0},{6,2},{8,12},{10,14},{12,8},{14,10},{1,7},{3,5},... | collective-permute-start | bytes 460808 | tf_op jit(solution)/shard_map/ppermute | solution.py:117
  19.0 15.2 %collective-permute-start.7 = (bf16[48,1600]{1,0:T(8,128)(2,1)S(1)}, bf16[48,1600]{1,0:T(8,128)(2,1)S(1)}, u32[]{:S(2)}, u32[]{:S(2)}) collective-permute-start(bf16[48,1600]{1,0:T(8,128)(2,1)S(1)} %get-tuple-element.46), channel_id=1, source_target_pairs={{0,8},{2,10},{4,12},{6,14},{8,0},{10,2},{12,4},{14,6},{1,13},{3,15... | collective-permute-start | bytes 460808 | tf_op jit(solution)/shard_map/ppermute | solution.py:117
  25.0 11.4 %collective-permute-start.8 = (bf16[48,1600]{1,0:T(8,128)(2,1)S(1)}, bf16[48,1600]{1,0:T(8,128)(2,1)S(1)}, u32[]{:S(2)}, u32[]{:S(2)}) collective-permute-start(bf16[48,1600]{1,0:T(8,128)(2,1)S(1)} %get-tuple-element.47), channel_id=1, source_target_pairs={{0,10},{2,8},{4,14},{6,12},{8,2},{10,0},{12,6},{14,4},{1,15},{3,13... | collective-permute-start | bytes 460808 | tf_op jit(solution)/shard_map/ppermute | solution.py:117
  25.0 11.4 %collective-permute-start.9 = (bf16[48,1600]{1,0:T(8,128)(2,1)S(1)}, bf16[48,1600]{1,0:T(8,128)(2,1)S(1)}, u32[]{:S(2)}, u32[]{:S(2)}) collective-permute-start(bf16[48,1600]{1,0:T(8,128)(2,1)S(1)} %get-tuple-element.48.refs_4_), channel_id=1, source_target_pairs={{0,2},{2,0},{4,6},{6,4},{8,10},{10,8},{12,14},{14,12},{16,18},{18,... | collective-permute-start | bytes 460808 | tf_op jit(solution)/shard_map/ppermute | solution.py:117
  27.0 3.3 %collective-permute-start.4 = (bf16[192,1664]{1,0:T(8,128)(2,1)S(1)}, bf16[192,1664]{1,0:T(8,128)(2,1)S(1)}, u32[]{:S(2)}, u32[]{:S(2)}) collective-permute-start(bf16[192,1664]{1,0:T(8,128)(2,1)S(1)} %pack.2.refs_0_.mine_ref), channel_id=1, source_target_pairs={{0,1},{1,0},{2,3},{3,2},{4,5},{5,4},{6,7},{7,6},{8,9},{9,8},{10,11... | collective-permute-start | bytes 1916936 | tf_op jit(solution)/shard_map/ppermute | solution.py:357
  36.5 8.0 %collective-permute-start.11 = (bf16[192,1664]{1,0:T(8,128)(2,1)S(1)}, bf16[192,1664]{1,0:T(8,128)(2,1)S(1)}, u32[]{:S(2)}, u32[]{:S(2)}) collective-permute-start(bf16[192,1664]{1,0:T(8,128)(2,1)S(1)} %pack.3.refs_2_.mine_ref), channel_id=1, source_target_pairs={{0,1},{1,0},{2,3},{3,2},{4,5},{5,4},{6,7},{7,6},{8,9},{9,8},{10,11... | collective-permute-start | bytes 1916936 | tf_op jit(solution)/shard_map/ppermute | solution.py:357
  36.5 7.8 %collective-permute-start.5 = (bf16[192,1024]{1,0:T(8,128)(2,1)S(1)}, bf16[192,1024]{1,0:T(8,128)(2,1)S(1)}, u32[]{:S(2)}, u32[]{:S(2)}) collective-permute-start(bf16[192,1024]{1,0:T(8,128)(2,1)S(1)} %get-tuple-element.44), channel_id=1, source_target_pairs={{0,2},{2,0},{4,6},{6,4},{8,10},{10,8},{12,14},{14,12},{1,5},{3,7},... | collective-permute-start | bytes 1179656 | tf_op jit(solution)/shard_map/ppermute | solution.py:288
  37.1 11.5 %collective-permute-start.12 = (bf16[192,1024]{1,0:T(8,128)(2,1)S(1)}, bf16[192,1024]{1,0:T(8,128)(2,1)S(1)}, u32[]{:S(2)}, u32[]{:S(2)}) collective-permute-start(bf16[192,1024]{1,0:T(8,128)(2,1)S(1)} %get-tuple-element.54), channel_id=1, source_target_pairs={{0,2},{2,0},{4,6},{6,4},{8,10},{10,8},{12,14},{14,12},{1,5},{3,7},... | collective-permute-start | bytes 1179656 | tf_op jit(solution)/shard_map/ppermute | solution.py:288
  46.7 12.3 %collective-permute-start.15 = (bf16[192,1024]{1,0:T(8,128)(2,1)S(1)}, bf16[192,1024]{1,0:T(8,128)(2,1)S(1)}, u32[]{:S(2)}, u32[]{:S(2)}) collective-permute-start(bf16[192,1024]{1,0:T(8,128)(2,1)S(1)} %get-tuple-element.61), channel_id=1, source_target_pairs={{0,2},{2,0},{4,6},{6,4},{8,10},{10,8},{12,14},{14,12},{1,5},{3,7},... | collective-permute-start | bytes 1179656 | tf_op jit(solution)/shard_map/ppermute | solution.py:288
  50.3 17.3 %copy-start.1 = (s32[8]{0:T(128)S(1)}, s32[8]{0:T(128)}, u32[]{:S(2)}) copy-start(s32[8]{0:T(128)} %count_hbm.3) | copy-start | bytes 100
  50.3 13.0 %collective-permute-start.18 = (bf16[192,1024]{1,0:T(8,128)(2,1)S(1)}, bf16[192,1024]{1,0:T(8,128)(2,1)S(1)}, u32[]{:S(2)}, u32[]{:S(2)}) collective-permute-start(bf16[192,1024]{1,0:T(8,128)(2,1)S(1)} %get-tuple-element.66), channel_id=1, source_target_pairs={{0,2},{2,0},{4,6},{6,4},{8,10},{10,8},{12,14},{14,12},{1,5},{3,7},... | collective-permute-start | bytes 1179656 | tf_op jit(solution)/shard_map/ppermute | solution.py:288
  50.9 8.0 %collective-permute-start.10 = (bf16[96,1024]{1,0:T(8,128)(2,1)S(1)}, bf16[96,1024]{1,0:T(8,128)(2,1)S(1)}, u32[]{:S(2)}, u32[]{:S(2)}) collective-permute-start(bf16[96,1024]{1,0:T(8,128)(2,1)S(1)} %get-tuple-element.52), channel_id=1, source_target_pairs={{0,4},{2,6},{4,0},{6,2},{8,12},{10,14},{12,8},{14,10},{1,3},{3,1},... | collective-permute-start | bytes 589832 | tf_op jit(solution)/shard_map/ppermute | solution.py:288
  53.1 8.6 %collective-permute-start.14 = (bf16[96,1024]{1,0:T(8,128)(2,1)S(1)}, bf16[96,1024]{1,0:T(8,128)(2,1)S(1)}, u32[]{:S(2)}, u32[]{:S(2)}) collective-permute-start(bf16[96,1024]{1,0:T(8,128)(2,1)S(1)} %get-tuple-element.60), channel_id=1, source_target_pairs={{0,4},{2,6},{4,0},{6,2},{8,12},{10,14},{12,8},{14,10},{1,3},{3,1},... | collective-permute-start | bytes 589832 | tf_op jit(solution)/shard_map/ppermute | solution.py:288
  59.0 25.0 %copy-start = (f32[2048]{0:T(1024)S(1)}, f32[2048]{0:T(1024)}, u32[]{:S(2)}) copy-start(f32[2048]{0:T(1024)} %param.14) | copy-start | bytes 24580
  59.1 11.7 %collective-permute-start.17 = (bf16[96,1024]{1,0:T(8,128)(2,1)S(1)}, bf16[96,1024]{1,0:T(8,128)(2,1)S(1)}, u32[]{:S(2)}, u32[]{:S(2)}) collective-permute-start(bf16[96,1024]{1,0:T(8,128)(2,1)S(1)} %get-tuple-element.65), channel_id=1, source_target_pairs={{0,4},{2,6},{4,0},{6,2},{8,12},{10,14},{12,8},{14,10},{1,3},{3,1},... | collective-permute-start | bytes 589832 | tf_op jit(solution)/shard_map/ppermute | solution.py:288
  63.4 10.7 %collective-permute-start.20 = (bf16[96,1024]{1,0:T(8,128)(2,1)S(1)}, bf16[96,1024]{1,0:T(8,128)(2,1)S(1)}, u32[]{:S(2)}, u32[]{:S(2)}) collective-permute-start(bf16[96,1024]{1,0:T(8,128)(2,1)S(1)} %get-tuple-element.70), channel_id=1, source_target_pairs={{0,4},{2,6},{4,0},{6,2},{8,12},{10,14},{12,8},{14,10},{1,3},{3,1},... | collective-permute-start | bytes 589832 | tf_op jit(solution)/shard_map/ppermute | solution.py:288
  67.8 11.7 %collective-permute-start.13 = (bf16[48,1024]{1,0:T(8,128)(2,1)S(1)}, bf16[48,1024]{1,0:T(8,128)(2,1)S(1)}, u32[]{:S(2)}, u32[]{:S(2)}) collective-permute-start(bf16[48,1024]{1,0:T(8,128)(2,1)S(1)} %get-tuple-element.59), channel_id=1, source_target_pairs={{0,8},{2,10},{4,12},{6,14},{8,0},{10,2},{12,4},{14,6},{1,9},{3,11}... | collective-permute-start | bytes 294920 | tf_op jit(solution)/shard_map/ppermute | solution.py:288
  67.9 13.9 %collective-permute-start.16 = (bf16[48,1024]{1,0:T(8,128)(2,1)S(1)}, bf16[48,1024]{1,0:T(8,128)(2,1)S(1)}, u32[]{:S(2)}, u32[]{:S(2)}) collective-permute-start(bf16[48,1024]{1,0:T(8,128)(2,1)S(1)} %get-tuple-element.64), channel_id=1, source_target_pairs={{0,8},{2,10},{4,12},{6,14},{8,0},{10,2},{12,4},{14,6},{1,9},{3,11}... | collective-permute-start | bytes 294920 | tf_op jit(solution)/shard_map/ppermute | solution.py:288
  74.1 8.7 %collective-permute-start.21 = (bf16[48,1024]{1,0:T(8,128)(2,1)S(1)}, bf16[48,1024]{1,0:T(8,128)(2,1)S(1)}, u32[]{:S(2)}, u32[]{:S(2)}) collective-permute-start(bf16[48,1024]{1,0:T(8,128)(2,1)S(1)} %get-tuple-element.72), channel_id=1, source_target_pairs={{0,8},{2,10},{4,12},{6,14},{8,0},{10,2},{12,4},{14,6},{1,9},{3,11}... | collective-permute-start | bytes 294920 | tf_op jit(solution)/shard_map/ppermute | solution.py:288
  74.2 9.7 %collective-permute-start.19 = (bf16[48,1024]{1,0:T(8,128)(2,1)S(1)}, bf16[48,1024]{1,0:T(8,128)(2,1)S(1)}, u32[]{:S(2)}, u32[]{:S(2)}) collective-permute-start(bf16[48,1024]{1,0:T(8,128)(2,1)S(1)} %get-tuple-element.69), channel_id=1, source_target_pairs={{0,8},{2,10},{4,12},{6,14},{8,0},{10,2},{12,4},{14,6},{1,9},{3,11}... | collective-permute-start | bytes 294920 | tf_op jit(solution)/shard_map/ppermute | solution.py:288

commit v3 on v2

--- a/solution.py
+++ b/solution.py
@@ -16,7 +16,7 @@
 BIG_VMEM = 20 * 1024 * 1024
 PROJECT_VMEM = 20 * 1024 * 1024
 LANES = 128
-STEPS = [(0, 0), (1, 0), (2, -1), (0, 1), (2, 0), (1, 1), (3, 0), (0, 2), (2, 1), (1, 2), (3, 1), (2, 2), (3, 2)]
+STEPS = [(0, 0), (1, -1), (1, 0), (0, 1), (2, 0), (1, 1), (2, 1), (0, 2), (1, 2), (0, 3), (2, 2)]
 
 
 def arrangement(bits):
@@ -39,6 +39,8 @@
 
 def prepare_kernel(peers, tiles, phase, x_hbm, gain_hbm, shift_hbm, count_hbm, *refs):
     outs, (pieces, x_ref, gain_ref, shift_ref, count_ref, sems) = refs[-6 - peers // 2:-6], refs[-6:]
+    if phase == 1:
+        outs[-1][:tiles * PART, :] = refs[0][...]
     me, core = lax.axis_index("dp"), lax.axis_index("tensor")
     width = x_hbm.shape[-1]
     total = 4 * width
@@ -80,20 +82,22 @@
         for part in range(per_patch):
             pieces[q * per_patch + part] = normed[:, part * block_width:(part + 1) * block_width]
     for out, first, second in zip(outs, *routes(peers)):
-        out[...] = pieces[jnp.bitwise_xor(me, jnp.where(core == 0, first, second))]
-
-
-def prepare(tile_count, patch_feats, ln_gain, ln_shift, peers, tiles, phase, after):
+        value = pieces[jnp.bitwise_xor(me, jnp.where(core == 0, first, second))]
+        out[out.shape[0] - tiles * PART:, :] = value
+
+
+def prepare(tile_count, patch_feats, ln_gain, ln_shift, peers, tiles, phase, last, after):
     width = patch_feats.shape[1]
     block_width = 4 * width // peers
     rows = tiles * PART
     x = patch_feats.reshape(tiles, PHASES, 4 * PART, width)
     vectors = (4 * width // LANES, LANES)
+    inside = pl.BlockSpec(memory_space=pltpu.VMEM)
     operands = [x, ln_gain.reshape(vectors), ln_shift.reshape(vectors), tile_count]
     return pl.pallas_call(
         functools.partial(prepare_kernel, peers, tiles, phase),
-        in_specs=[pl.BlockSpec(memory_space=pl.ANY)] * (4 + len(after)),
-        out_specs=[pl.BlockSpec(memory_space=pltpu.VMEM)] * (peers // 2),
+        in_specs=[pl.BlockSpec(memory_space=pl.ANY)] * 4 + [inside] * len(last) + [pl.BlockSpec(memory_space=pl.ANY)] * len(after),
+        out_specs=[inside] * (peers // 2),
         scratch_shapes=[
             pltpu.VMEM((peers, rows, block_width), jnp.bfloat16),
             pltpu.VMEM((tiles, 4 * PART, width), jnp.bfloat16),
@@ -102,47 +106,44 @@
             pltpu.SMEM(tile_count.shape, jnp.int32),
             pltpu.SemaphoreType.DMA((4,)),
         ],
-        out_shape=[pltpu.VMEM((rows, block_width), jnp.bfloat16)] * (peers // 2),
+        out_shape=[pltpu.VMEM((rows, block_width), jnp.bfloat16)] * (peers // 2 - 1)
+        + [pltpu.VMEM(((1 + len(last)) * rows, block_width), jnp.bfloat16)],
         compiler_params=pltpu.CompilerParams(vmem_limit_bytes=BIG_VMEM),
         cost_estimate=pl.CostEstimate(flops=0, bytes_accessed=32 * rows * width, transcendentals=0),
         name="prepare",
-    )(*[in_hbm(operand) for operand in operands], *after)
-
-
-def scatter_pieces(pieces, peers):
-    received = []
-    for piece, first, second in zip(pieces, *routes(peers)):
-        pairs = [(2 * d, 2 * (d ^ first)) for d in range(peers)]
-        pairs += [(2 * d + 1, 2 * (d ^ second) + 1) for d in range(peers) if second != 0]
-        received.append(lax.ppermute(piece, ("dp", "tensor"), pairs))
-    return received
-
-
-def pack_kernel(count, own_index, *refs):
-    pieces, own, out = refs[:count], refs[count], refs[-1]
-    rows, width = own.shape
+    )(*[in_hbm(operand) for operand in operands], *last, *after)
+
+
+def send_piece(piece, index, peers):
+    first, second = (route[index] for route in routes(peers))
+    pairs = [(2 * d, 2 * (d ^ first)) for d in range(peers)]
+    pairs += [(2 * d + 1, 2 * (d ^ second) + 1) for d in range(peers) if second != 0]
+    return lax.ppermute(piece, ("dp", "tensor"), pairs)
+
+
+def pack_kernel(count, phase, *refs):
+    pieces, last, own, out = refs[:count], refs[count], refs[count + 1], refs[-1]
+    rows, width = pieces[0].shape
     if out.shape[1] > width:
         out[:, width:] = jnp.zeros((out.shape[0], out.shape[1] - width), out.dtype)
     for i, piece in enumerate(pieces):
-        value = piece[...]
-        if i == own_index:
-            value = jnp.where(lax.axis_index("tensor") == 0, value, own[...])
-        out[i * rows:(i + 1) * rows, :width] = value
-
-
-def pack(received, own, after):
-    own_index = routes(2 * len(received))[1].index(0)
-    rows, width = own.shape
+        out[i * rows:(i + 1) * rows, :width] = piece[...]
+    at = slice(phase * rows, (phase + 1) * rows)
+    out[count * rows:, :width] = jnp.where(lax.axis_index("tensor") == 0, last[at, :], own[at, :])
+
+
+def pack(received, last, own, phase, after):
+    rows, width = received[0].shape
     padded = -(-width // LANES) * LANES
     inside = pl.BlockSpec(memory_space=pltpu.VMEM)
     return pl.pallas_call(
-        functools.partial(pack_kernel, len(received), own_index),
-        in_specs=[inside] * (len(received) + 1) + [pl.BlockSpec(memory_space=pl.ANY)] * len(after),
+        functools.partial(pack_kernel, len(received), phase),
+        in_specs=[inside] * (len(received) + 2) + [pl.BlockSpec(memory_space=pl.ANY)] * len(after),
         out_specs=inside,
-        out_shape=pltpu.VMEM((len(received) * rows, padded), jnp.bfloat16),
+        out_shape=pltpu.VMEM(((len(received) + 1) * rows, padded), jnp.bfloat16),
         compiler_params=pltpu.CompilerParams(vmem_limit_bytes=VMEM_LIMIT),
         name="pack",
-    )(*received, own, *after)
+    )(*received, last, own, *after)
 
 
 def load_kernel(w_hbm, *refs):
@@ -179,8 +180,11 @@
     multiply(first, block, a_ref, w_ref, *refs[-2:])
 
 
-def gather_kernel(first, block, order_ref, mine_ref, other_ref, w_ref, *refs):
-    sorted_ref, send_ref, keep_ref, held = refs[-4:]
+def gather_kernel(first, block, count, order_ref, mine_ref, other_ref, w_ref, *refs):
+    sorted_ref, send_ref, keep_ref = refs[-4 - count:-1 - count]
+    held = refs[-1]
+    for piece, out in zip(refs[:count], refs[-1 - count:-1]):
+        out[...] = piece[...]
     core = lax.axis_index("tensor")
     held[core] = mine_ref[...]
     held[1 - core] = other_ref[...]
@@ -217,21 +221,22 @@
     )(a, weight, *after)
 
 
-def gather_and_project(order, mine, other, weight, first, columns, after, block=256):
+def gather_and_project(order, mine, other, weight, first, columns, pieces, after, block=256):
     rows, padded = mine.shape
     depth = weight.shape[0]
     half = pltpu.VMEM((rows, columns), jnp.bfloat16)
     inside, outside = pl.BlockSpec(memory_space=pltpu.VMEM), pl.BlockSpec(memory_space=pl.ANY)
     return pl.pallas_call(
-        functools.partial(gather_kernel, first, block),
-        in_specs=[pl.BlockSpec(memory_space=pltpu.SMEM)] + [inside] * 3 + [outside] * len(after),
-        out_specs=[inside] * 3,
-        out_shape=[pltpu.VMEM((2 * rows, padded), jnp.bfloat16), half, half],
+        functools.partial(gather_kernel, first, block, len(pieces)),
+        in_specs=[pl.BlockSpec(memory_space=pltpu.SMEM)] + [inside] * (3 + len(pieces)) + [outside] * len(after),
+        out_specs=[inside] * (3 + len(pieces)),
+        out_shape=[pltpu.VMEM((2 * rows, padded), jnp.bfloat16), half, half]
+        + [pltpu.VMEM(piece.shape, piece.dtype) for piece in pieces],
         scratch_shapes=[pltpu.VMEM((2, rows, padded), jnp.bfloat16)],
         compiler_params=pltpu.CompilerParams(vmem_limit_bytes=PROJECT_VMEM),
         cost_estimate=cost(2 * rows, depth, columns),
         name="gather_and_project",
-    )(order, mine, other, weight, *after)
+    )(order, mine, other, weight, *pieces, *after)
 
 
 def activate(bias_ref, first, keep_ref, recv_ref):
@@ -324,26 +329,29 @@
     columns = merge_weight.shape[1]
 
     source_ids = jnp.arange(peers, dtype=jnp.int32)
-    sequences = [bits, [bits[1], bits[0]] + bits[2:]]
-    first_core = (lax.axis_index("tensor") == 0).astype(jnp.int32)
-    owners = [jnp.array(arrangement(sequence), jnp.int32) for sequence in sequences]
-    owners = jnp.where(first_core == 1, *owners) ^ me
-    wanted = (owners[:, None] * tiles + jnp.arange(tiles, dtype=jnp.int32)[None, :]).reshape(slots)
+    y_first, z_first = bits, [bits[1], bits[0]] + bits[2:]
+    is_first = lax.axis_index("tensor") == 0
     tile_ids = jnp.arange(slots, dtype=jnp.int32)
-    anchor = jnp.sum(jnp.where(tile_dest[None, :] == wanted[:, None], tile_ids[None, :], 0), axis=1)
-    source, place = anchor // tiles, anchor % tiles
-    sequence = jnp.array(sum(routes(peers), []), jnp.int32)
-    is_there = sequence[None, :] == (source ^ me)[:, None]
-    order = jnp.sum(jnp.where(is_there, source_ids[None, :], 0), axis=1) * tiles + place
+    sent = jnp.array(sum(routes(peers), []), jnp.int32)
+    all_sequences, orders = [(y_first, z_first), (y_first, z_first)], []
+    for sequences in all_sequences:
+        owners = [jnp.array(arrangement(sequence), jnp.int32) for sequence in sequences]
+        owners = jnp.where(is_first, *owners) ^ me
+        wanted = (owners[:, None] * tiles + jnp.arange(tiles, dtype=jnp.int32)[None, :]).reshape(slots)
+        anchor = jnp.sum(jnp.where(tile_dest[None, :] == wanted[:, None], tile_ids[None, :], 0), axis=1)
+        source, place = anchor // tiles, anchor % tiles
+        is_there = sent[None, :] == (source ^ me)[:, None]
+        orders.append(jnp.sum(jnp.where(is_there, source_ids[None, :], 0), axis=1) * tiles + place)
     own_source, own_place = source[-tiles:], place[-tiles:]
     own_count = jnp.sum(jnp.where(own_source[:, None] == source_ids[None, :], tile_count[None, :], 0), axis=1)
     live = (own_place < own_count).astype(jnp.int32)
 
     half = columns // 2
-    chunks = [(0, 0, half), (0, half, half), (1, 0, half), (1, half, half)]
-    pieces = [prepare(tile_count, patch_feats, ln_gain, ln_shift, peers, tiles, 0, [])]
-    pieces.append(prepare(tile_count, patch_feats, ln_gain, ln_shift, peers, tiles, 1, pieces[0][:1]))
-    scattered = [scatter_pieces(parts, peers) for parts in pieces]
+    chunks = [(0, 0, columns), (1, 0, half), (1, half, half)]
+    pieces = [prepare(tile_count, patch_feats, ln_gain, ln_shift, peers, tiles, 0, [], [])]
+    pieces.append(prepare(tile_count, patch_feats, ln_gain, ln_shift, peers, tiles, 1, pieces[0][-1:], pieces[0][:1]))
+    received = [[send_piece(piece, i, peers) for i, piece in enumerate(parts[:-1])] for parts in pieces]
+    last = send_piece(pieces[1][-1], peers // 2 - 1, peers)
     packed = {}
 
     flows, done, after = {}, {}, []
@@ -353,7 +361,7 @@
     for index, step in steps:
         phase, first, count = chunks[index]
         if step < 0 or (step == 0 and first == 0 and phase not in packed):
-            mine = pack(scattered[phase], pieces[phase][routes(peers)[1].index(0)], after)
+            mine = pack(received[phase], last, pieces[1][-1], phase, after)
             packed[phase] = mine, lax.ppermute(mine, "tensor", [(0, 1), (1, 0)])
             after = [mine]
             if phase == 0:
@@ -367,11 +375,11 @@
         if step > 0:
             send, keep = accumulate([flows[index]], after)
         elif first == 0:
-            rows, send, keep = gather_and_project(order, *packed[phase], weight, first, count, after)
+            rows, send, keep = gather_and_project(orders[phase], *packed[phase], weight, first, count, [], after)
         else:
             send, keep = project(rows, weight, first, count, after)
         after = [keep]
-        flows[index] = (keep, exchange(send, [1 << sequence[step] for sequence in sequences], peers))
+        flows[index] = (keep, exchange(send, [1 << sequence[step] for sequence in all_sequences[phase]], peers))
     flows = [(done[i],) if i in done else flows[i] for i in range(len(chunks))]
     return finish(live, merge_bias, chunks, flows, tiles)
 

time: 85.7 us -> 80.6 us (0.940)
  starting transfers between devices: 29.3 us -> 20.7 us
  waiting for transfers between devices: 36.3 us -> 40 us
    ppermute x12 -> x9, starting transfers between devices: 17.6 us -> 10.9 us  [exchange(): return lax.ppermute(array, ('dp', 'tensor'), pairs)]
    ppermute x2, waiting for transfers between devices: 0.01 us -> 2.06 us  [body(): packed[phase] = (mine, lax.ppermute(mine, 'tensor', [(0, 1), (1, 0)]))]
    ppermute x8 -> x7, starting transfers between devices: 11.5 us -> 9.64 us  [send_piece(): return lax.ppermute(piece, ('dp', 'tensor'), pairs)]
    ppermute x8 -> x7, waiting for transfers between devices: 11.3 us -> 13.1 us  [send_piece(): return lax.ppermute(piece, ('dp', 'tensor'), pairs)]
    pallas_call x2 -> x1, Pallas kernels: 3.23 us -> 1.61 us  [project(): pl.pallas_call(functools.partial(project_kernel, first, block), in_specs=...]
    pallas_call x4 -> x5, Pallas kernels: 4.56 us -> 6.11 us  [the longest x2 5.88 us: gather_and_project(): pl.pallas_call(functools.partial(gather_kernel, first, block, len(pieces)...]
    ppermute x12 -> x9, waiting for transfers between devices: 25 us -> 24.8 us  [exchange(): return lax.ppermute(array, ('dp', 'tensor'), pairs)]
  transfers between devices with their start and end apart: 22 -> 18, of which waited for: 13 -> 11; matrix products, arithmetic and copies ran while one was open for 1% -> 1% of each run, Pallas kernels for 17% -> 18%
where the time goes in v3:
time: 80.6 us; the launch traced here: 80.3 us
  waiting for transfers between devices  40 us (50%)
  starting transfers between devices  20.7 us (26%)
  Pallas kernels  18.6 us (23%)
    ppermute x9, waiting for transfers between devices, exchange(): return lax.ppermute(array, ('dp', 'tensor'), pairs)  24.8 us
    ppermute x7, waiting for transfers between devices, send_piece(): return lax.ppermute(piece, ('dp', 'tensor'), pairs)  13.1 us
    ppermute x9, starting transfers between devices, exchange(): return lax.ppermute(array, ('dp', 'tensor'), pairs)  10.9 us
    ppermute x7, starting transfers between devices, send_piece(): return lax.ppermute(piece, ('dp', 'tensor'), pairs)  9.64 us
    pallas_call x2, Pallas kernels, prepare(): pl.pallas_call(functools.partial(prepare_kernel, peers, tiles, phase), in...  6.11 us
    pallas_call x2, Pallas kernels, gather_and_project(): pl.pallas_call(functools.partial(gather_kernel, first, block, len(pieces)...  5.88 us
    pallas_call x1, Pallas kernels, load(): pl.pallas_call(load_kernel, in_specs=[pl.BlockSpec(memory_space=pl.ANY)]...  2.87 us
    ppermute x2, waiting for transfers between devices, body(): packed[phase] = (mine, lax.ppermute(mine, 'tensor', [(0, 1), (1, 0)]))  2.06 us
  transfers between devices with their start and end apart: 18, of which 11 were waited for; matrix products, arithmetic and copies ran while one was open for 1% of the time, Pallas kernels for 18%

profile of v3, /device:TPU:0, one launch (start us, length us, event | category | flops | bytes accessed | tf_op | source)
XLA Modules:
  0.0 80.3 jit_solution(1793767778219465401)
XLA Ops:
  0.0 3.1 %prepare.2 = (bf16[48,1600]{1,0:T(8,128)(2,1)S(1)}, bf16[48,1600]{1,0:T(8,128)(2,1)S(1)}, bf16[48,1600]{1,0:T(8,128)(2,1)S(1)}, bf16[48,1600]{1,0:T(8,128)(2,1)S(1)}) custom-call(bf16[3,2,64,3200]{3,2,1,0:T(8,128)(2,1)} %bitcast.7, f32[100,128]{1,0:T(8,128)} %bitcast.9, f32[100,128]{1,0:T(8,128)} %bitcast.11, s32[8]{0:T(128)} %count_hbm.3), custom_call_target="tpu_custom_call" | custom-call | bytes 4915200 | tf_op jit(solution)/shard_map/prepare/pallas_call | solution.py:97
  3.1 0.0 copy-start.4
  3.1 0.0 copy-start.5
  3.1 4.1 %collective-permute-start.1 = (bf16[48,1600]{1,0:T(8,128)(2,1)S(1)}, bf16[48,1600]{1,0:T(8,128)(2,1)S(1)}, u32[]{:S(2)}, u32[]{:S(2)}) collective-permute-start(bf16[48,1600]{1,0:T(8,128)(2,1)S(1)} %get-tuple-element.33), channel_id=1, source_target_pairs={{0,8},{2,10},{4,12},{6,14},{8,0},{10,2},{12,4},{14,6},{1,13},{3,15... | collective-permute-start | bytes 460808 | tf_op jit(solution)/shard_map/ppermute | solution.py:121
  7.2 1.3 %collective-permute-start.2 = (bf16[48,1600]{1,0:T(8,128)(2,1)S(1)}, bf16[48,1600]{1,0:T(8,128)(2,1)S(1)}, u32[]{:S(2)}, u32[]{:S(2)}) collective-permute-start(bf16[48,1600]{1,0:T(8,128)(2,1)S(1)} %get-tuple-element.34), channel_id=1, source_target_pairs={{0,10},{2,8},{4,14},{6,12},{8,2},{10,0},{12,6},{14,4},{1,15},{3,13... | collective-permute-start | bytes 460808 | tf_op jit(solution)/shard_map/ppermute | solution.py:121
  8.5 1.6 %collective-permute-start = (bf16[48,1600]{1,0:T(8,128)(2,1)S(1)}, bf16[48,1600]{1,0:T(8,128)(2,1)S(1)}, u32[]{:S(2)}, u32[]{:S(2)}) collective-permute-start(bf16[48,1600]{1,0:T(8,128)(2,1)S(1)} %get-tuple-element.32.refs_1_), channel_id=1, source_target_pairs={{0,4},{2,6},{4,0},{6,2},{8,12},{10,14},{12,8},{14,10},{1,7},{3,5},... | collective-permute-start | bytes 460808 | tf_op jit(solution)/shard_map/ppermute | solution.py:121
  10.1 3.0 %prepare.3 = (bf16[48,1600]{1,0:T(8,128)(2,1)S(1)}, bf16[48,1600]{1,0:T(8,128)(2,1)S(1)}, bf16[48,1600]{1,0:T(8,128)(2,1)S(1)}, bf16[96,1600]{1,0:T(8,128)(2,1)S(1)}) custom-call(bf16[3,2,64,3200]{3,2,1,0:T(8,128)(2,1)} %bitcast.8, f32[100,128]{1,0:T(8,128)} %bitcast.10, f32[100,128]{1,0:T(8,128)} %bitcast.12, s32[8]{0:T(128)} %count_hbm.3, ...), custom_call_target="tpu_custom_call" | custom-call | bytes 4915200 | tf_op jit(solution)/shard_map/prepare/pallas_call | solution.py:97
  13.1 0.5 collective-permute-start.6
  13.6 2.1 %collective-permute-start.3 = (bf16[96,1600]{1,0:T(8,128)(2,1)S(1)}, bf16[96,1600]{1,0:T(8,128)(2,1)S(1)}, u32[]{:S(2)}, u32[]{:S(2)}) collective-permute-start(bf16[96,1600]{1,0:T(8,128)(2,1)S(1)} %get-tuple-element.36.refs_4_), channel_id=1, source_target_pairs={{0,2},{2,0},{4,6},{6,4},{8,10},{10,8},{12,14},{14,12},{16,18},{18,... | collective-permute-start | bytes 921608 | tf_op jit(solution)/shard_map/ppermute | solution.py:121
  15.8 0.0 copy-done.2
  15.8 0.0 copy-done.3
  15.8 0.1 iota_add_fusion
  15.9 0.1 add.69
  16.0 3.0 %collective-permute-done.1.refs_1_ = bf16[48,1600]{1,0:T(8,128)(2,1)S(1)} collective-permute-done((bf16[48,1600]{1,0:T(8,128)(2,1)S(1)}, bf16[48,1600]{1,0:T(8,128)(2,1)S(1)}, u32[]{:S(2)}, u32[]{:S(2)}) %collective-permute-start.1) | collective-permute-done | bytes 153632 | tf_op jit(solution)/shard_map/ppermute | solution.py:121
  19.0 0.0 collective-permute-start.7
  19.0 4.9 %collective-permute-done.2.refs_2_ = bf16[48,1600]{1,0:T(8,128)(2,1)S(1)} collective-permute-done((bf16[48,1600]{1,0:T(8,128)(2,1)S(1)}, bf16[48,1600]{1,0:T(8,128)(2,1)S(1)}, u32[]{:S(2)}, u32[]{:S(2)}) %collective-permute-start.2) | collective-permute-done | bytes 153632 | tf_op jit(solution)/shard_map/ppermute | solution.py:121
  23.9 0.0 collective-permute-start.8
  23.9 0.0 collective-permute-done.refs_0_
  23.9 1.5 %collective-permute-done.3.refs_3_ = bf16[96,1600]{1,0:T(8,128)(2,1)S(1)} collective-permute-done((bf16[96,1600]{1,0:T(8,128)(2,1)S(1)}, bf16[96,1600]{1,0:T(8,128)(2,1)S(1)}, u32[]{:S(2)}, u32[]{:S(2)}) %collective-permute-start.3) | collective-permute-done | bytes 307232 | tf_op jit(solution)/shard_map/ppermute | solution.py:121
  25.4 0.1 pack.2.refs_0_.mine_ref
  25.5 0.1 collective-permute-start.4
  25.5 0.0 copy-done.4
  25.6 0.2 select_reduce_fusion
  25.8 0.1 select_reduce_fusion.1
  25.9 2.9 %load.1.w_ref = bf16[1600,2048]{1,0:T(8,128)(2,1)S(1)} custom-call(bf16[1600,2048]{1,0:T(8,128)(2,1)} %w_hbm.1, bf16[192,1664]{1,0:T(8,128)(2,1)S(1)} %pack.2.refs_0_.mine_ref), custom_call_target="tpu_custom_call" | custom-call | bytes 13107200 | tf_op jit(solution)/shard_map/load/pallas_call | solution.py:157
  28.7 0.0 collective-permute-done.4.other_ref
  28.8 3.7 %gather_and_project.2 = (bf16[384,1664]{1,0:T(8,128)(2,1)}, bf16[192,2048]{1,0:T(8,128)(2,1)S(1)}, bf16[192,2048]{1,0:T(8,128)(2,1)S(1)}) custom-call(s32[24]{0:T(128)S(1)} %get-tuple-element.59.order_ref, bf16[192,1664]{1,0:T(8,128)(2,1)S(1)} %pack.2.refs_0_.mine_ref, bf16[192,1664]{1,0:T(8,128)(2,1)S(1)} %collective-permute-done.4.other_ref, ...), custom_call_target="tpu_custom_call" | custom-call | flops 2516582400 | bytes 9355264 | tf_op jit(solution)/shard_map/gather_and_project/pallas_call | solution.py:229
  32.4 0.3 collective-permute-start.5
  32.7 0.0 collective-permute-done.6.refs_0_
  32.7 0.8 collective-permute-done.7.refs_1_
  33.5 2.9 %collective-permute-done.8.refs_2_ = bf16[48,1600]{1,0:T(8,128)(2,1)S(1)} collective-permute-done((bf16[48,1600]{1,0:T(8,128)(2,1)S(1)}, bf16[48,1600]{1,0:T(8,128)(2,1)S(1)}, u32[]{:S(2)}, u32[]{:S(2)}) %collective-permute-start.8) | collective-permute-done | bytes 153632 | tf_op jit(solution)/shard_map/ppermute | solution.py:121
  36.4 0.1 pack.3.mine_ref.refs_0_
  36.5 0.1 collective-permute-start.9
  36.6 2.1 %collective-permute-done.9.other_ref = bf16[192,1664]{1,0:T(8,128)(2,1)S(1)} collective-permute-done((bf16[192,1664]{1,0:T(8,128)(2,1)S(1)}, bf16[192,1664]{1,0:T(8,128)(2,1)S(1)}, u32[]{:S(2)}, u32[]{:S(2)}) %collective-permute-start.9) | collective-permute-done | bytes 639008 | tf_op jit(solution)/shard_map/ppermute | solution.py:365
  38.6 2.2 %gather_and_project.3 = (bf16[384,1664]{1,0:T(8,128)(2,1)S(1)}, bf16[192,1024]{1,0:T(8,128)(2,1)S(1)}, bf16[192,1024]{1,0:T(8,128)(2,1)S(1)}) custom-call(s32[24]{0:T(128)S(1)} %get-tuple-element.59.order_ref, bf16[192,1664]{1,0:T(8,128)(2,1)S(1)} %pack.3.mine_ref.refs_0_, bf16[192,1664]{1,0:T(8,128)(2,1)S(1)} %collective-permute-done.9.other_ref, ...), custom_call_target="tpu_custom_call" | custom-call | flops 1258291200 | bytes 5292032 | tf_op jit(solution)/shard_map/gather_and_project/pallas_call | solution.py:229
  40.9 0.6 collective-permute-start.12
  41.5 3.4 %collective-permute-done.5.refs_1_ = bf16[192,2048]{1,0:T(8,128)(2,1)S(1)} collective-permute-done((bf16[192,2048]{1,0:T(8,128)(2,1)S(1)}, bf16[192,2048]{1,0:T(8,128)(2,1)S(1)}, u32[]{:S(2)}, u32[]{:S(2)}) %collective-permute-start.5) | collective-permute-done | bytes 786464 | tf_op jit(solution)/shard_map/ppermute | solution.py:293
  44.8 0.2 accumulate.6
  45.0 1.6 %project.1 = (bf16[192,1024]{1,0:T(8,128)(2,1)S(1)}, bf16[192,1024]{1,0:T(8,128)(2,1)S(1)}) custom-call(bf16[384,1664]{1,0:T(8,128)(2,1)S(1)} %get-tuple-element.45.a_ref, bf16[1600,2048]{1,0:T(8,128)(2,1)S(1)} %load.1.w_ref, f32[96,2048]{1,0:T(8,128)S(1)} %get-tuple-element.43.refs_0_), custom_call_target="tpu_custom_call" | custom-call | flops 1258291200 | bytes 5292032 | tf_op jit(solution)/shard_map/project/pallas_call | solution.py:213
  46.6 0.0 copy-start.1
  46.6 0.6 collective-permute-start.11
  47.2 3.0 %collective-permute-start.10 = (bf16[96,2048]{1,0:T(8,128)(2,1)S(1)}, bf16[96,2048]{1,0:T(8,128)(2,1)S(1)}, u32[]{:S(2)}, u32[]{:S(2)}) collective-permute-start(bf16[96,2048]{1,0:T(8,128)(2,1)S(1)} %get-tuple-element.44), channel_id=1, source_target_pairs={{0,4},{2,6},{4,0},{6,2},{8,12},{10,14},{12,8},{14,10},{1,3},{3,1},... | collective-permute-start | bytes 1179656 | tf_op jit(solution)/shard_map/ppermute | solution.py:293
  50.3 0.0 collective-permute-done.12.refs_1_
  50.3 0.1 accumulate.7
  50.3 0.9 %collective-permute-start.14 = (bf16[96,1024]{1,0:T(8,128)(2,1)S(1)}, bf16[96,1024]{1,0:T(8,128)(2,1)S(1)}, u32[]{:S(2)}, u32[]{:S(2)}) collective-permute-start(bf16[96,1024]{1,0:T(8,128)(2,1)S(1)} %get-tuple-element.53), channel_id=1, source_target_pairs={{0,4},{2,6},{4,0},{6,2},{8,12},{10,14},{12,8},{14,10},{1,3},{3,1},... | collective-permute-start | bytes 589832 | tf_op jit(solution)/shard_map/ppermute | solution.py:293
  51.2 7.1 %collective-permute-done.11.refs_1_ = bf16[192,1024]{1,0:T(8,128)(2,1)S(1)} collective-permute-done((bf16[192,1024]{1,0:T(8,128)(2,1)S(1)}, bf16[192,1024]{1,0:T(8,128)(2,1)S(1)}, u32[]{:S(2)}, u32[]{:S(2)}) %collective-permute-start.11) | collective-permute-done | bytes 393248 | tf_op jit(solution)/shard_map/ppermute | solution.py:293
  58.3 0.1 accumulate.8
  58.4 0.0 collective-permute-done.10.refs_1_
  58.4 0.1 accumulate.9
  58.5 1.5 %collective-permute-start.13 = (bf16[48,2048]{1,0:T(8,128)(2,1)S(1)}, bf16[48,2048]{1,0:T(8,128)(2,1)S(1)}, u32[]{:S(2)}, u32[]{:S(2)}) collective-permute-start(bf16[48,2048]{1,0:T(8,128)(2,1)S(1)} %get-tuple-element.52), channel_id=1, source_target_pairs={{0,8},{2,10},{4,12},{6,14},{8,0},{10,2},{12,4},{14,6},{1,9},{3,11}... | collective-permute-start | bytes 589832 | tf_op jit(solution)/shard_map/ppermute | solution.py:293
  60.0 3.2 %collective-permute-start.16 = (bf16[96,1024]{1,0:T(8,128)(2,1)S(1)}, bf16[96,1024]{1,0:T(8,128)(2,1)S(1)}, u32[]{:S(2)}, u32[]{:S(2)}) collective-permute-start(bf16[96,1024]{1,0:T(8,128)(2,1)S(1)} %get-tuple-element.56), channel_id=1, source_target_pairs={{0,4},{2,6},{4,0},{6,2},{8,12},{10,14},{12,8},{14,10},{1,3},{3,1},... | collective-permute-start | bytes 589832 | tf_op jit(solution)/shard_map/ppermute | solution.py:293
  63.2 0.1 slice.7
  63.3 0.0 copy-done.1
  63.3 0.2 select_reduce_fusion.2
  63.5 0.0 collective-permute-done.14.refs_1_
  63.5 0.7 collective-permute-start.15
  64.3 7.7 %collective-permute-done.13.recv_ref = bf16[48,2048]{1,0:T(8,128)(2,1)S(1)} collective-permute-done((bf16[48,2048]{1,0:T(8,128)(2,1)S(1)}, bf16[48,2048]{1,0:T(8,128)(2,1)S(1)}, u32[]{:S(2)}, u32[]{:S(2)}) %collective-permute-start.13) | collective-permute-done | bytes 196640 | tf_op jit(solution)/shard_map/ppermute | solution.py:293
  72.0 0.1 early.1.refs_2_.refs_0_
  72.2 0.0 collective-permute-done.16.refs_1_
  72.2 0.1 collective-permute-start.17
  72.3 0.1 compare_convert_fusion.live_ref
  72.4 1.7 %collective-permute-done.15.refs_2_ = bf16[48,1024]{1,0:T(8,128)(2,1)S(1)} collective-permute-done((bf16[48,1024]{1,0:T(8,128)(2,1)S(1)}, bf16[48,1024]{1,0:T(8,128)(2,1)S(1)}, u32[]{:S(2)}, u32[]{:S(2)}) %collective-permute-start.15) | collective-permute-done | bytes 98336 | tf_op jit(solution)/shard_map/ppermute | solution.py:293
  74.1 4.8 %collective-permute-done.17.refs_4_ = bf16[48,1024]{1,0:T(8,128)(2,1)S(1)} collective-permute-done((bf16[48,1024]{1,0:T(8,128)(2,1)S(1)}, bf16[48,1024]{1,0:T(8,128)(2,1)S(1)}, u32[]{:S(2)}, u32[]{:S(2)}) %collective-permute-start.17) | collective-permute-done | bytes 98336 | tf_op jit(solution)/shard_map/ppermute | solution.py:293
  78.9 1.4 %finish.1 = bf16[3,2,16,2048]{3,2,1,0:T(8,128)(2,1)} custom-call(s32[3]{0:T(128)S(1)} %compare_convert_fusion.live_ref, f32[1,2048]{1,0:T(1,128)S(1)} %bitcast.6, bf16[48,2048]{1,0:T(8,128)(2,1)S(1)} %early.1.refs_2_.refs_0_, f32[48,1024]{1,0:T(8,128)S(1)} %get-tuple-element.54.refs_0_.refs_1_, bf16[48,1024]{1,0:T(8,128)(2,1)S(1)} %collective-permute-done.15.refs_2_, ...), custom_call_target="tpu_custom_call" | custom-call | tf_op jit(solution)/shard_map/finish/pallas_call | solution.py:280
  (10 shorter events, 0.1 us)
Async XLA Ops:
  0.0 15.8 %copy-start.2 = (s32[8]{0:T(128)S(1)}, s32[8]{0:T(128)}, u32[]{:S(2)}) copy-start(s32[8]{0:T(128)} %constant.45.clone) | copy-start | bytes 100
  0.0 15.8 %copy-start.3 = (s32[8]{0:T(128)S(1)}, s32[8]{0:T(128)}, u32[]{:S(2)}) copy-start(s32[8]{0:T(128)} %constant.44.clone) | copy-start | bytes 100
  3.1 22.5 %copy-start.4 = (s32[24]{0:T(128)S(1)}, s32[24]{0:T(128)}, u32[]{:S(2)}) copy-start(s32[24]{0:T(128)} %param.18) | copy-start | bytes 292
  3.1 22.7 %copy-start.5 = (s32[8]{0:T(128)S(1)}, s32[8]{0:T(128)}, u32[]{:S(2)}) copy-start(s32[8]{0:T(128)} %constant.43.clone) | copy-start | bytes 100
  3.1 15.9 %collective-permute-start.1 = (bf16[48,1600]{1,0:T(8,128)(2,1)S(1)}, bf16[48,1600]{1,0:T(8,128)(2,1)S(1)}, u32[]{:S(2)}, u32[]{:S(2)}) collective-permute-start(bf16[48,1600]{1,0:T(8,128)(2,1)S(1)} %get-tuple-element.33), channel_id=1, source_target_pairs={{0,8},{2,10},{4,12},{6,14},{8,0},{10,2},{12,4},{14,6},{1,13},{3,15... | collective-permute-start | bytes 460808 | tf_op jit(solution)/shard_map/ppermute | solution.py:121
  7.2 16.7 %collective-permute-start.2 = (bf16[48,1600]{1,0:T(8,128)(2,1)S(1)}, bf16[48,1600]{1,0:T(8,128)(2,1)S(1)}, u32[]{:S(2)}, u32[]{:S(2)}) collective-permute-start(bf16[48,1600]{1,0:T(8,128)(2,1)S(1)} %get-tuple-element.34), channel_id=1, source_target_pairs={{0,10},{2,8},{4,14},{6,12},{8,2},{10,0},{12,6},{14,4},{1,15},{3,13... | collective-permute-start | bytes 460808 | tf_op jit(solution)/shard_map/ppermute | solution.py:121
  8.5 15.4 %collective-permute-start = (bf16[48,1600]{1,0:T(8,128)(2,1)S(1)}, bf16[48,1600]{1,0:T(8,128)(2,1)S(1)}, u32[]{:S(2)}, u32[]{:S(2)}) collective-permute-start(bf16[48,1600]{1,0:T(8,128)(2,1)S(1)} %get-tuple-element.32.refs_1_), channel_id=1, source_target_pairs={{0,4},{2,6},{4,0},{6,2},{8,12},{10,14},{12,8},{14,10},{1,7},{3,5},... | collective-permute-start | bytes 460808 | tf_op jit(solution)/shard_map/ppermute | solution.py:121
  13.1 19.6 %collective-permute-start.6 = (bf16[48,1600]{1,0:T(8,128)(2,1)S(1)}, bf16[48,1600]{1,0:T(8,128)(2,1)S(1)}, u32[]{:S(2)}, u32[]{:S(2)}) collective-permute-start(bf16[48,1600]{1,0:T(8,128)(2,1)S(1)} %get-tuple-element.39), channel_id=1, source_target_pairs={{0,4},{2,6},{4,0},{6,2},{8,12},{10,14},{12,8},{14,10},{1,7},{3,5},... | collective-permute-start | bytes 460808 | tf_op jit(solution)/shard_map/ppermute | solution.py:121
  13.6 11.8 %collective-permute-start.3 = (bf16[96,1600]{1,0:T(8,128)(2,1)S(1)}, bf16[96,1600]{1,0:T(8,128)(2,1)S(1)}, u32[]{:S(2)}, u32[]{:S(2)}) collective-permute-start(bf16[96,1600]{1,0:T(8,128)(2,1)S(1)} %get-tuple-element.36.refs_4_), channel_id=1, source_target_pairs={{0,2},{2,0},{4,6},{6,4},{8,10},{10,8},{12,14},{14,12},{16,18},{18,... | collective-permute-start | bytes 921608 | tf_op jit(solution)/shard_map/ppermute | solution.py:121
  19.0 14.6 %collective-permute-start.7 = (bf16[48,1600]{1,0:T(8,128)(2,1)S(1)}, bf16[48,1600]{1,0:T(8,128)(2,1)S(1)}, u32[]{:S(2)}, u32[]{:S(2)}) collective-permute-start(bf16[48,1600]{1,0:T(8,128)(2,1)S(1)} %get-tuple-element.40), channel_id=1, source_target_pairs={{0,8},{2,10},{4,12},{6,14},{8,0},{10,2},{12,4},{14,6},{1,13},{3,15... | collective-permute-start | bytes 460808 | tf_op jit(solution)/shard_map/ppermute | solution.py:121
  23.9 12.5 %collective-permute-start.8 = (bf16[48,1600]{1,0:T(8,128)(2,1)S(1)}, bf16[48,1600]{1,0:T(8,128)(2,1)S(1)}, u32[]{:S(2)}, u32[]{:S(2)}) collective-permute-start(bf16[48,1600]{1,0:T(8,128)(2,1)S(1)} %get-tuple-element.41), channel_id=1, source_target_pairs={{0,10},{2,8},{4,14},{6,12},{8,2},{10,0},{12,6},{14,4},{1,15},{3,13... | collective-permute-start | bytes 460808 | tf_op jit(solution)/shard_map/ppermute | solution.py:121
  25.5 3.3 %collective-permute-start.4 = (bf16[192,1664]{1,0:T(8,128)(2,1)S(1)}, bf16[192,1664]{1,0:T(8,128)(2,1)S(1)}, u32[]{:S(2)}, u32[]{:S(2)}) collective-permute-start(bf16[192,1664]{1,0:T(8,128)(2,1)S(1)} %pack.2.refs_0_.mine_ref), channel_id=1, source_target_pairs={{0,1},{1,0},{2,3},{3,2},{4,5},{5,4},{6,7},{7,6},{8,9},{9,8},{10,11... | collective-permute-start | bytes 1916936 | tf_op jit(solution)/shard_map/ppermute | solution.py:365
  32.4 12.4 %collective-permute-start.5 = (bf16[192,2048]{1,0:T(8,128)(2,1)S(1)}, bf16[192,2048]{1,0:T(8,128)(2,1)S(1)}, u32[]{:S(2)}, u32[]{:S(2)}) collective-permute-start(bf16[192,2048]{1,0:T(8,128)(2,1)S(1)} %get-tuple-element.38), channel_id=1, source_target_pairs={{0,2},{2,0},{4,6},{6,4},{8,10},{10,8},{12,14},{14,12},{1,5},{3,7},... | collective-permute-start | bytes 2359304 | tf_op jit(solution)/shard_map/ppermute | solution.py:293
  36.5 2.1 %collective-permute-start.9 = (bf16[192,1664]{1,0:T(8,128)(2,1)S(1)}, bf16[192,1664]{1,0:T(8,128)(2,1)S(1)}, u32[]{:S(2)}, u32[]{:S(2)}) collective-permute-start(bf16[192,1664]{1,0:T(8,128)(2,1)S(1)} %pack.3.mine_ref.refs_0_), channel_id=1, source_target_pairs={{0,1},{1,0},{2,3},{3,2},{4,5},{5,4},{6,7},{7,6},{8,9},{9,8},{10,11... | collective-permute-start | bytes 1916936 | tf_op jit(solution)/shard_map/ppermute | solution.py:365
  40.9 9.4 %collective-permute-start.12 = (bf16[192,1024]{1,0:T(8,128)(2,1)S(1)}, bf16[192,1024]{1,0:T(8,128)(2,1)S(1)}, u32[]{:S(2)}, u32[]{:S(2)}) collective-permute-start(bf16[192,1024]{1,0:T(8,128)(2,1)S(1)} %get-tuple-element.48), channel_id=1, source_target_pairs={{0,2},{2,0},{4,6},{6,4},{8,10},{10,8},{12,14},{14,12},{1,5},{3,7},... | collective-permute-start | bytes 1179656 | tf_op jit(solution)/shard_map/ppermute | solution.py:293
  46.6 16.7 %copy-start.1 = (s32[8]{0:T(128)S(1)}, s32[8]{0:T(128)}, u32[]{:S(2)}) copy-start(s32[8]{0:T(128)} %count_hbm.3) | copy-start | bytes 100
  46.6 11.7 %collective-permute-start.11 = (bf16[192,1024]{1,0:T(8,128)(2,1)S(1)}, bf16[192,1024]{1,0:T(8,128)(2,1)S(1)}, u32[]{:S(2)}, u32[]{:S(2)}) collective-permute-start(bf16[192,1024]{1,0:T(8,128)(2,1)S(1)} %get-tuple-element.47), channel_id=1, source_target_pairs={{0,2},{2,0},{4,6},{6,4},{8,10},{10,8},{12,14},{14,12},{1,5},{3,7},... | collective-permute-start | bytes 1179656 | tf_op jit(solution)/shard_map/ppermute | solution.py:293
  47.2 11.2 %collective-permute-start.10 = (bf16[96,2048]{1,0:T(8,128)(2,1)S(1)}, bf16[96,2048]{1,0:T(8,128)(2,1)S(1)}, u32[]{:S(2)}, u32[]{:S(2)}) collective-permute-start(bf16[96,2048]{1,0:T(8,128)(2,1)S(1)} %get-tuple-element.44), channel_id=1, source_target_pairs={{0,4},{2,6},{4,0},{6,2},{8,12},{10,14},{12,8},{14,10},{1,3},{3,1},... | collective-permute-start | bytes 1179656 | tf_op jit(solution)/shard_map/ppermute | solution.py:293
  50.3 21.8 %copy-start = (f32[2048]{0:T(1024)S(1)}, f32[2048]{0:T(1024)}, u32[]{:S(2)}) copy-start(f32[2048]{0:T(1024)} %param.16) | copy-start | bytes 24580
  50.3 13.1 %collective-permute-start.14 = (bf16[96,1024]{1,0:T(8,128)(2,1)S(1)}, bf16[96,1024]{1,0:T(8,128)(2,1)S(1)}, u32[]{:S(2)}, u32[]{:S(2)}) collective-permute-start(bf16[96,1024]{1,0:T(8,128)(2,1)S(1)} %get-tuple-element.53), channel_id=1, source_target_pairs={{0,4},{2,6},{4,0},{6,2},{8,12},{10,14},{12,8},{14,10},{1,3},{3,1},... | collective-permute-start | bytes 589832 | tf_op jit(solution)/shard_map/ppermute | solution.py:293
  58.5 13.5 %collective-permute-start.13 = (bf16[48,2048]{1,0:T(8,128)(2,1)S(1)}, bf16[48,2048]{1,0:T(8,128)(2,1)S(1)}, u32[]{:S(2)}, u32[]{:S(2)}) collective-permute-start(bf16[48,2048]{1,0:T(8,128)(2,1)S(1)} %get-tuple-element.52), channel_id=1, source_target_pairs={{0,8},{2,10},{4,12},{6,14},{8,0},{10,2},{12,4},{14,6},{1,9},{3,11}... | collective-permute-start | bytes 589832 | tf_op jit(solution)/shard_map/ppermute | solution.py:293
  60.0 12.1 %collective-permute-start.16 = (bf16[96,1024]{1,0:T(8,128)(2,1)S(1)}, bf16[96,1024]{1,0:T(8,128)(2,1)S(1)}, u32[]{:S(2)}, u32[]{:S(2)}) collective-permute-start(bf16[96,1024]{1,0:T(8,128)(2,1)S(1)} %get-tuple-element.56), channel_id=1, source_target_pairs={{0,4},{2,6},{4,0},{6,2},{8,12},{10,14},{12,8},{14,10},{1,3},{3,1},... | collective-permute-start | bytes 589832 | tf_op jit(solution)/shard_map/ppermute | solution.py:293
  63.5 10.5 %collective-permute-start.15 = (bf16[48,1024]{1,0:T(8,128)(2,1)S(1)}, bf16[48,1024]{1,0:T(8,128)(2,1)S(1)}, u32[]{:S(2)}, u32[]{:S(2)}) collective-permute-start(bf16[48,1024]{1,0:T(8,128)(2,1)S(1)} %get-tuple-element.55), channel_id=1, source_target_pairs={{0,8},{2,10},{4,12},{6,14},{8,0},{10,2},{12,4},{14,6},{1,9},{3,11}... | collective-permute-start | bytes 294920 | tf_op jit(solution)/shard_map/ppermute | solution.py:293
  72.2 6.7 %collective-permute-start.17 = (bf16[48,1024]{1,0:T(8,128)(2,1)S(1)}, bf16[48,1024]{1,0:T(8,128)(2,1)S(1)}, u32[]{:S(2)}, u32[]{:S(2)}) collective-permute-start(bf16[48,1024]{1,0:T(8,128)(2,1)S(1)} %get-tuple-element.58), channel_id=1, source_target_pairs={{0,8},{2,10},{4,12},{6,14},{8,0},{10,2},{12,4},{14,6},{1,9},{3,11}... | collective-permute-start | bytes 294920 | tf_op jit(solution)/shard_map/ppermute | solution.py:293

commit v4 on v3

--- a/solution.py
+++ b/solution.py
@@ -16,7 +16,7 @@
 BIG_VMEM = 20 * 1024 * 1024
 PROJECT_VMEM = 20 * 1024 * 1024
 LANES = 128
-STEPS = [(0, 0), (1, -1), (1, 0), (0, 1), (2, 0), (1, 1), (2, 1), (0, 2), (1, 2), (0, 3), (2, 2)]
+STEPS = [(0, 0), (1, -1), (1, 0), (0, 1), (2, 0), (1, 1), (0, 2), (2, 1), (1, 2), (0, 3), (2, 2)]
 
 
 def arrangement(bits):

time: 80.6 us -> 79.9 us (level)
  waiting for transfers between devices: 40 us -> 35.8 us
  starting transfers between devices: 20.7 us -> 24.2 us
    ppermute x9, waiting for transfers between devices: 24.8 us -> 20.6 us  [exchange(): return lax.ppermute(array, ('dp', 'tensor'), pairs)]
    ppermute x9, starting transfers between devices: 10.9 us -> 14.4 us  [exchange(): return lax.ppermute(array, ('dp', 'tensor'), pairs)]
  transfers between devices with their start and end apart: 18 -> 18, of which waited for: 11 -> 14; matrix products, arithmetic and copies ran while one was open for 1% -> 1% of each run, Pallas kernels for 18% -> 18%
where the time goes in v4:
time: 79.9 us; the launch traced here: 79.7 us
  waiting for transfers between devices  35.8 us (45%)
  starting transfers between devices  24.2 us (30%)
  Pallas kernels  18.6 us (23%)
    ppermute x9, waiting for transfers between devices, exchange(): return lax.ppermute(array, ('dp', 'tensor'), pairs)  20.6 us
    ppermute x9, starting transfers between devices, exchange(): return lax.ppermute(array, ('dp', 'tensor'), pairs)  14.4 us
    ppermute x7, waiting for transfers between devices, send_piece(): return lax.ppermute(piece, ('dp', 'tensor'), pairs)  13.1 us
    ppermute x7, starting transfers between devices, send_piece(): return lax.ppermute(piece, ('dp', 'tensor'), pairs)  9.64 us
    pallas_call x2, Pallas kernels, prepare(): pl.pallas_call(functools.partial(prepare_kernel, peers, tiles, phase), in...  6.11 us
    pallas_call x2, Pallas kernels, gather_and_project(): pl.pallas_call(functools.partial(gather_kernel, first, block, len(pieces)...  5.89 us
    pallas_call x1, Pallas kernels, load(): pl.pallas_call(load_kernel, in_specs=[pl.BlockSpec(memory_space=pl.ANY)]...  2.87 us
    ppermute x2, waiting for transfers between devices, body(): packed[phase] = (mine, lax.ppermute(mine, 'tensor', [(0, 1), (1, 0)]))  2.06 us
  transfers between devices with their start and end apart: 18, of which 14 were waited for; matrix products, arithmetic and copies ran while one was open for 1% of the time, Pallas kernels for 18%

profile of v4, /device:TPU:0, one launch (start us, length us, event | category | flops | bytes accessed | tf_op | source)
XLA Modules:
  0.0 79.7 jit_solution(8881451362517169357)
XLA Ops:
  0.0 3.1 %prepare.2 = (bf16[48,1600]{1,0:T(8,128)(2,1)S(1)}, bf16[48,1600]{1,0:T(8,128)(2,1)S(1)}, bf16[48,1600]{1,0:T(8,128)(2,1)S(1)}, bf16[48,1600]{1,0:T(8,128)(2,1)S(1)}) custom-call(bf16[3,2,64,3200]{3,2,1,0:T(8,128)(2,1)} %bitcast.7, f32[100,128]{1,0:T(8,128)} %bitcast.9, f32[100,128]{1,0:T(8,128)} %bitcast.11, s32[8]{0:T(128)} %count_hbm.3), custom_call_target="tpu_custom_call" | custom-call | bytes 4915200 | tf_op jit(solution)/shard_map/prepare/pallas_call | solution.py:97
  3.1 0.0 copy-start.4
  3.1 0.0 copy-start.5
  3.1 4.1 %collective-permute-start.1 = (bf16[48,1600]{1,0:T(8,128)(2,1)S(1)}, bf16[48,1600]{1,0:T(8,128)(2,1)S(1)}, u32[]{:S(2)}, u32[]{:S(2)}) collective-permute-start(bf16[48,1600]{1,0:T(8,128)(2,1)S(1)} %get-tuple-element.33), channel_id=1, source_target_pairs={{0,8},{2,10},{4,12},{6,14},{8,0},{10,2},{12,4},{14,6},{1,13},{3,15... | collective-permute-start | bytes 460808 | tf_op jit(solution)/shard_map/ppermute | solution.py:121
  7.2 1.3 %collective-permute-start.2 = (bf16[48,1600]{1,0:T(8,128)(2,1)S(1)}, bf16[48,1600]{1,0:T(8,128)(2,1)S(1)}, u32[]{:S(2)}, u32[]{:S(2)}) collective-permute-start(bf16[48,1600]{1,0:T(8,128)(2,1)S(1)} %get-tuple-element.34), channel_id=1, source_target_pairs={{0,10},{2,8},{4,14},{6,12},{8,2},{10,0},{12,6},{14,4},{1,15},{3,13... | collective-permute-start | bytes 460808 | tf_op jit(solution)/shard_map/ppermute | solution.py:121
  8.5 1.6 %collective-permute-start = (bf16[48,1600]{1,0:T(8,128)(2,1)S(1)}, bf16[48,1600]{1,0:T(8,128)(2,1)S(1)}, u32[]{:S(2)}, u32[]{:S(2)}) collective-permute-start(bf16[48,1600]{1,0:T(8,128)(2,1)S(1)} %get-tuple-element.32.refs_1_), channel_id=1, source_target_pairs={{0,4},{2,6},{4,0},{6,2},{8,12},{10,14},{12,8},{14,10},{1,7},{3,5},... | collective-permute-start | bytes 460808 | tf_op jit(solution)/shard_map/ppermute | solution.py:121
  10.1 3.0 %prepare.3 = (bf16[48,1600]{1,0:T(8,128)(2,1)S(1)}, bf16[48,1600]{1,0:T(8,128)(2,1)S(1)}, bf16[48,1600]{1,0:T(8,128)(2,1)S(1)}, bf16[96,1600]{1,0:T(8,128)(2,1)S(1)}) custom-call(bf16[3,2,64,3200]{3,2,1,0:T(8,128)(2,1)} %bitcast.8, f32[100,128]{1,0:T(8,128)} %bitcast.10, f32[100,128]{1,0:T(8,128)} %bitcast.12, s32[8]{0:T(128)} %count_hbm.3, ...), custom_call_target="tpu_custom_call" | custom-call | bytes 4915200 | tf_op jit(solution)/shard_map/prepare/pallas_call | solution.py:97
  13.1 0.5 collective-permute-start.6
  13.6 2.1 %collective-permute-start.3 = (bf16[96,1600]{1,0:T(8,128)(2,1)S(1)}, bf16[96,1600]{1,0:T(8,128)(2,1)S(1)}, u32[]{:S(2)}, u32[]{:S(2)}) collective-permute-start(bf16[96,1600]{1,0:T(8,128)(2,1)S(1)} %get-tuple-element.36.refs_4_), channel_id=1, source_target_pairs={{0,2},{2,0},{4,6},{6,4},{8,10},{10,8},{12,14},{14,12},{16,18},{18,... | collective-permute-start | bytes 921608 | tf_op jit(solution)/shard_map/ppermute | solution.py:121
  15.8 0.0 copy-done.2
  15.8 0.0 copy-done.3
  15.8 0.1 iota_add_fusion
  15.9 0.1 add.69
  16.0 3.0 %collective-permute-done.1.refs_1_ = bf16[48,1600]{1,0:T(8,128)(2,1)S(1)} collective-permute-done((bf16[48,1600]{1,0:T(8,128)(2,1)S(1)}, bf16[48,1600]{1,0:T(8,128)(2,1)S(1)}, u32[]{:S(2)}, u32[]{:S(2)}) %collective-permute-start.1) | collective-permute-done | bytes 153632 | tf_op jit(solution)/shard_map/ppermute | solution.py:121
  19.0 0.0 collective-permute-start.7
  19.0 4.9 %collective-permute-done.2.refs_2_ = bf16[48,1600]{1,0:T(8,128)(2,1)S(1)} collective-permute-done((bf16[48,1600]{1,0:T(8,128)(2,1)S(1)}, bf16[48,1600]{1,0:T(8,128)(2,1)S(1)}, u32[]{:S(2)}, u32[]{:S(2)}) %collective-permute-start.2) | collective-permute-done | bytes 153632 | tf_op jit(solution)/shard_map/ppermute | solution.py:121
  23.9 0.0 collective-permute-start.8
  23.9 0.0 collective-permute-done.refs_0_
  23.9 1.5 %collective-permute-done.3.refs_3_ = bf16[96,1600]{1,0:T(8,128)(2,1)S(1)} collective-permute-done((bf16[96,1600]{1,0:T(8,128)(2,1)S(1)}, bf16[96,1600]{1,0:T(8,128)(2,1)S(1)}, u32[]{:S(2)}, u32[]{:S(2)}) %collective-permute-start.3) | collective-permute-done | bytes 307232 | tf_op jit(solution)/shard_map/ppermute | solution.py:121
  25.4 0.1 pack.2.refs_0_.mine_ref
  25.5 0.1 collective-permute-start.4
  25.5 0.0 copy-done.4
  25.6 0.2 select_reduce_fusion
  25.8 0.1 select_reduce_fusion.1
  25.9 2.9 %load.1.w_ref = bf16[1600,2048]{1,0:T(8,128)(2,1)S(1)} custom-call(bf16[1600,2048]{1,0:T(8,128)(2,1)} %w_hbm.1, bf16[192,1664]{1,0:T(8,128)(2,1)S(1)} %pack.2.refs_0_.mine_ref), custom_call_target="tpu_custom_call" | custom-call | bytes 13107200 | tf_op jit(solution)/shard_map/load/pallas_call | solution.py:157
  28.7 0.0 collective-permute-done.4.other_ref
  28.8 3.7 %gather_and_project.2 = (bf16[384,1664]{1,0:T(8,128)(2,1)}, bf16[192,2048]{1,0:T(8,128)(2,1)S(1)}, bf16[192,2048]{1,0:T(8,128)(2,1)S(1)}) custom-call(s32[24]{0:T(128)S(1)} %get-tuple-element.59.order_ref, bf16[192,1664]{1,0:T(8,128)(2,1)S(1)} %pack.2.refs_0_.mine_ref, bf16[192,1664]{1,0:T(8,128)(2,1)S(1)} %collective-permute-done.4.other_ref, ...), custom_call_target="tpu_custom_call" | custom-call | flops 2516582400 | bytes 9355264 | tf_op jit(solution)/shard_map/gather_and_project/pallas_call | solution.py:229
  32.4 0.3 collective-permute-start.5
  32.7 0.0 collective-permute-done.6.refs_0_
  32.7 0.8 %collective-permute-done.7.refs_1_ = bf16[48,1600]{1,0:T(8,128)(2,1)S(1)} collective-permute-done((bf16[48,1600]{1,0:T(8,128)(2,1)S(1)}, bf16[48,1600]{1,0:T(8,128)(2,1)S(1)}, u32[]{:S(2)}, u32[]{:S(2)}) %collective-permute-start.7) | collective-permute-done | bytes 153632 | tf_op jit(solution)/shard_map/ppermute | solution.py:121
  33.5 2.9 %collective-permute-done.8.refs_2_ = bf16[48,1600]{1,0:T(8,128)(2,1)S(1)} collective-permute-done((bf16[48,1600]{1,0:T(8,128)(2,1)S(1)}, bf16[48,1600]{1,0:T(8,128)(2,1)S(1)}, u32[]{:S(2)}, u32[]{:S(2)}) %collective-permute-start.8) | collective-permute-done | bytes 153632 | tf_op jit(solution)/shard_map/ppermute | solution.py:121
  36.4 0.1 pack.3.mine_ref.refs_0_
  36.5 0.1 collective-permute-start.9
  36.6 2.1 %collective-permute-done.9.other_ref = bf16[192,1664]{1,0:T(8,128)(2,1)S(1)} collective-permute-done((bf16[192,1664]{1,0:T(8,128)(2,1)S(1)}, bf16[192,1664]{1,0:T(8,128)(2,1)S(1)}, u32[]{:S(2)}, u32[]{:S(2)}) %collective-permute-start.9) | collective-permute-done | bytes 639008 | tf_op jit(solution)/shard_map/ppermute | solution.py:365
  38.6 2.2 %gather_and_project.3 = (bf16[384,1664]{1,0:T(8,128)(2,1)S(1)}, bf16[192,1024]{1,0:T(8,128)(2,1)S(1)}, bf16[192,1024]{1,0:T(8,128)(2,1)S(1)}) custom-call(s32[24]{0:T(128)S(1)} %get-tuple-element.59.order_ref, bf16[192,1664]{1,0:T(8,128)(2,1)S(1)} %pack.3.mine_ref.refs_0_, bf16[192,1664]{1,0:T(8,128)(2,1)S(1)} %collective-permute-done.9.other_ref, ...), custom_call_target="tpu_custom_call" | custom-call | flops 1258291200 | bytes 5292032 | tf_op jit(solution)/shard_map/gather_and_project/pallas_call | solution.py:229
  40.9 0.6 collective-permute-start.11
  41.5 3.4 %collective-permute-done.5.refs_1_ = bf16[192,2048]{1,0:T(8,128)(2,1)S(1)} collective-permute-done((bf16[192,2048]{1,0:T(8,128)(2,1)S(1)}, bf16[192,2048]{1,0:T(8,128)(2,1)S(1)}, u32[]{:S(2)}, u32[]{:S(2)}) %collective-permute-start.5) | collective-permute-done | bytes 786464 | tf_op jit(solution)/shard_map/ppermute | solution.py:293
  44.8 0.2 accumulate.6
  45.0 2.1 %collective-permute-start.10 = (bf16[96,2048]{1,0:T(8,128)(2,1)S(1)}, bf16[96,2048]{1,0:T(8,128)(2,1)S(1)}, u32[]{:S(2)}, u32[]{:S(2)}) collective-permute-start(bf16[96,2048]{1,0:T(8,128)(2,1)S(1)} %get-tuple-element.44), channel_id=1, source_target_pairs={{0,4},{2,6},{4,0},{6,2},{8,12},{10,14},{12,8},{14,10},{1,3},{3,1},... | collective-permute-start | bytes 1179656 | tf_op jit(solution)/shard_map/ppermute | solution.py:293
  47.1 1.6 %project.1 = (bf16[192,1024]{1,0:T(8,128)(2,1)S(1)}, bf16[192,1024]{1,0:T(8,128)(2,1)S(1)}) custom-call(bf16[384,1664]{1,0:T(8,128)(2,1)S(1)} %get-tuple-element.46.a_ref, bf16[1600,2048]{1,0:T(8,128)(2,1)S(1)} %load.1.w_ref, f32[96,2048]{1,0:T(8,128)S(1)} %get-tuple-element.43.refs_0_), custom_call_target="tpu_custom_call" | custom-call | flops 1258291200 | bytes 5292032 | tf_op jit(solution)/shard_map/project/pallas_call | solution.py:213
  48.7 0.0 copy-start.1
  48.7 1.6 %collective-permute-start.14 = (bf16[192,1024]{1,0:T(8,128)(2,1)S(1)}, bf16[192,1024]{1,0:T(8,128)(2,1)S(1)}, u32[]{:S(2)}, u32[]{:S(2)}) collective-permute-start(bf16[192,1024]{1,0:T(8,128)(2,1)S(1)} %get-tuple-element.52), channel_id=1, source_target_pairs={{0,2},{2,0},{4,6},{6,4},{8,10},{10,8},{12,14},{14,12},{1,5},{3,7},... | collective-permute-start | bytes 1179656 | tf_op jit(solution)/shard_map/ppermute | solution.py:293
  50.3 0.1 collective-permute-done.11.refs_1_
  50.4 0.1 accumulate.7
  50.5 2.4 %collective-permute-start.13 = (bf16[96,1024]{1,0:T(8,128)(2,1)S(1)}, bf16[96,1024]{1,0:T(8,128)(2,1)S(1)}, u32[]{:S(2)}, u32[]{:S(2)}) collective-permute-start(bf16[96,1024]{1,0:T(8,128)(2,1)S(1)} %get-tuple-element.51), channel_id=1, source_target_pairs={{0,4},{2,6},{4,0},{6,2},{8,12},{10,14},{12,8},{14,10},{1,3},{3,1},... | collective-permute-start | bytes 589832 | tf_op jit(solution)/shard_map/ppermute | solution.py:293
  52.9 2.7 %collective-permute-done.10.refs_1_ = bf16[96,2048]{1,0:T(8,128)(2,1)S(1)} collective-permute-done((bf16[96,2048]{1,0:T(8,128)(2,1)S(1)}, bf16[96,2048]{1,0:T(8,128)(2,1)S(1)}, u32[]{:S(2)}, u32[]{:S(2)}) %collective-permute-start.10) | collective-permute-done | bytes 393248 | tf_op jit(solution)/shard_map/ppermute | solution.py:293
  55.6 0.1 accumulate.8
  55.7 3.6 %collective-permute-start.12 = (bf16[48,2048]{1,0:T(8,128)(2,1)S(1)}, bf16[48,2048]{1,0:T(8,128)(2,1)S(1)}, u32[]{:S(2)}, u32[]{:S(2)}) collective-permute-start(bf16[48,2048]{1,0:T(8,128)(2,1)S(1)} %get-tuple-element.50), channel_id=1, source_target_pairs={{0,8},{2,10},{4,12},{6,14},{8,0},{10,2},{12,4},{14,6},{1,9},{3,11}... | collective-permute-start | bytes 589832 | tf_op jit(solution)/shard_map/ppermute | solution.py:293
  59.3 0.3 collective-permute-done.14.refs_1_
  59.6 0.1 accumulate.9
  59.7 1.7 %collective-permute-start.16 = (bf16[96,1024]{1,0:T(8,128)(2,1)S(1)}, bf16[96,1024]{1,0:T(8,128)(2,1)S(1)}, u32[]{:S(2)}, u32[]{:S(2)}) collective-permute-start(bf16[96,1024]{1,0:T(8,128)(2,1)S(1)} %get-tuple-element.56), channel_id=1, source_target_pairs={{0,4},{2,6},{4,0},{6,2},{8,12},{10,14},{12,8},{14,10},{1,3},{3,1},... | collective-permute-start | bytes 589832 | tf_op jit(solution)/shard_map/ppermute | solution.py:293
  61.3 0.1 slice.7
  61.4 0.2 select_reduce_fusion.2
  61.6 0.3 collective-permute-done.13.refs_1_
  61.9 2.0 %collective-permute-start.15 = (bf16[48,1024]{1,0:T(8,128)(2,1)S(1)}, bf16[48,1024]{1,0:T(8,128)(2,1)S(1)}, u32[]{:S(2)}, u32[]{:S(2)}) collective-permute-start(bf16[48,1024]{1,0:T(8,128)(2,1)S(1)} %get-tuple-element.55), channel_id=1, source_target_pairs={{0,8},{2,10},{4,12},{6,14},{8,0},{10,2},{12,4},{14,6},{1,9},{3,11}... | collective-permute-start | bytes 294920 | tf_op jit(solution)/shard_map/ppermute | solution.py:293
  64.0 6.4 %collective-permute-done.12.recv_ref = bf16[48,2048]{1,0:T(8,128)(2,1)S(1)} collective-permute-done((bf16[48,2048]{1,0:T(8,128)(2,1)S(1)}, bf16[48,2048]{1,0:T(8,128)(2,1)S(1)}, u32[]{:S(2)}, u32[]{:S(2)}) %collective-permute-start.12) | collective-permute-done | bytes 196640 | tf_op jit(solution)/shard_map/ppermute | solution.py:293
  70.4 0.0 copy-done
  70.4 0.1 early.1.refs_2_.refs_0_
  70.5 0.0 collective-permute-done.16.refs_1_
  70.6 0.1 collective-permute-start.17
  70.6 0.1 compare_convert_fusion.live_ref
  70.7 1.7 %collective-permute-done.15.refs_2_ = bf16[48,1024]{1,0:T(8,128)(2,1)S(1)} collective-permute-done((bf16[48,1024]{1,0:T(8,128)(2,1)S(1)}, bf16[48,1024]{1,0:T(8,128)(2,1)S(1)}, u32[]{:S(2)}, u32[]{:S(2)}) %collective-permute-start.15) | collective-permute-done | bytes 98336 | tf_op jit(solution)/shard_map/ppermute | solution.py:293
  72.4 5.8 %collective-permute-done.17.refs_4_ = bf16[48,1024]{1,0:T(8,128)(2,1)S(1)} collective-permute-done((bf16[48,1024]{1,0:T(8,128)(2,1)S(1)}, bf16[48,1024]{1,0:T(8,128)(2,1)S(1)}, u32[]{:S(2)}, u32[]{:S(2)}) %collective-permute-start.17) | collective-permute-done | bytes 98336 | tf_op jit(solution)/shard_map/ppermute | solution.py:293
  78.2 1.4 %finish.1 = bf16[3,2,16,2048]{3,2,1,0:T(8,128)(2,1)} custom-call(s32[3]{0:T(128)S(1)} %compare_convert_fusion.live_ref, f32[1,2048]{1,0:T(1,128)S(1)} %bitcast.6, bf16[48,2048]{1,0:T(8,128)(2,1)S(1)} %early.1.refs_2_.refs_0_, f32[48,1024]{1,0:T(8,128)S(1)} %get-tuple-element.54.refs_0_.refs_1_, bf16[48,1024]{1,0:T(8,128)(2,1)S(1)} %collective-permute-done.15.refs_2_, ...), custom_call_target="tpu_custom_call" | custom-call | tf_op jit(solution)/shard_map/finish/pallas_call | solution.py:280
  (10 shorter events, 0.1 us)
Async XLA Ops:
  0.0 15.8 %copy-start.2 = (s32[8]{0:T(128)S(1)}, s32[8]{0:T(128)}, u32[]{:S(2)}) copy-start(s32[8]{0:T(128)} %constant.45.clone) | copy-start | bytes 100
  0.0 15.8 %copy-start.3 = (s32[8]{0:T(128)S(1)}, s32[8]{0:T(128)}, u32[]{:S(2)}) copy-start(s32[8]{0:T(128)} %constant.44.clone) | copy-start | bytes 100
  3.1 22.5 %copy-start.4 = (s32[24]{0:T(128)S(1)}, s32[24]{0:T(128)}, u32[]{:S(2)}) copy-start(s32[24]{0:T(128)} %param.18) | copy-start | bytes 292
  3.1 22.7 %copy-start.5 = (s32[8]{0:T(128)S(1)}, s32[8]{0:T(128)}, u32[]{:S(2)}) copy-start(s32[8]{0:T(128)} %constant.43.clone) | copy-start | bytes 100
  3.1 15.9 %collective-permute-start.1 = (bf16[48,1600]{1,0:T(8,128)(2,1)S(1)}, bf16[48,1600]{1,0:T(8,128)(2,1)S(1)}, u32[]{:S(2)}, u32[]{:S(2)}) collective-permute-start(bf16[48,1600]{1,0:T(8,128)(2,1)S(1)} %get-tuple-element.33), channel_id=1, source_target_pairs={{0,8},{2,10},{4,12},{6,14},{8,0},{10,2},{12,4},{14,6},{1,13},{3,15... | collective-permute-start | bytes 460808 | tf_op jit(solution)/shard_map/ppermute | solution.py:121
  7.2 16.7 %collective-permute-start.2 = (bf16[48,1600]{1,0:T(8,128)(2,1)S(1)}, bf16[48,1600]{1,0:T(8,128)(2,1)S(1)}, u32[]{:S(2)}, u32[]{:S(2)}) collective-permute-start(bf16[48,1600]{1,0:T(8,128)(2,1)S(1)} %get-tuple-element.34), channel_id=1, source_target_pairs={{0,10},{2,8},{4,14},{6,12},{8,2},{10,0},{12,6},{14,4},{1,15},{3,13... | collective-permute-start | bytes 460808 | tf_op jit(solution)/shard_map/ppermute | solution.py:121
  8.5 15.4 %collective-permute-start = (bf16[48,1600]{1,0:T(8,128)(2,1)S(1)}, bf16[48,1600]{1,0:T(8,128)(2,1)S(1)}, u32[]{:S(2)}, u32[]{:S(2)}) collective-permute-start(bf16[48,1600]{1,0:T(8,128)(2,1)S(1)} %get-tuple-element.32.refs_1_), channel_id=1, source_target_pairs={{0,4},{2,6},{4,0},{6,2},{8,12},{10,14},{12,8},{14,10},{1,7},{3,5},... | collective-permute-start | bytes 460808 | tf_op jit(solution)/shard_map/ppermute | solution.py:121
  13.1 19.6 %collective-permute-start.6 = (bf16[48,1600]{1,0:T(8,128)(2,1)S(1)}, bf16[48,1600]{1,0:T(8,128)(2,1)S(1)}, u32[]{:S(2)}, u32[]{:S(2)}) collective-permute-start(bf16[48,1600]{1,0:T(8,128)(2,1)S(1)} %get-tuple-element.39), channel_id=1, source_target_pairs={{0,4},{2,6},{4,0},{6,2},{8,12},{10,14},{12,8},{14,10},{1,7},{3,5},... | collective-permute-start | bytes 460808 | tf_op jit(solution)/shard_map/ppermute | solution.py:121
  13.6 11.8 %collective-permute-start.3 = (bf16[96,1600]{1,0:T(8,128)(2,1)S(1)}, bf16[96,1600]{1,0:T(8,128)(2,1)S(1)}, u32[]{:S(2)}, u32[]{:S(2)}) collective-permute-start(bf16[96,1600]{1,0:T(8,128)(2,1)S(1)} %get-tuple-element.36.refs_4_), channel_id=1, source_target_pairs={{0,2},{2,0},{4,6},{6,4},{8,10},{10,8},{12,14},{14,12},{16,18},{18,... | collective-permute-start | bytes 921608 | tf_op jit(solution)/shard_map/ppermute | solution.py:121
  19.0 14.6 %collective-permute-start.7 = (bf16[48,1600]{1,0:T(8,128)(2,1)S(1)}, bf16[48,1600]{1,0:T(8,128)(2,1)S(1)}, u32[]{:S(2)}, u32[]{:S(2)}) collective-permute-start(bf16[48,1600]{1,0:T(8,128)(2,1)S(1)} %get-tuple-element.40), channel_id=1, source_target_pairs={{0,8},{2,10},{4,12},{6,14},{8,0},{10,2},{12,4},{14,6},{1,13},{3,15... | collective-permute-start | bytes 460808 | tf_op jit(solution)/shard_map/ppermute | solution.py:121
  23.9 12.5 %collective-permute-start.8 = (bf16[48,1600]{1,0:T(8,128)(2,1)S(1)}, bf16[48,1600]{1,0:T(8,128)(2,1)S(1)}, u32[]{:S(2)}, u32[]{:S(2)}) collective-permute-start(bf16[48,1600]{1,0:T(8,128)(2,1)S(1)} %get-tuple-element.41), channel_id=1, source_target_pairs={{0,10},{2,8},{4,14},{6,12},{8,2},{10,0},{12,6},{14,4},{1,15},{3,13... | collective-permute-start | bytes 460808 | tf_op jit(solution)/shard_map/ppermute | solution.py:121
  25.5 3.3 %collective-permute-start.4 = (bf16[192,1664]{1,0:T(8,128)(2,1)S(1)}, bf16[192,1664]{1,0:T(8,128)(2,1)S(1)}, u32[]{:S(2)}, u32[]{:S(2)}) collective-permute-start(bf16[192,1664]{1,0:T(8,128)(2,1)S(1)} %pack.2.refs_0_.mine_ref), channel_id=1, source_target_pairs={{0,1},{1,0},{2,3},{3,2},{4,5},{5,4},{6,7},{7,6},{8,9},{9,8},{10,11... | collective-permute-start | bytes 1916936 | tf_op jit(solution)/shard_map/ppermute | solution.py:365
  32.4 12.4 %collective-permute-start.5 = (bf16[192,2048]{1,0:T(8,128)(2,1)S(1)}, bf16[192,2048]{1,0:T(8,128)(2,1)S(1)}, u32[]{:S(2)}, u32[]{:S(2)}) collective-permute-start(bf16[192,2048]{1,0:T(8,128)(2,1)S(1)} %get-tuple-element.38), channel_id=1, source_target_pairs={{0,2},{2,0},{4,6},{6,4},{8,10},{10,8},{12,14},{14,12},{1,5},{3,7},... | collective-permute-start | bytes 2359304 | tf_op jit(solution)/shard_map/ppermute | solution.py:293
  36.5 2.1 %collective-permute-start.9 = (bf16[192,1664]{1,0:T(8,128)(2,1)S(1)}, bf16[192,1664]{1,0:T(8,128)(2,1)S(1)}, u32[]{:S(2)}, u32[]{:S(2)}) collective-permute-start(bf16[192,1664]{1,0:T(8,128)(2,1)S(1)} %pack.3.mine_ref.refs_0_), channel_id=1, source_target_pairs={{0,1},{1,0},{2,3},{3,2},{4,5},{5,4},{6,7},{7,6},{8,9},{9,8},{10,11... | collective-permute-start | bytes 1916936 | tf_op jit(solution)/shard_map/ppermute | solution.py:365
  40.9 9.6 %collective-permute-start.11 = (bf16[192,1024]{1,0:T(8,128)(2,1)S(1)}, bf16[192,1024]{1,0:T(8,128)(2,1)S(1)}, u32[]{:S(2)}, u32[]{:S(2)}) collective-permute-start(bf16[192,1024]{1,0:T(8,128)(2,1)S(1)} %get-tuple-element.45), channel_id=1, source_target_pairs={{0,2},{2,0},{4,6},{6,4},{8,10},{10,8},{12,14},{14,12},{1,5},{3,7},... | collective-permute-start | bytes 1179656 | tf_op jit(solution)/shard_map/ppermute | solution.py:293
  45.0 10.6 %collective-permute-start.10 = (bf16[96,2048]{1,0:T(8,128)(2,1)S(1)}, bf16[96,2048]{1,0:T(8,128)(2,1)S(1)}, u32[]{:S(2)}, u32[]{:S(2)}) collective-permute-start(bf16[96,2048]{1,0:T(8,128)(2,1)S(1)} %get-tuple-element.44), channel_id=1, source_target_pairs={{0,4},{2,6},{4,0},{6,2},{8,12},{10,14},{12,8},{14,10},{1,3},{3,1},... | collective-permute-start | bytes 1179656 | tf_op jit(solution)/shard_map/ppermute | solution.py:293
  48.7 12.7 %copy-start.1 = (s32[8]{0:T(128)S(1)}, s32[8]{0:T(128)}, u32[]{:S(2)}) copy-start(s32[8]{0:T(128)} %count_hbm.3) | copy-start | bytes 100
  48.7 10.8 %collective-permute-start.14 = (bf16[192,1024]{1,0:T(8,128)(2,1)S(1)}, bf16[192,1024]{1,0:T(8,128)(2,1)S(1)}, u32[]{:S(2)}, u32[]{:S(2)}) collective-permute-start(bf16[192,1024]{1,0:T(8,128)(2,1)S(1)} %get-tuple-element.52), channel_id=1, source_target_pairs={{0,2},{2,0},{4,6},{6,4},{8,10},{10,8},{12,14},{14,12},{1,5},{3,7},... | collective-permute-start | bytes 1179656 | tf_op jit(solution)/shard_map/ppermute | solution.py:293
  50.4 20.0 %copy-start = (f32[2048]{0:T(1024)S(1)}, f32[2048]{0:T(1024)}, u32[]{:S(2)}) copy-start(f32[2048]{0:T(1024)} %param.16) | copy-start | bytes 24580
  50.5 11.3 %collective-permute-start.13 = (bf16[96,1024]{1,0:T(8,128)(2,1)S(1)}, bf16[96,1024]{1,0:T(8,128)(2,1)S(1)}, u32[]{:S(2)}, u32[]{:S(2)}) collective-permute-start(bf16[96,1024]{1,0:T(8,128)(2,1)S(1)} %get-tuple-element.51), channel_id=1, source_target_pairs={{0,4},{2,6},{4,0},{6,2},{8,12},{10,14},{12,8},{14,10},{1,3},{3,1},... | collective-permute-start | bytes 589832 | tf_op jit(solution)/shard_map/ppermute | solution.py:293
  55.7 14.7 %collective-permute-start.12 = (bf16[48,2048]{1,0:T(8,128)(2,1)S(1)}, bf16[48,2048]{1,0:T(8,128)(2,1)S(1)}, u32[]{:S(2)}, u32[]{:S(2)}) collective-permute-start(bf16[48,2048]{1,0:T(8,128)(2,1)S(1)} %get-tuple-element.50), channel_id=1, source_target_pairs={{0,8},{2,10},{4,12},{6,14},{8,0},{10,2},{12,4},{14,6},{1,9},{3,11}... | collective-permute-start | bytes 589832 | tf_op jit(solution)/shard_map/ppermute | solution.py:293
  59.7 10.8 %collective-permute-start.16 = (bf16[96,1024]{1,0:T(8,128)(2,1)S(1)}, bf16[96,1024]{1,0:T(8,128)(2,1)S(1)}, u32[]{:S(2)}, u32[]{:S(2)}) collective-permute-start(bf16[96,1024]{1,0:T(8,128)(2,1)S(1)} %get-tuple-element.56), channel_id=1, source_target_pairs={{0,4},{2,6},{4,0},{6,2},{8,12},{10,14},{12,8},{14,10},{1,3},{3,1},... | collective-permute-start | bytes 589832 | tf_op jit(solution)/shard_map/ppermute | solution.py:293
  61.9 10.5 %collective-permute-start.15 = (bf16[48,1024]{1,0:T(8,128)(2,1)S(1)}, bf16[48,1024]{1,0:T(8,128)(2,1)S(1)}, u32[]{:S(2)}, u32[]{:S(2)}) collective-permute-start(bf16[48,1024]{1,0:T(8,128)(2,1)S(1)} %get-tuple-element.55), channel_id=1, source_target_pairs={{0,8},{2,10},{4,12},{6,14},{8,0},{10,2},{12,4},{14,6},{1,9},{3,11}... | collective-permute-start | bytes 294920 | tf_op jit(solution)/shard_map/ppermute | solution.py:293
  70.6 7.7 %collective-permute-start.17 = (bf16[48,1024]{1,0:T(8,128)(2,1)S(1)}, bf16[48,1024]{1,0:T(8,128)(2,1)S(1)}, u32[]{:S(2)}, u32[]{:S(2)}) collective-permute-start(bf16[48,1024]{1,0:T(8,128)(2,1)S(1)} %get-tuple-element.58), channel_id=1, source_target_pairs={{0,8},{2,10},{4,12},{6,14},{8,0},{10,2},{12,4},{14,6},{1,9},{3,11}... | collective-permute-start | bytes 294920 | tf_op jit(solution)/shard_map/ppermute | solution.py:293

commit v5 on v4

--- a/solution.py
+++ b/solution.py
@@ -146,24 +146,25 @@
     )(*received, last, own, *after)
 
 
-def load_kernel(w_hbm, *refs):
-    w_ref, sem = refs[-2:]
+def load_kernel(w_hbm, piece_ref, w_ref, out_ref, sem):
     copy = pltpu.make_async_copy(w_hbm, w_ref, sem)
     copy.start()
+    out_ref[...] = piece_ref[...]
     copy.wait()
 
 
-def load(array, after):
+def load(array, piece):
+    inside = pl.BlockSpec(memory_space=pltpu.VMEM)
     return pl.pallas_call(
         load_kernel,
-        in_specs=[pl.BlockSpec(memory_space=pl.ANY)] * (1 + len(after)),
-        out_specs=pl.BlockSpec(memory_space=pltpu.VMEM),
-        out_shape=pltpu.VMEM(array.shape, array.dtype),
+        in_specs=[pl.BlockSpec(memory_space=pl.ANY), inside],
+        out_specs=[inside, inside],
+        out_shape=[pltpu.VMEM(array.shape, array.dtype), pltpu.VMEM(piece.shape, piece.dtype)],
         scratch_shapes=[pltpu.SemaphoreType.DMA],
         compiler_params=pltpu.CompilerParams(vmem_limit_bytes=VMEM_LIMIT),
         cost_estimate=pl.CostEstimate(flops=0, bytes_accessed=4 * array.size, transcendentals=0),
         name="load",
-    )(in_hbm(array), *after)
+    )(in_hbm(array), piece)
 
 
 def multiply(first, block, a_ref, w_ref, send_ref, keep_ref):
@@ -350,6 +351,8 @@
     chunks = [(0, 0, columns), (1, 0, half), (1, half, half)]
     pieces = [prepare(tile_count, patch_feats, ln_gain, ln_shift, peers, tiles, 0, [], [])]
     pieces.append(prepare(tile_count, patch_feats, ln_gain, ln_shift, peers, tiles, 1, pieces[0][-1:], pieces[0][:1]))
+    pieces[1] = list(pieces[1])
+    weight, pieces[1][-2] = load(merge_weight, pieces[1][-2])
     received = [[send_piece(piece, i, peers) for i, piece in enumerate(parts[:-1])] for parts in pieces]
     last = send_piece(pieces[1][-1], peers // 2 - 1, peers)
     packed = {}
@@ -364,8 +367,6 @@
             mine = pack(received[phase], last, pieces[1][-1], phase, after)
             packed[phase] = mine, lax.ppermute(mine, "tensor", [(0, 1), (1, 0)])
             after = [mine]
-            if phase == 0:
-                weight = load(merge_weight, after)
             if step < 0:
                 continue
         if step == len(bits):

time: 79.9 us -> 78.7 us (0.985)
  starting transfers between devices: 24.2 us -> 20.8 us
  waiting for transfers between devices: 35.8 us -> 38 us
    ppermute x9, starting transfers between devices: 14.4 us -> 8.15 us  [exchange(): return lax.ppermute(array, ('dp', 'tensor'), pairs)]
    ppermute x9, waiting for transfers between devices: 20.6 us -> 25.6 us  [exchange(): return lax.ppermute(array, ('dp', 'tensor'), pairs)]
    ppermute x7, waiting for transfers between devices: 13.1 us -> 8.64 us  [send_piece(): return lax.ppermute(piece, ('dp', 'tensor'), pairs)]
    ppermute x7, starting transfers between devices: 9.64 us -> 12.5 us  [send_piece(): return lax.ppermute(piece, ('dp', 'tensor'), pairs)]
    ppermute x2, waiting for transfers between devices: 2.06 us -> 3.8 us  [body(): packed[phase] = (mine, lax.ppermute(mine, 'tensor', [(0, 1), (1, 0)]))]
where the time goes in v5:
time: 78.7 us; the launch traced here: 78.5 us
  waiting for transfers between devices  38 us (48%)
  starting transfers between devices  20.8 us (26%)
  Pallas kernels  18.7 us (24%)
    ppermute x9, waiting for transfers between devices, exchange(): return lax.ppermute(array, ('dp', 'tensor'), pairs)  25.6 us
    ppermute x7, starting transfers between devices, send_piece(): return lax.ppermute(piece, ('dp', 'tensor'), pairs)  12.5 us
    ppermute x7, waiting for transfers between devices, send_piece(): return lax.ppermute(piece, ('dp', 'tensor'), pairs)  8.64 us
    ppermute x9, starting transfers between devices, exchange(): return lax.ppermute(array, ('dp', 'tensor'), pairs)  8.15 us
    pallas_call x2, Pallas kernels, prepare(): pl.pallas_call(functools.partial(prepare_kernel, peers, tiles, phase), in...  6.11 us
    pallas_call x2, Pallas kernels, gather_and_project(): pl.pallas_call(functools.partial(gather_kernel, first, block, len(pieces)...  5.87 us
    ppermute x2, waiting for transfers between devices, body(): packed[phase] = (mine, lax.ppermute(mine, 'tensor', [(0, 1), (1, 0)]))  3.8 us
    pallas_call x1, Pallas kernels, load(): pl.pallas_call(load_kernel, in_specs=[pl.BlockSpec(memory_space=pl.ANY),...  2.9 us
  transfers between devices with their start and end apart: 18, of which 14 were waited for; matrix products, arithmetic and copies ran while one was open for 1% of the time, Pallas kernels for 18%

profile of v5, /device:TPU:0, one launch (start us, length us, event | category | flops | bytes accessed | tf_op | source)
XLA Modules:
  0.0 78.5 jit_solution(15788593263176516553)
XLA Ops:
  0.0 3.1 %prepare.2 = (bf16[48,1600]{1,0:T(8,128)(2,1)S(1)}, bf16[48,1600]{1,0:T(8,128)(2,1)S(1)}, bf16[48,1600]{1,0:T(8,128)(2,1)S(1)}, bf16[48,1600]{1,0:T(8,128)(2,1)S(1)}) custom-call(bf16[3,2,64,3200]{3,2,1,0:T(8,128)(2,1)} %bitcast.7, f32[100,128]{1,0:T(8,128)} %bitcast.9, f32[100,128]{1,0:T(8,128)} %bitcast.11, s32[8]{0:T(128)} %count_hbm.3), custom_call_target="tpu_custom_call" | custom-call | bytes 4915200 | tf_op jit(solution)/shard_map/prepare/pallas_call | solution.py:97
  3.1 4.1 %collective-permute-start.1 = (bf16[48,1600]{1,0:T(8,128)(2,1)S(1)}, bf16[48,1600]{1,0:T(8,128)(2,1)S(1)}, u32[]{:S(2)}, u32[]{:S(2)}) collective-permute-start(bf16[48,1600]{1,0:T(8,128)(2,1)S(1)} %get-tuple-element.35), channel_id=1, source_target_pairs={{0,8},{2,10},{4,12},{6,14},{8,0},{10,2},{12,4},{14,6},{1,13},{3,15... | collective-permute-start | bytes 460808 | tf_op jit(solution)/shard_map/ppermute | solution.py:121
  7.2 1.3 %collective-permute-start.2 = (bf16[48,1600]{1,0:T(8,128)(2,1)S(1)}, bf16[48,1600]{1,0:T(8,128)(2,1)S(1)}, u32[]{:S(2)}, u32[]{:S(2)}) collective-permute-start(bf16[48,1600]{1,0:T(8,128)(2,1)S(1)} %get-tuple-element.36), channel_id=1, source_target_pairs={{0,10},{2,8},{4,14},{6,12},{8,2},{10,0},{12,6},{14,4},{1,15},{3,13... | collective-permute-start | bytes 460808 | tf_op jit(solution)/shard_map/ppermute | solution.py:121
  8.5 1.6 %collective-permute-start = (bf16[48,1600]{1,0:T(8,128)(2,1)S(1)}, bf16[48,1600]{1,0:T(8,128)(2,1)S(1)}, u32[]{:S(2)}, u32[]{:S(2)}) collective-permute-start(bf16[48,1600]{1,0:T(8,128)(2,1)S(1)} %get-tuple-element.34.refs_1_), channel_id=1, source_target_pairs={{0,4},{2,6},{4,0},{6,2},{8,12},{10,14},{12,8},{14,10},{1,7},{3,5},... | collective-permute-start | bytes 460808 | tf_op jit(solution)/shard_map/ppermute | solution.py:121
  10.0 3.0 %prepare.3 = (bf16[48,1600]{1,0:T(8,128)(2,1)S(1)}, bf16[48,1600]{1,0:T(8,128)(2,1)S(1)}, bf16[48,1600]{1,0:T(8,128)(2,1)S(1)}, bf16[96,1600]{1,0:T(8,128)(2,1)S(1)}) custom-call(bf16[3,2,64,3200]{3,2,1,0:T(8,128)(2,1)} %bitcast.8, f32[100,128]{1,0:T(8,128)} %bitcast.10, f32[100,128]{1,0:T(8,128)} %bitcast.12, s32[8]{0:T(128)} %count_hbm.3, ...), custom_call_target="tpu_custom_call" | custom-call | bytes 4915200 | tf_op jit(solution)/shard_map/prepare/pallas_call | solution.py:97
  13.1 0.5 collective-permute-start.6
  13.6 2.1 %collective-permute-start.3 = (bf16[96,1600]{1,0:T(8,128)(2,1)S(1)}, bf16[96,1600]{1,0:T(8,128)(2,1)S(1)}, u32[]{:S(2)}, u32[]{:S(2)}) collective-permute-start(bf16[96,1600]{1,0:T(8,128)(2,1)S(1)} %get-tuple-element.38.refs_4_), channel_id=1, source_target_pairs={{0,2},{2,0},{4,6},{6,4},{8,10},{10,8},{12,14},{14,12},{16,18},{18,... | collective-permute-start | bytes 921608 | tf_op jit(solution)/shard_map/ppermute | solution.py:121
  15.8 0.0 copy-done.2
  15.8 0.0 copy-done.3
  15.8 0.1 iota_add_fusion
  15.9 0.1 add.69
  16.0 2.9 %load.1 = (bf16[1600,2048]{1,0:T(8,128)(2,1)S(1)}, bf16[48,1600]{1,0:T(8,128)(2,1)S(1)}) custom-call(bf16[1600,2048]{1,0:T(8,128)(2,1)} %w_hbm.1, bf16[48,1600]{1,0:T(8,128)(2,1)S(1)} %get-tuple-element.39.piece_ref), custom_call_target="tpu_custom_call" | custom-call | bytes 13107200 | tf_op jit(solution)/shard_map/load/pallas_call | solution.py:158
  18.9 0.1 collective-permute-done.1.refs_1_
  18.9 2.8 %collective-permute-start.7 = (bf16[48,1600]{1,0:T(8,128)(2,1)S(1)}, bf16[48,1600]{1,0:T(8,128)(2,1)S(1)}, u32[]{:S(2)}, u32[]{:S(2)}) collective-permute-start(bf16[48,1600]{1,0:T(8,128)(2,1)S(1)} %get-tuple-element.44), channel_id=1, source_target_pairs={{0,8},{2,10},{4,12},{6,14},{8,0},{10,2},{12,4},{14,6},{1,13},{3,15... | collective-permute-start | bytes 460808 | tf_op jit(solution)/shard_map/ppermute | solution.py:121
  21.8 2.1 %collective-permute-done.2.refs_2_ = bf16[48,1600]{1,0:T(8,128)(2,1)S(1)} collective-permute-done((bf16[48,1600]{1,0:T(8,128)(2,1)S(1)}, bf16[48,1600]{1,0:T(8,128)(2,1)S(1)}, u32[]{:S(2)}, u32[]{:S(2)}) %collective-permute-start.2) | collective-permute-done | bytes 153632 | tf_op jit(solution)/shard_map/ppermute | solution.py:121
  23.9 0.0 collective-permute-start.8
  23.9 0.0 collective-permute-done.refs_0_
  23.9 1.5 %collective-permute-done.3.refs_3_ = bf16[96,1600]{1,0:T(8,128)(2,1)S(1)} collective-permute-done((bf16[96,1600]{1,0:T(8,128)(2,1)S(1)}, bf16[96,1600]{1,0:T(8,128)(2,1)S(1)}, u32[]{:S(2)}, u32[]{:S(2)}) %collective-permute-start.3) | collective-permute-done | bytes 307232 | tf_op jit(solution)/shard_map/ppermute | solution.py:121
  25.4 0.1 pack.2.mine_ref.refs_0_
  25.4 0.1 collective-permute-start.4
  25.5 0.0 copy-done.4
  25.5 0.2 select_reduce_fusion
  25.7 0.0 copy-done.5
  25.7 0.1 select_reduce_fusion.1
  25.8 1.7 %collective-permute-done.4.other_ref = bf16[192,1664]{1,0:T(8,128)(2,1)S(1)} collective-permute-done((bf16[192,1664]{1,0:T(8,128)(2,1)S(1)}, bf16[192,1664]{1,0:T(8,128)(2,1)S(1)}, u32[]{:S(2)}, u32[]{:S(2)}) %collective-permute-start.4) | collective-permute-done | bytes 639008 | tf_op jit(solution)/shard_map/ppermute | solution.py:368
  27.6 3.7 %gather_and_project.2 = (bf16[384,1664]{1,0:T(8,128)(2,1)}, bf16[192,2048]{1,0:T(8,128)(2,1)S(1)}, bf16[192,2048]{1,0:T(8,128)(2,1)S(1)}) custom-call(s32[24]{0:T(128)S(1)} %get-tuple-element.63.order_ref, bf16[192,1664]{1,0:T(8,128)(2,1)S(1)} %pack.2.mine_ref.refs_0_, bf16[192,1664]{1,0:T(8,128)(2,1)S(1)} %collective-permute-done.4.other_ref, ...), custom_call_target="tpu_custom_call" | custom-call | flops 2516582400 | bytes 9355264 | tf_op jit(solution)/shard_map/gather_and_project/pallas_call | solution.py:230
  31.3 0.3 collective-permute-start.5
  31.6 0.0 collective-permute-done.6.refs_0_
  31.6 2.0 %collective-permute-done.7.refs_1_ = bf16[48,1600]{1,0:T(8,128)(2,1)S(1)} collective-permute-done((bf16[48,1600]{1,0:T(8,128)(2,1)S(1)}, bf16[48,1600]{1,0:T(8,128)(2,1)S(1)}, u32[]{:S(2)}, u32[]{:S(2)}) %collective-permute-start.7) | collective-permute-done | bytes 153632 | tf_op jit(solution)/shard_map/ppermute | solution.py:121
  33.5 3.0 %collective-permute-done.8.refs_2_ = bf16[48,1600]{1,0:T(8,128)(2,1)S(1)} collective-permute-done((bf16[48,1600]{1,0:T(8,128)(2,1)S(1)}, bf16[48,1600]{1,0:T(8,128)(2,1)S(1)}, u32[]{:S(2)}, u32[]{:S(2)}) %collective-permute-start.8) | collective-permute-done | bytes 153632 | tf_op jit(solution)/shard_map/ppermute | solution.py:121
  36.5 0.1 pack.3.mine_ref.refs_0_
  36.6 0.1 collective-permute-start.9
  36.7 2.1 %collective-permute-done.9.other_ref = bf16[192,1664]{1,0:T(8,128)(2,1)S(1)} collective-permute-done((bf16[192,1664]{1,0:T(8,128)(2,1)S(1)}, bf16[192,1664]{1,0:T(8,128)(2,1)S(1)}, u32[]{:S(2)}, u32[]{:S(2)}) %collective-permute-start.9) | collective-permute-done | bytes 639008 | tf_op jit(solution)/shard_map/ppermute | solution.py:368
  38.7 2.2 %gather_and_project.3 = (bf16[384,1664]{1,0:T(8,128)(2,1)S(1)}, bf16[192,1024]{1,0:T(8,128)(2,1)S(1)}, bf16[192,1024]{1,0:T(8,128)(2,1)S(1)}) custom-call(s32[24]{0:T(128)S(1)} %get-tuple-element.63.order_ref, bf16[192,1664]{1,0:T(8,128)(2,1)S(1)} %pack.3.mine_ref.refs_0_, bf16[192,1664]{1,0:T(8,128)(2,1)S(1)} %collective-permute-done.9.other_ref, ...), custom_call_target="tpu_custom_call" | custom-call | flops 1258291200 | bytes 5292032 | tf_op jit(solution)/shard_map/gather_and_project/pallas_call | solution.py:230
  41.0 0.6 collective-permute-start.11
  41.5 3.1 %collective-permute-done.5.refs_1_ = bf16[192,2048]{1,0:T(8,128)(2,1)S(1)} collective-permute-done((bf16[192,2048]{1,0:T(8,128)(2,1)S(1)}, bf16[192,2048]{1,0:T(8,128)(2,1)S(1)}, u32[]{:S(2)}, u32[]{:S(2)}) %collective-permute-start.5) | collective-permute-done | bytes 786464 | tf_op jit(solution)/shard_map/ppermute | solution.py:294
  44.6 0.2 accumulate.6
  44.8 0.6 collective-permute-start.10
  45.3 1.6 %project.1 = (bf16[192,1024]{1,0:T(8,128)(2,1)S(1)}, bf16[192,1024]{1,0:T(8,128)(2,1)S(1)}) custom-call(bf16[384,1664]{1,0:T(8,128)(2,1)S(1)} %get-tuple-element.50.a_ref, bf16[1600,2048]{1,0:T(8,128)(2,1)S(1)} %get-tuple-element.40.w_ref, f32[96,2048]{1,0:T(8,128)S(1)} %get-tuple-element.47.refs_0_), custom_call_target="tpu_custom_call" | custom-call | flops 1258291200 | bytes 5292032 | tf_op jit(solution)/shard_map/project/pallas_call | solution.py:214
  46.9 0.0 copy-start.1
  47.0 1.3 %collective-permute-start.14 = (bf16[192,1024]{1,0:T(8,128)(2,1)S(1)}, bf16[192,1024]{1,0:T(8,128)(2,1)S(1)}, u32[]{:S(2)}, u32[]{:S(2)}) collective-permute-start(bf16[192,1024]{1,0:T(8,128)(2,1)S(1)} %get-tuple-element.56), channel_id=1, source_target_pairs={{0,2},{2,0},{4,6},{6,4},{8,10},{10,8},{12,14},{14,12},{1,5},{3,7},... | collective-permute-start | bytes 1179656 | tf_op jit(solution)/shard_map/ppermute | solution.py:294
  48.2 2.5 %collective-permute-done.11.refs_1_ = bf16[192,1024]{1,0:T(8,128)(2,1)S(1)} collective-permute-done((bf16[192,1024]{1,0:T(8,128)(2,1)S(1)}, bf16[192,1024]{1,0:T(8,128)(2,1)S(1)}, u32[]{:S(2)}, u32[]{:S(2)}) %collective-permute-start.11) | collective-permute-done | bytes 393248 | tf_op jit(solution)/shard_map/ppermute | solution.py:294
  50.7 0.1 accumulate.7
  50.8 0.7 collective-permute-start.13
  51.5 4.3 %collective-permute-done.10.refs_1_ = bf16[96,2048]{1,0:T(8,128)(2,1)S(1)} collective-permute-done((bf16[96,2048]{1,0:T(8,128)(2,1)S(1)}, bf16[96,2048]{1,0:T(8,128)(2,1)S(1)}, u32[]{:S(2)}, u32[]{:S(2)}) %collective-permute-start.10) | collective-permute-done | bytes 393248 | tf_op jit(solution)/shard_map/ppermute | solution.py:294
  55.8 0.1 accumulate.8
  55.9 1.1 %collective-permute-start.12 = (bf16[48,2048]{1,0:T(8,128)(2,1)S(1)}, bf16[48,2048]{1,0:T(8,128)(2,1)S(1)}, u32[]{:S(2)}, u32[]{:S(2)}) collective-permute-start(bf16[48,2048]{1,0:T(8,128)(2,1)S(1)} %get-tuple-element.54), channel_id=1, source_target_pairs={{0,8},{2,10},{4,12},{6,14},{8,0},{10,2},{12,4},{14,6},{1,9},{3,11}... | collective-permute-start | bytes 589832 | tf_op jit(solution)/shard_map/ppermute | solution.py:294
  56.9 2.2 %collective-permute-done.14.refs_1_ = bf16[192,1024]{1,0:T(8,128)(2,1)S(1)} collective-permute-done((bf16[192,1024]{1,0:T(8,128)(2,1)S(1)}, bf16[192,1024]{1,0:T(8,128)(2,1)S(1)}, u32[]{:S(2)}, u32[]{:S(2)}) %collective-permute-start.14) | collective-permute-done | bytes 393248 | tf_op jit(solution)/shard_map/ppermute | solution.py:294
  59.2 0.1 accumulate.9
  59.3 0.7 collective-permute-start.16
  60.0 0.1 slice.7
  60.1 0.0 copy-done.1
  60.1 0.2 select_reduce_fusion.2
  60.3 0.0 collective-permute-done.13.refs_1_
  60.3 2.9 %collective-permute-start.15 = (bf16[48,1024]{1,0:T(8,128)(2,1)S(1)}, bf16[48,1024]{1,0:T(8,128)(2,1)S(1)}, u32[]{:S(2)}, u32[]{:S(2)}) collective-permute-start(bf16[48,1024]{1,0:T(8,128)(2,1)S(1)} %get-tuple-element.59), channel_id=1, source_target_pairs={{0,8},{2,10},{4,12},{6,14},{8,0},{10,2},{12,4},{14,6},{1,9},{3,11}... | collective-permute-start | bytes 294920 | tf_op jit(solution)/shard_map/ppermute | solution.py:294
  63.2 7.0 %collective-permute-done.12.recv_ref = bf16[48,2048]{1,0:T(8,128)(2,1)S(1)} collective-permute-done((bf16[48,2048]{1,0:T(8,128)(2,1)S(1)}, bf16[48,2048]{1,0:T(8,128)(2,1)S(1)}, u32[]{:S(2)}, u32[]{:S(2)}) %collective-permute-start.12) | collective-permute-done | bytes 196640 | tf_op jit(solution)/shard_map/ppermute | solution.py:294
  70.2 0.0 copy-done
  70.2 0.1 early.1.refs_2_.refs_0_
  70.4 0.0 collective-permute-done.16.refs_1_
  70.4 0.1 collective-permute-start.17
  70.5 0.1 compare_convert_fusion.live_ref
  70.6 1.1 %collective-permute-done.15.refs_2_ = bf16[48,1024]{1,0:T(8,128)(2,1)S(1)} collective-permute-done((bf16[48,1024]{1,0:T(8,128)(2,1)S(1)}, bf16[48,1024]{1,0:T(8,128)(2,1)S(1)}, u32[]{:S(2)}, u32[]{:S(2)}) %collective-permute-start.15) | collective-permute-done | bytes 98336 | tf_op jit(solution)/shard_map/ppermute | solution.py:294
  71.6 5.4 %collective-permute-done.17.refs_4_ = bf16[48,1024]{1,0:T(8,128)(2,1)S(1)} collective-permute-done((bf16[48,1024]{1,0:T(8,128)(2,1)S(1)}, bf16[48,1024]{1,0:T(8,128)(2,1)S(1)}, u32[]{:S(2)}, u32[]{:S(2)}) %collective-permute-start.17) | collective-permute-done | bytes 98336 | tf_op jit(solution)/shard_map/ppermute | solution.py:294
  77.0 1.4 %finish.1 = bf16[3,2,16,2048]{3,2,1,0:T(8,128)(2,1)} custom-call(s32[3]{0:T(128)S(1)} %compare_convert_fusion.live_ref, f32[1,2048]{1,0:T(1,128)S(1)} %bitcast.6, bf16[48,2048]{1,0:T(8,128)(2,1)S(1)} %early.1.refs_2_.refs_0_, f32[48,1024]{1,0:T(8,128)S(1)} %get-tuple-element.58.refs_0_.refs_1_, bf16[48,1024]{1,0:T(8,128)(2,1)S(1)} %collective-permute-done.15.refs_2_, ...), custom_call_target="tpu_custom_call" | custom-call | tf_op jit(solution)/shard_map/finish/pallas_call | solution.py:281
  (10 shorter events, 0.1 us)
Async XLA Ops:
  0.0 15.8 %copy-start.2 = (s32[8]{0:T(128)S(1)}, s32[8]{0:T(128)}, u32[]{:S(2)}) copy-start(s32[8]{0:T(128)} %constant.45.clone) | copy-start | bytes 100
  0.0 15.8 %copy-start.3 = (s32[8]{0:T(128)S(1)}, s32[8]{0:T(128)}, u32[]{:S(2)}) copy-start(s32[8]{0:T(128)} %constant.44.clone) | copy-start | bytes 100
  3.1 15.9 %collective-permute-start.1 = (bf16[48,1600]{1,0:T(8,128)(2,1)S(1)}, bf16[48,1600]{1,0:T(8,128)(2,1)S(1)}, u32[]{:S(2)}, u32[]{:S(2)}) collective-permute-start(bf16[48,1600]{1,0:T(8,128)(2,1)S(1)} %get-tuple-element.35), channel_id=1, source_target_pairs={{0,8},{2,10},{4,12},{6,14},{8,0},{10,2},{12,4},{14,6},{1,13},{3,15... | collective-permute-start | bytes 460808 | tf_op jit(solution)/shard_map/ppermute | solution.py:121
  7.2 16.7 %collective-permute-start.2 = (bf16[48,1600]{1,0:T(8,128)(2,1)S(1)}, bf16[48,1600]{1,0:T(8,128)(2,1)S(1)}, u32[]{:S(2)}, u32[]{:S(2)}) collective-permute-start(bf16[48,1600]{1,0:T(8,128)(2,1)S(1)} %get-tuple-element.36), channel_id=1, source_target_pairs={{0,10},{2,8},{4,14},{6,12},{8,2},{10,0},{12,6},{14,4},{1,15},{3,13... | collective-permute-start | bytes 460808 | tf_op jit(solution)/shard_map/ppermute | solution.py:121
  8.5 15.4 %collective-permute-start = (bf16[48,1600]{1,0:T(8,128)(2,1)S(1)}, bf16[48,1600]{1,0:T(8,128)(2,1)S(1)}, u32[]{:S(2)}, u32[]{:S(2)}) collective-permute-start(bf16[48,1600]{1,0:T(8,128)(2,1)S(1)} %get-tuple-element.34.refs_1_), channel_id=1, source_target_pairs={{0,4},{2,6},{4,0},{6,2},{8,12},{10,14},{12,8},{14,10},{1,7},{3,5},... | collective-permute-start | bytes 460808 | tf_op jit(solution)/shard_map/ppermute | solution.py:121
  13.1 18.5 %collective-permute-start.6 = (bf16[48,1600]{1,0:T(8,128)(2,1)S(1)}, bf16[48,1600]{1,0:T(8,128)(2,1)S(1)}, u32[]{:S(2)}, u32[]{:S(2)}) collective-permute-start(bf16[48,1600]{1,0:T(8,128)(2,1)S(1)} %get-tuple-element.43), channel_id=1, source_target_pairs={{0,4},{2,6},{4,0},{6,2},{8,12},{10,14},{12,8},{14,10},{1,7},{3,5},... | collective-permute-start | bytes 460808 | tf_op jit(solution)/shard_map/ppermute | solution.py:121
  13.6 11.8 %collective-permute-start.3 = (bf16[96,1600]{1,0:T(8,128)(2,1)S(1)}, bf16[96,1600]{1,0:T(8,128)(2,1)S(1)}, u32[]{:S(2)}, u32[]{:S(2)}) collective-permute-start(bf16[96,1600]{1,0:T(8,128)(2,1)S(1)} %get-tuple-element.38.refs_4_), channel_id=1, source_target_pairs={{0,2},{2,0},{4,6},{6,4},{8,10},{10,8},{12,14},{14,12},{16,18},{18,... | collective-permute-start | bytes 921608 | tf_op jit(solution)/shard_map/ppermute | solution.py:121
  16.0 9.6 %copy-start.4 = (s32[24]{0:T(128)S(1)}, s32[24]{0:T(128)}, u32[]{:S(2)}) copy-start(s32[24]{0:T(128)} %param.18) | copy-start | bytes 292
  16.0 9.8 %copy-start.5 = (s32[8]{0:T(128)S(1)}, s32[8]{0:T(128)}, u32[]{:S(2)}) copy-start(s32[8]{0:T(128)} %constant.43.clone) | copy-start | bytes 100
  18.9 14.6 %collective-permute-start.7 = (bf16[48,1600]{1,0:T(8,128)(2,1)S(1)}, bf16[48,1600]{1,0:T(8,128)(2,1)S(1)}, u32[]{:S(2)}, u32[]{:S(2)}) collective-permute-start(bf16[48,1600]{1,0:T(8,128)(2,1)S(1)} %get-tuple-element.44), channel_id=1, source_target_pairs={{0,8},{2,10},{4,12},{6,14},{8,0},{10,2},{12,4},{14,6},{1,13},{3,15... | collective-permute-start | bytes 460808 | tf_op jit(solution)/shard_map/ppermute | solution.py:121
  23.9 12.7 %collective-permute-start.8 = (bf16[48,1600]{1,0:T(8,128)(2,1)S(1)}, bf16[48,1600]{1,0:T(8,128)(2,1)S(1)}, u32[]{:S(2)}, u32[]{:S(2)}) collective-permute-start(bf16[48,1600]{1,0:T(8,128)(2,1)S(1)} %get-tuple-element.45), channel_id=1, source_target_pairs={{0,10},{2,8},{4,14},{6,12},{8,2},{10,0},{12,6},{14,4},{1,15},{3,13... | collective-permute-start | bytes 460808 | tf_op jit(solution)/shard_map/ppermute | solution.py:121
  25.4 2.1 %collective-permute-start.4 = (bf16[192,1664]{1,0:T(8,128)(2,1)S(1)}, bf16[192,1664]{1,0:T(8,128)(2,1)S(1)}, u32[]{:S(2)}, u32[]{:S(2)}) collective-permute-start(bf16[192,1664]{1,0:T(8,128)(2,1)S(1)} %pack.2.mine_ref.refs_0_), channel_id=1, source_target_pairs={{0,1},{1,0},{2,3},{3,2},{4,5},{5,4},{6,7},{7,6},{8,9},{9,8},{10,11... | collective-permute-start | bytes 1916936 | tf_op jit(solution)/shard_map/ppermute | solution.py:368
  31.3 13.3 %collective-permute-start.5 = (bf16[192,2048]{1,0:T(8,128)(2,1)S(1)}, bf16[192,2048]{1,0:T(8,128)(2,1)S(1)}, u32[]{:S(2)}, u32[]{:S(2)}) collective-permute-start(bf16[192,2048]{1,0:T(8,128)(2,1)S(1)} %get-tuple-element.42), channel_id=1, source_target_pairs={{0,2},{2,0},{4,6},{6,4},{8,10},{10,8},{12,14},{14,12},{1,5},{3,7},... | collective-permute-start | bytes 2359304 | tf_op jit(solution)/shard_map/ppermute | solution.py:294
  36.6 2.1 %collective-permute-start.9 = (bf16[192,1664]{1,0:T(8,128)(2,1)S(1)}, bf16[192,1664]{1,0:T(8,128)(2,1)S(1)}, u32[]{:S(2)}, u32[]{:S(2)}) collective-permute-start(bf16[192,1664]{1,0:T(8,128)(2,1)S(1)} %pack.3.mine_ref.refs_0_), channel_id=1, source_target_pairs={{0,1},{1,0},{2,3},{3,2},{4,5},{5,4},{6,7},{7,6},{8,9},{9,8},{10,11... | collective-permute-start | bytes 1916936 | tf_op jit(solution)/shard_map/ppermute | solution.py:368
  41.0 9.8 %collective-permute-start.11 = (bf16[192,1024]{1,0:T(8,128)(2,1)S(1)}, bf16[192,1024]{1,0:T(8,128)(2,1)S(1)}, u32[]{:S(2)}, u32[]{:S(2)}) collective-permute-start(bf16[192,1024]{1,0:T(8,128)(2,1)S(1)} %get-tuple-element.49), channel_id=1, source_target_pairs={{0,2},{2,0},{4,6},{6,4},{8,10},{10,8},{12,14},{14,12},{1,5},{3,7},... | collective-permute-start | bytes 1179656 | tf_op jit(solution)/shard_map/ppermute | solution.py:294
  44.8 11.0 %collective-permute-start.10 = (bf16[96,2048]{1,0:T(8,128)(2,1)S(1)}, bf16[96,2048]{1,0:T(8,128)(2,1)S(1)}, u32[]{:S(2)}, u32[]{:S(2)}) collective-permute-start(bf16[96,2048]{1,0:T(8,128)(2,1)S(1)} %get-tuple-element.48), channel_id=1, source_target_pairs={{0,4},{2,6},{4,0},{6,2},{8,12},{10,14},{12,8},{14,10},{1,3},{3,1},... | collective-permute-start | bytes 1179656 | tf_op jit(solution)/shard_map/ppermute | solution.py:294
  46.9 13.1 %copy-start.1 = (s32[8]{0:T(128)S(1)}, s32[8]{0:T(128)}, u32[]{:S(2)}) copy-start(s32[8]{0:T(128)} %count_hbm.3) | copy-start | bytes 100
  47.0 12.2 %collective-permute-start.14 = (bf16[192,1024]{1,0:T(8,128)(2,1)S(1)}, bf16[192,1024]{1,0:T(8,128)(2,1)S(1)}, u32[]{:S(2)}, u32[]{:S(2)}) collective-permute-start(bf16[192,1024]{1,0:T(8,128)(2,1)S(1)} %get-tuple-element.56), channel_id=1, source_target_pairs={{0,2},{2,0},{4,6},{6,4},{8,10},{10,8},{12,14},{14,12},{1,5},{3,7},... | collective-permute-start | bytes 1179656 | tf_op jit(solution)/shard_map/ppermute | solution.py:294
  50.7 19.5 %copy-start = (f32[2048]{0:T(1024)S(1)}, f32[2048]{0:T(1024)}, u32[]{:S(2)}) copy-start(f32[2048]{0:T(1024)} %param.16) | copy-start | bytes 24580
  50.8 9.4 %collective-permute-start.13 = (bf16[96,1024]{1,0:T(8,128)(2,1)S(1)}, bf16[96,1024]{1,0:T(8,128)(2,1)S(1)}, u32[]{:S(2)}, u32[]{:S(2)}) collective-permute-start(bf16[96,1024]{1,0:T(8,128)(2,1)S(1)} %get-tuple-element.55), channel_id=1, source_target_pairs={{0,4},{2,6},{4,0},{6,2},{8,12},{10,14},{12,8},{14,10},{1,3},{3,1},... | collective-permute-start | bytes 589832 | tf_op jit(solution)/shard_map/ppermute | solution.py:294
  55.9 14.4 %collective-permute-start.12 = (bf16[48,2048]{1,0:T(8,128)(2,1)S(1)}, bf16[48,2048]{1,0:T(8,128)(2,1)S(1)}, u32[]{:S(2)}, u32[]{:S(2)}) collective-permute-start(bf16[48,2048]{1,0:T(8,128)(2,1)S(1)} %get-tuple-element.54), channel_id=1, source_target_pairs={{0,8},{2,10},{4,12},{6,14},{8,0},{10,2},{12,4},{14,6},{1,9},{3,11}... | collective-permute-start | bytes 589832 | tf_op jit(solution)/shard_map/ppermute | solution.py:294
  59.3 11.1 %collective-permute-start.16 = (bf16[96,1024]{1,0:T(8,128)(2,1)S(1)}, bf16[96,1024]{1,0:T(8,128)(2,1)S(1)}, u32[]{:S(2)}, u32[]{:S(2)}) collective-permute-start(bf16[96,1024]{1,0:T(8,128)(2,1)S(1)} %get-tuple-element.60), channel_id=1, source_target_pairs={{0,4},{2,6},{4,0},{6,2},{8,12},{10,14},{12,8},{14,10},{1,3},{3,1},... | collective-permute-start | bytes 589832 | tf_op jit(solution)/shard_map/ppermute | solution.py:294
  60.3 11.3 %collective-permute-start.15 = (bf16[48,1024]{1,0:T(8,128)(2,1)S(1)}, bf16[48,1024]{1,0:T(8,128)(2,1)S(1)}, u32[]{:S(2)}, u32[]{:S(2)}) collective-permute-start(bf16[48,1024]{1,0:T(8,128)(2,1)S(1)} %get-tuple-element.59), channel_id=1, source_target_pairs={{0,8},{2,10},{4,12},{6,14},{8,0},{10,2},{12,4},{14,6},{1,9},{3,11}... | collective-permute-start | bytes 294920 | tf_op jit(solution)/shard_map/ppermute | solution.py:294
  70.4 6.6 %collective-permute-start.17 = (bf16[48,1024]{1,0:T(8,128)(2,1)S(1)}, bf16[48,1024]{1,0:T(8,128)(2,1)S(1)}, u32[]{:S(2)}, u32[]{:S(2)}) collective-permute-start(bf16[48,1024]{1,0:T(8,128)(2,1)S(1)} %get-tuple-element.62), channel_id=1, source_target_pairs={{0,8},{2,10},{4,12},{6,14},{8,0},{10,2},{12,4},{14,6},{1,9},{3,11}... | collective-permute-start | bytes 294920 | tf_op jit(solution)/shard_map/ppermute | solution.py:294

commit v6 on v5

--- a/solution.py
+++ b/solution.py
@@ -187,14 +187,13 @@
     for piece, out in zip(refs[:count], refs[-1 - count:-1]):
         out[...] = piece[...]
     core = lax.axis_index("tensor")
-    held[core] = mine_ref[...]
-    held[1 - core] = other_ref[...]
     half = mine_ref.shape[0] // PART
     for i in range(sorted_ref.shape[0] // PART):
         place = order_ref[i]
         side = (place >= half).astype(jnp.int32)
         start = pl.multiple_of((place - side * half) * PART, PART)
-        sorted_ref[pl.ds(i * PART, PART), :] = held[side, pl.ds(start, PART), :]
+        tile = jnp.where(side == core, mine_ref[pl.ds(start, PART), :], other_ref[pl.ds(start, PART), :])
+        sorted_ref[pl.ds(i * PART, PART), :] = tile
     multiply(first, block, sorted_ref, w_ref, send_ref, keep_ref)
 
 

time: 78.7 us -> 78.7 us (level)
  starting transfers between devices: 20.8 us -> 22.5 us
  waiting for transfers between devices: 38 us -> 36.4 us
    ppermute x9, starting transfers between devices: 8.15 us -> 9.84 us  [exchange(): return lax.ppermute(array, ('dp', 'tensor'), pairs)]
    ppermute x9, waiting for transfers between devices: 25.6 us -> 23.9 us  [exchange(): return lax.ppermute(array, ('dp', 'tensor'), pairs)]
  transfers between devices with their start and end apart: 18 -> 18, of which waited for: 14 -> 13; matrix products, arithmetic and copies ran while one was open for 1% -> 1% of each run, Pallas kernels for 18% -> 18%
where the time goes in v6:
time: 78.7 us; the launch traced here: 78.4 us
  waiting for transfers between devices  36.4 us (46%)
  starting transfers between devices  22.5 us (29%)
  Pallas kernels  18.6 us (24%)
    ppermute x9, waiting for transfers between devices, exchange(): return lax.ppermute(array, ('dp', 'tensor'), pairs)  23.9 us
    ppermute x7, starting transfers between devices, send_piece(): return lax.ppermute(piece, ('dp', 'tensor'), pairs)  12.5 us
    ppermute x9, starting transfers between devices, exchange(): return lax.ppermute(array, ('dp', 'tensor'), pairs)  9.84 us
    ppermute x7, waiting for transfers between devices, send_piece(): return lax.ppermute(piece, ('dp', 'tensor'), pairs)  8.67 us
    pallas_call x2, Pallas kernels, prepare(): pl.pallas_call(functools.partial(prepare_kernel, peers, tiles, phase), in...  6.11 us
    pallas_call x2, Pallas kernels, gather_and_project(): pl.pallas_call(functools.partial(gather_kernel, first, block, len(pieces)...  5.79 us
    ppermute x2, waiting for transfers between devices, body(): packed[phase] = (mine, lax.ppermute(mine, 'tensor', [(0, 1), (1, 0)]))  3.8 us
    pallas_call x1, Pallas kernels, load(): pl.pallas_call(load_kernel, in_specs=[pl.BlockSpec(memory_space=pl.ANY),...  2.9 us
  transfers between devices with their start and end apart: 18, of which 13 were waited for; matrix products, arithmetic and copies ran while one was open for 1% of the time, Pallas kernels for 18%

profile of v6, /device:TPU:0, one launch (start us, length us, event | category | flops | bytes accessed | tf_op | source)
XLA Modules:
  0.0 78.4 jit_solution(8211173495221667104)
XLA Ops:
  0.0 3.1 %prepare.2 = (bf16[48,1600]{1,0:T(8,128)(2,1)S(1)}, bf16[48,1600]{1,0:T(8,128)(2,1)S(1)}, bf16[48,1600]{1,0:T(8,128)(2,1)S(1)}, bf16[48,1600]{1,0:T(8,128)(2,1)S(1)}) custom-call(bf16[3,2,64,3200]{3,2,1,0:T(8,128)(2,1)} %bitcast.7, f32[100,128]{1,0:T(8,128)} %bitcast.9, f32[100,128]{1,0:T(8,128)} %bitcast.11, s32[8]{0:T(128)} %count_hbm.3), custom_call_target="tpu_custom_call" | custom-call | bytes 4915200 | tf_op jit(solution)/shard_map/prepare/pallas_call | solution.py:97
  3.1 4.1 %collective-permute-start.1 = (bf16[48,1600]{1,0:T(8,128)(2,1)S(1)}, bf16[48,1600]{1,0:T(8,128)(2,1)S(1)}, u32[]{:S(2)}, u32[]{:S(2)}) collective-permute-start(bf16[48,1600]{1,0:T(8,128)(2,1)S(1)} %get-tuple-element.35), channel_id=1, source_target_pairs={{0,8},{2,10},{4,12},{6,14},{8,0},{10,2},{12,4},{14,6},{1,13},{3,15... | collective-permute-start | bytes 460808 | tf_op jit(solution)/shard_map/ppermute | solution.py:121
  7.2 1.3 %collective-permute-start.2 = (bf16[48,1600]{1,0:T(8,128)(2,1)S(1)}, bf16[48,1600]{1,0:T(8,128)(2,1)S(1)}, u32[]{:S(2)}, u32[]{:S(2)}) collective-permute-start(bf16[48,1600]{1,0:T(8,128)(2,1)S(1)} %get-tuple-element.36), channel_id=1, source_target_pairs={{0,10},{2,8},{4,14},{6,12},{8,2},{10,0},{12,6},{14,4},{1,15},{3,13... | collective-permute-start | bytes 460808 | tf_op jit(solution)/shard_map/ppermute | solution.py:121
  8.5 1.6 %collective-permute-start = (bf16[48,1600]{1,0:T(8,128)(2,1)S(1)}, bf16[48,1600]{1,0:T(8,128)(2,1)S(1)}, u32[]{:S(2)}, u32[]{:S(2)}) collective-permute-start(bf16[48,1600]{1,0:T(8,128)(2,1)S(1)} %get-tuple-element.34.refs_1_), channel_id=1, source_target_pairs={{0,4},{2,6},{4,0},{6,2},{8,12},{10,14},{12,8},{14,10},{1,7},{3,5},... | collective-permute-start | bytes 460808 | tf_op jit(solution)/shard_map/ppermute | solution.py:121
  10.0 3.0 %prepare.3 = (bf16[48,1600]{1,0:T(8,128)(2,1)S(1)}, bf16[48,1600]{1,0:T(8,128)(2,1)S(1)}, bf16[48,1600]{1,0:T(8,128)(2,1)S(1)}, bf16[96,1600]{1,0:T(8,128)(2,1)S(1)}) custom-call(bf16[3,2,64,3200]{3,2,1,0:T(8,128)(2,1)} %bitcast.8, f32[100,128]{1,0:T(8,128)} %bitcast.10, f32[100,128]{1,0:T(8,128)} %bitcast.12, s32[8]{0:T(128)} %count_hbm.3, ...), custom_call_target="tpu_custom_call" | custom-call | bytes 4915200 | tf_op jit(solution)/shard_map/prepare/pallas_call | solution.py:97
  13.1 0.5 collective-permute-start.6
  13.6 2.1 %collective-permute-start.3 = (bf16[96,1600]{1,0:T(8,128)(2,1)S(1)}, bf16[96,1600]{1,0:T(8,128)(2,1)S(1)}, u32[]{:S(2)}, u32[]{:S(2)}) collective-permute-start(bf16[96,1600]{1,0:T(8,128)(2,1)S(1)} %get-tuple-element.38.refs_4_), channel_id=1, source_target_pairs={{0,2},{2,0},{4,6},{6,4},{8,10},{10,8},{12,14},{14,12},{16,18},{18,... | collective-permute-start | bytes 921608 | tf_op jit(solution)/shard_map/ppermute | solution.py:121
  15.8 0.0 copy-done.2
  15.8 0.0 copy-done.3
  15.8 0.1 iota_add_fusion
  15.9 0.1 add.69
  16.0 2.9 %load.1 = (bf16[1600,2048]{1,0:T(8,128)(2,1)S(1)}, bf16[48,1600]{1,0:T(8,128)(2,1)S(1)}) custom-call(bf16[1600,2048]{1,0:T(8,128)(2,1)} %w_hbm.1, bf16[48,1600]{1,0:T(8,128)(2,1)S(1)} %get-tuple-element.39.piece_ref), custom_call_target="tpu_custom_call" | custom-call | bytes 13107200 | tf_op jit(solution)/shard_map/load/pallas_call | solution.py:158
  18.9 0.1 collective-permute-done.1.refs_1_
  18.9 2.8 %collective-permute-start.7 = (bf16[48,1600]{1,0:T(8,128)(2,1)S(1)}, bf16[48,1600]{1,0:T(8,128)(2,1)S(1)}, u32[]{:S(2)}, u32[]{:S(2)}) collective-permute-start(bf16[48,1600]{1,0:T(8,128)(2,1)S(1)} %get-tuple-element.44), channel_id=1, source_target_pairs={{0,8},{2,10},{4,12},{6,14},{8,0},{10,2},{12,4},{14,6},{1,13},{3,15... | collective-permute-start | bytes 460808 | tf_op jit(solution)/shard_map/ppermute | solution.py:121
  21.8 2.1 %collective-permute-done.2.refs_2_ = bf16[48,1600]{1,0:T(8,128)(2,1)S(1)} collective-permute-done((bf16[48,1600]{1,0:T(8,128)(2,1)S(1)}, bf16[48,1600]{1,0:T(8,128)(2,1)S(1)}, u32[]{:S(2)}, u32[]{:S(2)}) %collective-permute-start.2) | collective-permute-done | bytes 153632 | tf_op jit(solution)/shard_map/ppermute | solution.py:121
  23.9 0.0 collective-permute-start.8
  23.9 0.0 collective-permute-done.refs_0_
  23.9 1.5 %collective-permute-done.3.refs_3_ = bf16[96,1600]{1,0:T(8,128)(2,1)S(1)} collective-permute-done((bf16[96,1600]{1,0:T(8,128)(2,1)S(1)}, bf16[96,1600]{1,0:T(8,128)(2,1)S(1)}, u32[]{:S(2)}, u32[]{:S(2)}) %collective-permute-start.3) | collective-permute-done | bytes 307232 | tf_op jit(solution)/shard_map/ppermute | solution.py:121
  25.4 0.1 pack.2.mine_ref.refs_0_
  25.4 0.1 collective-permute-start.4
  25.5 0.0 copy-done.4
  25.5 0.2 select_reduce_fusion
  25.7 0.0 copy-done.5
  25.7 0.1 select_reduce_fusion.1
  25.8 1.7 %collective-permute-done.4.other_ref = bf16[192,1664]{1,0:T(8,128)(2,1)S(1)} collective-permute-done((bf16[192,1664]{1,0:T(8,128)(2,1)S(1)}, bf16[192,1664]{1,0:T(8,128)(2,1)S(1)}, u32[]{:S(2)}, u32[]{:S(2)}) %collective-permute-start.4) | collective-permute-done | bytes 639008 | tf_op jit(solution)/shard_map/ppermute | solution.py:367
  27.6 3.6 %gather_and_project.2 = (bf16[384,1664]{1,0:T(8,128)(2,1)}, bf16[192,2048]{1,0:T(8,128)(2,1)S(1)}, bf16[192,2048]{1,0:T(8,128)(2,1)S(1)}) custom-call(s32[24]{0:T(128)S(1)} %get-tuple-element.63.order_ref, bf16[192,1664]{1,0:T(8,128)(2,1)S(1)} %pack.2.mine_ref.refs_0_, bf16[192,1664]{1,0:T(8,128)(2,1)S(1)} %collective-permute-done.4.other_ref, ...), custom_call_target="tpu_custom_call" | custom-call | flops 2516582400 | bytes 9355264 | tf_op jit(solution)/shard_map/gather_and_project/pallas_call | solution.py:229
  31.2 0.3 collective-permute-start.5
  31.5 0.0 collective-permute-done.6.refs_0_
  31.5 2.0 %collective-permute-done.7.refs_1_ = bf16[48,1600]{1,0:T(8,128)(2,1)S(1)} collective-permute-done((bf16[48,1600]{1,0:T(8,128)(2,1)S(1)}, bf16[48,1600]{1,0:T(8,128)(2,1)S(1)}, u32[]{:S(2)}, u32[]{:S(2)}) %collective-permute-start.7) | collective-permute-done | bytes 153632 | tf_op jit(solution)/shard_map/ppermute | solution.py:121
  33.5 3.0 %collective-permute-done.8.refs_2_ = bf16[48,1600]{1,0:T(8,128)(2,1)S(1)} collective-permute-done((bf16[48,1600]{1,0:T(8,128)(2,1)S(1)}, bf16[48,1600]{1,0:T(8,128)(2,1)S(1)}, u32[]{:S(2)}, u32[]{:S(2)}) %collective-permute-start.8) | collective-permute-done | bytes 153632 | tf_op jit(solution)/shard_map/ppermute | solution.py:121
  36.5 0.1 pack.3.mine_ref.refs_0_
  36.6 0.1 collective-permute-start.9
  36.7 2.1 %collective-permute-done.9.other_ref = bf16[192,1664]{1,0:T(8,128)(2,1)S(1)} collective-permute-done((bf16[192,1664]{1,0:T(8,128)(2,1)S(1)}, bf16[192,1664]{1,0:T(8,128)(2,1)S(1)}, u32[]{:S(2)}, u32[]{:S(2)}) %collective-permute-start.9) | collective-permute-done | bytes 639008 | tf_op jit(solution)/shard_map/ppermute | solution.py:367
  38.7 2.2 %gather_and_project.3 = (bf16[384,1664]{1,0:T(8,128)(2,1)S(1)}, bf16[192,1024]{1,0:T(8,128)(2,1)S(1)}, bf16[192,1024]{1,0:T(8,128)(2,1)S(1)}) custom-call(s32[24]{0:T(128)S(1)} %get-tuple-element.63.order_ref, bf16[192,1664]{1,0:T(8,128)(2,1)S(1)} %pack.3.mine_ref.refs_0_, bf16[192,1664]{1,0:T(8,128)(2,1)S(1)} %collective-permute-done.9.other_ref, ...), custom_call_target="tpu_custom_call" | custom-call | flops 1258291200 | bytes 5292032 | tf_op jit(solution)/shard_map/gather_and_project/pallas_call | solution.py:229
  40.9 0.6 collective-permute-start.11
  41.5 3.1 %collective-permute-done.5.refs_1_ = bf16[192,2048]{1,0:T(8,128)(2,1)S(1)} collective-permute-done((bf16[192,2048]{1,0:T(8,128)(2,1)S(1)}, bf16[192,2048]{1,0:T(8,128)(2,1)S(1)}, u32[]{:S(2)}, u32[]{:S(2)}) %collective-permute-start.5) | collective-permute-done | bytes 786464 | tf_op jit(solution)/shard_map/ppermute | solution.py:293
  44.6 0.2 accumulate.6
  44.7 0.6 collective-permute-start.10
  45.3 1.6 %project.1 = (bf16[192,1024]{1,0:T(8,128)(2,1)S(1)}, bf16[192,1024]{1,0:T(8,128)(2,1)S(1)}) custom-call(bf16[384,1664]{1,0:T(8,128)(2,1)S(1)} %get-tuple-element.50.a_ref, bf16[1600,2048]{1,0:T(8,128)(2,1)S(1)} %get-tuple-element.40.w_ref, f32[96,2048]{1,0:T(8,128)S(1)} %get-tuple-element.47.refs_0_), custom_call_target="tpu_custom_call" | custom-call | flops 1258291200 | bytes 5292032 | tf_op jit(solution)/shard_map/project/pallas_call | solution.py:213
  46.9 0.0 copy-start.1
  46.9 1.3 %collective-permute-start.14 = (bf16[192,1024]{1,0:T(8,128)(2,1)S(1)}, bf16[192,1024]{1,0:T(8,128)(2,1)S(1)}, u32[]{:S(2)}, u32[]{:S(2)}) collective-permute-start(bf16[192,1024]{1,0:T(8,128)(2,1)S(1)} %get-tuple-element.56), channel_id=1, source_target_pairs={{0,2},{2,0},{4,6},{6,4},{8,10},{10,8},{12,14},{14,12},{1,5},{3,7},... | collective-permute-start | bytes 1179656 | tf_op jit(solution)/shard_map/ppermute | solution.py:293
  48.2 2.5 %collective-permute-done.11.refs_1_ = bf16[192,1024]{1,0:T(8,128)(2,1)S(1)} collective-permute-done((bf16[192,1024]{1,0:T(8,128)(2,1)S(1)}, bf16[192,1024]{1,0:T(8,128)(2,1)S(1)}, u32[]{:S(2)}, u32[]{:S(2)}) %collective-permute-start.11) | collective-permute-done | bytes 393248 | tf_op jit(solution)/shard_map/ppermute | solution.py:293
  50.7 0.1 accumulate.7
  50.8 0.7 collective-permute-start.13
  51.5 4.3 %collective-permute-done.10.refs_1_ = bf16[96,2048]{1,0:T(8,128)(2,1)S(1)} collective-permute-done((bf16[96,2048]{1,0:T(8,128)(2,1)S(1)}, bf16[96,2048]{1,0:T(8,128)(2,1)S(1)}, u32[]{:S(2)}, u32[]{:S(2)}) %collective-permute-start.10) | collective-permute-done | bytes 393248 | tf_op jit(solution)/shard_map/ppermute | solution.py:293
  55.7 0.1 accumulate.8
  55.8 1.1 %collective-permute-start.12 = (bf16[48,2048]{1,0:T(8,128)(2,1)S(1)}, bf16[48,2048]{1,0:T(8,128)(2,1)S(1)}, u32[]{:S(2)}, u32[]{:S(2)}) collective-permute-start(bf16[48,2048]{1,0:T(8,128)(2,1)S(1)} %get-tuple-element.54), channel_id=1, source_target_pairs={{0,8},{2,10},{4,12},{6,14},{8,0},{10,2},{12,4},{14,6},{1,9},{3,11}... | collective-permute-start | bytes 589832 | tf_op jit(solution)/shard_map/ppermute | solution.py:293
  56.9 2.2 %collective-permute-done.14.refs_1_ = bf16[192,1024]{1,0:T(8,128)(2,1)S(1)} collective-permute-done((bf16[192,1024]{1,0:T(8,128)(2,1)S(1)}, bf16[192,1024]{1,0:T(8,128)(2,1)S(1)}, u32[]{:S(2)}, u32[]{:S(2)}) %collective-permute-start.14) | collective-permute-done | bytes 393248 | tf_op jit(solution)/shard_map/ppermute | solution.py:293
  59.1 0.1 accumulate.9
  59.2 0.7 collective-permute-start.16
  60.0 0.1 slice.7
  60.0 0.0 copy-done.1
  60.0 0.2 select_reduce_fusion.2
  60.2 0.0 collective-permute-done.13.refs_1_
  60.3 2.9 %collective-permute-start.15 = (bf16[48,1024]{1,0:T(8,128)(2,1)S(1)}, bf16[48,1024]{1,0:T(8,128)(2,1)S(1)}, u32[]{:S(2)}, u32[]{:S(2)}) collective-permute-start(bf16[48,1024]{1,0:T(8,128)(2,1)S(1)} %get-tuple-element.59), channel_id=1, source_target_pairs={{0,8},{2,10},{4,12},{6,14},{8,0},{10,2},{12,4},{14,6},{1,9},{3,11}... | collective-permute-start | bytes 294920 | tf_op jit(solution)/shard_map/ppermute | solution.py:293
  63.2 7.0 %collective-permute-done.12.recv_ref = bf16[48,2048]{1,0:T(8,128)(2,1)S(1)} collective-permute-done((bf16[48,2048]{1,0:T(8,128)(2,1)S(1)}, bf16[48,2048]{1,0:T(8,128)(2,1)S(1)}, u32[]{:S(2)}, u32[]{:S(2)}) %collective-permute-start.12) | collective-permute-done | bytes 196640 | tf_op jit(solution)/shard_map/ppermute | solution.py:293
  70.2 0.0 copy-done
  70.2 0.1 early.1.refs_2_.refs_0_
  70.3 0.0 collective-permute-done.16.refs_1_
  70.4 1.7 %collective-permute-start.17 = (bf16[48,1024]{1,0:T(8,128)(2,1)S(1)}, bf16[48,1024]{1,0:T(8,128)(2,1)S(1)}, u32[]{:S(2)}, u32[]{:S(2)}) collective-permute-start(bf16[48,1024]{1,0:T(8,128)(2,1)S(1)} %get-tuple-element.62), channel_id=1, source_target_pairs={{0,8},{2,10},{4,12},{6,14},{8,0},{10,2},{12,4},{14,6},{1,9},{3,11}... | collective-permute-start | bytes 294920 | tf_op jit(solution)/shard_map/ppermute | solution.py:293
  72.1 0.1 compare_convert_fusion.live_ref
  72.2 0.0 collective-permute-done.15.refs_2_
  72.2 4.9 %collective-permute-done.17.refs_4_ = bf16[48,1024]{1,0:T(8,128)(2,1)S(1)} collective-permute-done((bf16[48,1024]{1,0:T(8,128)(2,1)S(1)}, bf16[48,1024]{1,0:T(8,128)(2,1)S(1)}, u32[]{:S(2)}, u32[]{:S(2)}) %collective-permute-start.17) | collective-permute-done | bytes 98336 | tf_op jit(solution)/shard_map/ppermute | solution.py:293
  77.0 1.4 %finish.1 = bf16[3,2,16,2048]{3,2,1,0:T(8,128)(2,1)} custom-call(s32[3]{0:T(128)S(1)} %compare_convert_fusion.live_ref, f32[1,2048]{1,0:T(1,128)S(1)} %bitcast.6, bf16[48,2048]{1,0:T(8,128)(2,1)S(1)} %early.1.refs_2_.refs_0_, f32[48,1024]{1,0:T(8,128)S(1)} %get-tuple-element.58.refs_0_.refs_1_, bf16[48,1024]{1,0:T(8,128)(2,1)S(1)} %collective-permute-done.15.refs_2_, ...), custom_call_target="tpu_custom_call" | custom-call | tf_op jit(solution)/shard_map/finish/pallas_call | solution.py:280
  (10 shorter events, 0.1 us)
Async XLA Ops:
  0.0 15.8 %copy-start.2 = (s32[8]{0:T(128)S(1)}, s32[8]{0:T(128)}, u32[]{:S(2)}) copy-start(s32[8]{0:T(128)} %constant.45.clone) | copy-start | bytes 100
  0.0 15.8 %copy-start.3 = (s32[8]{0:T(128)S(1)}, s32[8]{0:T(128)}, u32[]{:S(2)}) copy-start(s32[8]{0:T(128)} %constant.44.clone) | copy-start | bytes 100
  3.1 15.9 %collective-permute-start.1 = (bf16[48,1600]{1,0:T(8,128)(2,1)S(1)}, bf16[48,1600]{1,0:T(8,128)(2,1)S(1)}, u32[]{:S(2)}, u32[]{:S(2)}) collective-permute-start(bf16[48,1600]{1,0:T(8,128)(2,1)S(1)} %get-tuple-element.35), channel_id=1, source_target_pairs={{0,8},{2,10},{4,12},{6,14},{8,0},{10,2},{12,4},{14,6},{1,13},{3,15... | collective-permute-start | bytes 460808 | tf_op jit(solution)/shard_map/ppermute | solution.py:121
  7.2 16.7 %collective-permute-start.2 = (bf16[48,1600]{1,0:T(8,128)(2,1)S(1)}, bf16[48,1600]{1,0:T(8,128)(2,1)S(1)}, u32[]{:S(2)}, u32[]{:S(2)}) collective-permute-start(bf16[48,1600]{1,0:T(8,128)(2,1)S(1)} %get-tuple-element.36), channel_id=1, source_target_pairs={{0,10},{2,8},{4,14},{6,12},{8,2},{10,0},{12,6},{14,4},{1,15},{3,13... | collective-permute-start | bytes 460808 | tf_op jit(solution)/shard_map/ppermute | solution.py:121
  8.5 15.4 %collective-permute-start = (bf16[48,1600]{1,0:T(8,128)(2,1)S(1)}, bf16[48,1600]{1,0:T(8,128)(2,1)S(1)}, u32[]{:S(2)}, u32[]{:S(2)}) collective-permute-start(bf16[48,1600]{1,0:T(8,128)(2,1)S(1)} %get-tuple-element.34.refs_1_), channel_id=1, source_target_pairs={{0,4},{2,6},{4,0},{6,2},{8,12},{10,14},{12,8},{14,10},{1,7},{3,5},... | collective-permute-start | bytes 460808 | tf_op jit(solution)/shard_map/ppermute | solution.py:121
  13.1 18.4 %collective-permute-start.6 = (bf16[48,1600]{1,0:T(8,128)(2,1)S(1)}, bf16[48,1600]{1,0:T(8,128)(2,1)S(1)}, u32[]{:S(2)}, u32[]{:S(2)}) collective-permute-start(bf16[48,1600]{1,0:T(8,128)(2,1)S(1)} %get-tuple-element.43), channel_id=1, source_target_pairs={{0,4},{2,6},{4,0},{6,2},{8,12},{10,14},{12,8},{14,10},{1,7},{3,5},... | collective-permute-start | bytes 460808 | tf_op jit(solution)/shard_map/ppermute | solution.py:121
  13.6 11.8 %collective-permute-start.3 = (bf16[96,1600]{1,0:T(8,128)(2,1)S(1)}, bf16[96,1600]{1,0:T(8,128)(2,1)S(1)}, u32[]{:S(2)}, u32[]{:S(2)}) collective-permute-start(bf16[96,1600]{1,0:T(8,128)(2,1)S(1)} %get-tuple-element.38.refs_4_), channel_id=1, source_target_pairs={{0,2},{2,0},{4,6},{6,4},{8,10},{10,8},{12,14},{14,12},{16,18},{18,... | collective-permute-start | bytes 921608 | tf_op jit(solution)/shard_map/ppermute | solution.py:121
  16.0 9.6 %copy-start.4 = (s32[24]{0:T(128)S(1)}, s32[24]{0:T(128)}, u32[]{:S(2)}) copy-start(s32[24]{0:T(128)} %param.18) | copy-start | bytes 292
  16.0 9.8 %copy-start.5 = (s32[8]{0:T(128)S(1)}, s32[8]{0:T(128)}, u32[]{:S(2)}) copy-start(s32[8]{0:T(128)} %constant.43.clone) | copy-start | bytes 100
  18.9 14.6 %collective-permute-start.7 = (bf16[48,1600]{1,0:T(8,128)(2,1)S(1)}, bf16[48,1600]{1,0:T(8,128)(2,1)S(1)}, u32[]{:S(2)}, u32[]{:S(2)}) collective-permute-start(bf16[48,1600]{1,0:T(8,128)(2,1)S(1)} %get-tuple-element.44), channel_id=1, source_target_pairs={{0,8},{2,10},{4,12},{6,14},{8,0},{10,2},{12,4},{14,6},{1,13},{3,15... | collective-permute-start | bytes 460808 | tf_op jit(solution)/shard_map/ppermute | solution.py:121
  23.9 12.6 %collective-permute-start.8 = (bf16[48,1600]{1,0:T(8,128)(2,1)S(1)}, bf16[48,1600]{1,0:T(8,128)(2,1)S(1)}, u32[]{:S(2)}, u32[]{:S(2)}) collective-permute-start(bf16[48,1600]{1,0:T(8,128)(2,1)S(1)} %get-tuple-element.45), channel_id=1, source_target_pairs={{0,10},{2,8},{4,14},{6,12},{8,2},{10,0},{12,6},{14,4},{1,15},{3,13... | collective-permute-start | bytes 460808 | tf_op jit(solution)/shard_map/ppermute | solution.py:121
  25.4 2.1 %collective-permute-start.4 = (bf16[192,1664]{1,0:T(8,128)(2,1)S(1)}, bf16[192,1664]{1,0:T(8,128)(2,1)S(1)}, u32[]{:S(2)}, u32[]{:S(2)}) collective-permute-start(bf16[192,1664]{1,0:T(8,128)(2,1)S(1)} %pack.2.mine_ref.refs_0_), channel_id=1, source_target_pairs={{0,1},{1,0},{2,3},{3,2},{4,5},{5,4},{6,7},{7,6},{8,9},{9,8},{10,11... | collective-permute-start | bytes 1916936 | tf_op jit(solution)/shard_map/ppermute | solution.py:367
  31.2 13.3 %collective-permute-start.5 = (bf16[192,2048]{1,0:T(8,128)(2,1)S(1)}, bf16[192,2048]{1,0:T(8,128)(2,1)S(1)}, u32[]{:S(2)}, u32[]{:S(2)}) collective-permute-start(bf16[192,2048]{1,0:T(8,128)(2,1)S(1)} %get-tuple-element.42), channel_id=1, source_target_pairs={{0,2},{2,0},{4,6},{6,4},{8,10},{10,8},{12,14},{14,12},{1,5},{3,7},... | collective-permute-start | bytes 2359304 | tf_op jit(solution)/shard_map/ppermute | solution.py:293
  36.6 2.1 %collective-permute-start.9 = (bf16[192,1664]{1,0:T(8,128)(2,1)S(1)}, bf16[192,1664]{1,0:T(8,128)(2,1)S(1)}, u32[]{:S(2)}, u32[]{:S(2)}) collective-permute-start(bf16[192,1664]{1,0:T(8,128)(2,1)S(1)} %pack.3.mine_ref.refs_0_), channel_id=1, source_target_pairs={{0,1},{1,0},{2,3},{3,2},{4,5},{5,4},{6,7},{7,6},{8,9},{9,8},{10,11... | collective-permute-start | bytes 1916936 | tf_op jit(solution)/shard_map/ppermute | solution.py:367
  40.9 9.8 %collective-permute-start.11 = (bf16[192,1024]{1,0:T(8,128)(2,1)S(1)}, bf16[192,1024]{1,0:T(8,128)(2,1)S(1)}, u32[]{:S(2)}, u32[]{:S(2)}) collective-permute-start(bf16[192,1024]{1,0:T(8,128)(2,1)S(1)} %get-tuple-element.49), channel_id=1, source_target_pairs={{0,2},{2,0},{4,6},{6,4},{8,10},{10,8},{12,14},{14,12},{1,5},{3,7},... | collective-permute-start | bytes 1179656 | tf_op jit(solution)/shard_map/ppermute | solution.py:293
  44.7 11.0 %collective-permute-start.10 = (bf16[96,2048]{1,0:T(8,128)(2,1)S(1)}, bf16[96,2048]{1,0:T(8,128)(2,1)S(1)}, u32[]{:S(2)}, u32[]{:S(2)}) collective-permute-start(bf16[96,2048]{1,0:T(8,128)(2,1)S(1)} %get-tuple-element.48), channel_id=1, source_target_pairs={{0,4},{2,6},{4,0},{6,2},{8,12},{10,14},{12,8},{14,10},{1,3},{3,1},... | collective-permute-start | bytes 1179656 | tf_op jit(solution)/shard_map/ppermute | solution.py:293
  46.9 13.1 %copy-start.1 = (s32[8]{0:T(128)S(1)}, s32[8]{0:T(128)}, u32[]{:S(2)}) copy-start(s32[8]{0:T(128)} %count_hbm.3) | copy-start | bytes 100
  46.9 12.2 %collective-permute-start.14 = (bf16[192,1024]{1,0:T(8,128)(2,1)S(1)}, bf16[192,1024]{1,0:T(8,128)(2,1)S(1)}, u32[]{:S(2)}, u32[]{:S(2)}) collective-permute-start(bf16[192,1024]{1,0:T(8,128)(2,1)S(1)} %get-tuple-element.56), channel_id=1, source_target_pairs={{0,2},{2,0},{4,6},{6,4},{8,10},{10,8},{12,14},{14,12},{1,5},{3,7},... | collective-permute-start | bytes 1179656 | tf_op jit(solution)/shard_map/ppermute | solution.py:293
  50.7 19.5 %copy-start = (f32[2048]{0:T(1024)S(1)}, f32[2048]{0:T(1024)}, u32[]{:S(2)}) copy-start(f32[2048]{0:T(1024)} %param.16) | copy-start | bytes 24580
  50.8 9.4 %collective-permute-start.13 = (bf16[96,1024]{1,0:T(8,128)(2,1)S(1)}, bf16[96,1024]{1,0:T(8,128)(2,1)S(1)}, u32[]{:S(2)}, u32[]{:S(2)}) collective-permute-start(bf16[96,1024]{1,0:T(8,128)(2,1)S(1)} %get-tuple-element.55), channel_id=1, source_target_pairs={{0,4},{2,6},{4,0},{6,2},{8,12},{10,14},{12,8},{14,10},{1,3},{3,1},... | collective-permute-start | bytes 589832 | tf_op jit(solution)/shard_map/ppermute | solution.py:293
  55.8 14.4 %collective-permute-start.12 = (bf16[48,2048]{1,0:T(8,128)(2,1)S(1)}, bf16[48,2048]{1,0:T(8,128)(2,1)S(1)}, u32[]{:S(2)}, u32[]{:S(2)}) collective-permute-start(bf16[48,2048]{1,0:T(8,128)(2,1)S(1)} %get-tuple-element.54), channel_id=1, source_target_pairs={{0,8},{2,10},{4,12},{6,14},{8,0},{10,2},{12,4},{14,6},{1,9},{3,11}... | collective-permute-start | bytes 589832 | tf_op jit(solution)/shard_map/ppermute | solution.py:293
  59.2 11.1 %collective-permute-start.16 = (bf16[96,1024]{1,0:T(8,128)(2,1)S(1)}, bf16[96,1024]{1,0:T(8,128)(2,1)S(1)}, u32[]{:S(2)}, u32[]{:S(2)}) collective-permute-start(bf16[96,1024]{1,0:T(8,128)(2,1)S(1)} %get-tuple-element.60), channel_id=1, source_target_pairs={{0,4},{2,6},{4,0},{6,2},{8,12},{10,14},{12,8},{14,10},{1,3},{3,1},... | collective-permute-start | bytes 589832 | tf_op jit(solution)/shard_map/ppermute | solution.py:293
  60.3 11.9 %collective-permute-start.15 = (bf16[48,1024]{1,0:T(8,128)(2,1)S(1)}, bf16[48,1024]{1,0:T(8,128)(2,1)S(1)}, u32[]{:S(2)}, u32[]{:S(2)}) collective-permute-start(bf16[48,1024]{1,0:T(8,128)(2,1)S(1)} %get-tuple-element.59), channel_id=1, source_target_pairs={{0,8},{2,10},{4,12},{6,14},{8,0},{10,2},{12,4},{14,6},{1,9},{3,11}... | collective-permute-start | bytes 294920 | tf_op jit(solution)/shard_map/ppermute | solution.py:293
  70.4 6.6 %collective-permute-start.17 = (bf16[48,1024]{1,0:T(8,128)(2,1)S(1)}, bf16[48,1024]{1,0:T(8,128)(2,1)S(1)}, u32[]{:S(2)}, u32[]{:S(2)}) collective-permute-start(bf16[48,1024]{1,0:T(8,128)(2,1)S(1)} %get-tuple-element.62), channel_id=1, source_target_pairs={{0,8},{2,10},{4,12},{6,14},{8,0},{10,2},{12,4},{14,6},{1,9},{3,11}... | collective-permute-start | bytes 294920 | tf_op jit(solution)/shard_map/ppermute | solution.py:293
